TPU v7x, 32 devices: a whole 2x2x4 slice. The times are simulated.
32 devices in a mesh: seq: 32 (over z, y, x, core).
Axes of the slice: x: 2, y: 2, z: 4, core: 2. Of those that a mesh axis runs over, the one named last changes fastest.
Arguments:
- tokens: bfloat16 [32768, 1024], P('seq'), may hold values from -6 to 6
- norm_gain: bfloat16 [1024], P('seq'), may hold values from 0.5 to 1.5
- query_weight: bfloat16 [1024, 512], P('seq'), may hold values from -0.1875 to 0.1875
- key_weight: bfloat16 [1024, 512], P('seq'), may hold values from -0.1875 to 0.1875
- value_weight: bfloat16 [1024, 1024], P('seq'), may hold values from -0.1875 to 0.1875
- gate_weight: bfloat16 [1024, 1024], P('seq'), may hold values from -0.1875 to 0.1875
- rank_down: bfloat16 [1024, 16], P('seq'), may hold values from -0.1875 to 0.1875
- rank_up: bfloat16 [16, 512], P(None, 'seq'), may hold values from -1.5 to 1.5
- gate_bias: bfloat16 [512], P('seq'), may hold values from 1 to 12
- head_gain: bfloat16 [1024], P('seq'), may hold values from 0.5 to 1.5
- out_weight: bfloat16 [1024, 1024], P('seq'), may hold values from -0.1875 to 0.1875
- ffn_gain: bfloat16 [1024], P('seq'), may hold values from 0.5 to 1.5
- ffn_gate: bfloat16 [1024, 2816], P('seq'), may hold values from -0.1875 to 0.1875
- ffn_up: bfloat16 [1024, 2816], P('seq'), may hold values from -0.1875 to 0.1875
- ffn_down: bfloat16 [2816, 1024], P('seq'), may hold values from -0.109375 to 0.109375
- cotangent: bfloat16 [32768, 1024], P('seq'), may hold values from -6 to 6
Outputs:
- block_output: float32 [32768, 1024], P('seq')
- tokens_grad: float32 [32768, 1024], P('seq')
- norm_gain_grad: float32 [1024], P('seq')
- query_grad: float32 [1024, 512], P('seq')
- key_grad: float32 [1024, 512], P('seq')
- value_grad: float32 [1024, 1024], P('seq')
- gate_grad: float32 [1024, 1024], P('seq')
- rank_down_grad: float32 [1024, 16], P('seq')
- rank_up_grad: float32 [16, 512], P(None, 'seq')
- gate_bias_grad: float32 [512], P('seq')
- head_gain_grad: float32 [1024], P('seq')
- out_grad: float32 [1024, 1024], P('seq')
- ffn_gain_grad: float32 [1024], P('seq')
- ffn_gate_grad: float32 [1024, 2816], P('seq')
- ffn_up_grad: float32 [1024, 2816], P('seq')
- ffn_down_grad: float32 [2816, 1024], P('seq')
All inputs are finite; a program needn't handle non-finite values.
Results may differ from a plain program's by a relative error of at most 0.038.
Values may be sent and summed in bfloat16 or wider, within the bound.
A program may use at most 384 MiB of HBM per device.

v0:
```python
import jax
import jax.numpy as jnp
from jax import lax
from jax.sharding import PartitionSpec as P

HEADS = 4
HK = 128
HV = 256
GROUP = 64
SEQS = 1


def carried_in(value, axis, join, neutral, backward):
    count, mine = (lax.axis_size(axis), lax.axis_index(axis))
    pieces = jax.tree.map(lambda part: lax.all_gather(part, axis), value)
    if backward:
        pieces = jax.tree.map(lambda part: part[::-1], pieces)
        mine = count - 1 - mine
    total = jax.tree.map(
        lambda part, zero: jnp.full_like(part, 0) + jnp.asarray(zero, part.dtype), value, neutral
    )

    def hop(position, total):
        longer = join(total, jax.tree.map(lambda part: part[position], pieces))
        return jax.tree.map(lambda new, old: jnp.where(position < mine, new, old), longer, total)

    return lax.fori_loop(0, count - 1, hop, total)


def matmul(left, right):
    return jnp.dot(left, right, preferred_element_type=jnp.float32)


def left_t(left, right):
    return lax.dot_general(
        left, right, (((0,), (0,)), ((), ())), preferred_element_type=jnp.float32
    )


def right_t(left, right):
    return lax.dot_general(
        left, right, (((1,), (1,)), ((), ())), preferred_element_type=jnp.float32
    )


def rms_norm(values, gain):
    return values * lax.rsqrt(jnp.mean(values * values, axis=-1, keepdims=True) + 1e-06) * gain


def head_norm(mixed, gain, gate):
    length = mixed.shape[0]
    shaped = mixed.reshape(length, HEADS, HV)
    headed = shaped * lax.rsqrt(jnp.mean(shaped * shaped, axis=-1, keepdims=True) + 1e-06)
    return headed.reshape(length, HEADS * HV) * gain * jax.nn.silu(gate)


def swiglu(fgate, fup):
    return jax.nn.silu(fgate) * fup


def mixer_local(query, key, value_rows, decay):
    length = query.shape[0]
    blocks = length // GROUP
    q_blocks = query.reshape(blocks, GROUP, HEADS, HK) * HK ** (-0.5)
    k_blocks = key.reshape(blocks, GROUP, HEADS, HK)
    v_blocks = value_rows.reshape(blocks, GROUP, HEADS, HV)
    within = jnp.cumsum(decay.reshape(blocks, GROUP, HEADS, HK), axis=1)
    total = within[:, -1]
    query_with_decay = q_blocks * jnp.exp(within)
    k_decayed = k_blocks * jnp.exp(-within)
    key_to_segment_end = k_blocks * jnp.exp(total[:, None] - within)
    causal = (jnp.arange(GROUP)[:, None] >= jnp.arange(GROUP)[None, :]).astype(jnp.float32)
    scores = (
        jnp.einsum("nihk,njhk->nhij", query_with_decay, k_decayed, precision=lax.Precision.HIGHEST)
        * causal
    )
    segment_result = jnp.einsum(
        "nhij,njhv->nihv", scores, v_blocks, precision=lax.Precision.HIGHEST
    )
    updates = jnp.einsum(
        "njhk,njhv->nhkv", key_to_segment_end, v_blocks, precision=lax.Precision.HIGHEST
    )

    def advance(state_matrix, pair):
        factor, state_increment = pair
        return (jnp.exp(factor)[:, :, None] * state_matrix + state_increment, state_matrix)

    final, starts = lax.scan(advance, jnp.zeros((HEADS, HK, HV), jnp.float32), (total, updates))
    segment_result = segment_result + jnp.einsum(
        "nihk,nhkv->nihv", query_with_decay, starts, precision=lax.Precision.HIGHEST
    )
    return (segment_result.reshape(length, HEADS * HV), final, jnp.sum(total, axis=0))


def mixer_carried(query, decay, incoming_state):
    length = query.shape[0]
    blocks = length // GROUP
    q_blocks = query.reshape(blocks, GROUP, HEADS, HK) * HK ** (-0.5)
    within = jnp.cumsum(decay.reshape(blocks, GROUP, HEADS, HK), axis=1)
    before = jnp.cumsum(within[:, -1], axis=0) - within[:, -1]
    weighted_scores = q_blocks * jnp.exp(within + before[:, None])
    segment_result = jnp.einsum(
        "blfs,fsq->blfq", weighted_scores, incoming_state, precision=lax.Precision.HIGHEST
    )
    return segment_result.reshape(length, HEADS * HV)


def chain(earlier, later):
    return (earlier[0] * later[0], later[0][:, :, None] * earlier[1] + later[1])


def local(
    tokens,
    norm_gain,
    query_weight,
    key_weight,
    value_weight,
    gate_weight,
    rank_down,
    rank_up,
    gate_bias,
    head_gain,
    out_weight,
    ffn_gain,
    ffn_gate,
    ffn_up,
    ffn_down,
    cotangent,
):
    gathered = (
        lax.all_gather(norm_gain, "seq", axis=0, tiled=True),
        lax.all_gather(query_weight, "seq", axis=0, tiled=True),
        lax.all_gather(key_weight, "seq", axis=0, tiled=True),
        lax.all_gather(value_weight, "seq", axis=0, tiled=True),
        lax.all_gather(gate_weight, "seq", axis=0, tiled=True),
        lax.all_gather(rank_down, "seq", axis=0, tiled=True),
        lax.all_gather(rank_up, "seq", axis=1, tiled=True),
        lax.all_gather(gate_bias, "seq", axis=0, tiled=True),
        lax.all_gather(head_gain, "seq", axis=0, tiled=True),
        lax.all_gather(out_weight, "seq", axis=0, tiled=True),
        lax.all_gather(ffn_gain, "seq", axis=0, tiled=True),
        lax.all_gather(ffn_gate, "seq", axis=0, tiled=True),
        lax.all_gather(ffn_up, "seq", axis=0, tiled=True),
        lax.all_gather(ffn_down, "seq", axis=0, tiled=True),
    )
    (
        full_gain,
        full_query,
        full_key,
        full_value,
        full_gate,
        full_down_rank,
        full_up_rank,
        full_bias,
        full_head_gain,
        full_out,
        full_ffn_gain,
        full_fgate,
        full_fup,
        full_fdown,
    ) = gathered
    gain_one = full_gain.astype(jnp.float32)
    gain_two = full_ffn_gain.astype(jnp.float32)
    heads_gain = full_head_gain.astype(jnp.float32)
    segments = lax.axis_size("seq") // SEQS
    not_first = (lax.axis_index("seq") % segments != 0).astype(jnp.float32)
    inputs = tokens.astype(jnp.float32)
    normed = rms_norm(inputs, gain_one)
    normed_low = normed.astype(jnp.bfloat16)
    query_low = matmul(normed_low, full_query).astype(jnp.bfloat16)
    key_low = matmul(normed_low, full_key).astype(jnp.bfloat16)
    value_low = matmul(normed_low, full_value).astype(jnp.bfloat16)
    rank_mid = matmul(normed_low, full_down_rank).astype(jnp.bfloat16)
    logit = matmul(rank_mid, full_up_rank) + full_bias.astype(jnp.float32)
    decay = jax.nn.log_sigmoid(logit) / 16.0
    gate = matmul(normed_low, full_gate)
    query_f = query_low.astype(jnp.float32)
    key_f = key_low.astype(jnp.float32)
    value_f = value_low.astype(jnp.float32)
    local_out, local_pull = jax.vjp(mixer_local, query_f, key_f, value_f, decay)
    mixed_local, final_state, log_total = local_out
    factor = jnp.exp(log_total)
    passed = factor * not_first
    incoming_state = (
        carried_in(
            (passed, final_state),
            "seq",
            chain,
            (jnp.ones_like(factor), jnp.zeros_like(final_state)),
            False,
        )[1]
        * not_first
    )
    carried_out, carried_pull = jax.vjp(mixer_carried, query_f, decay, incoming_state)
    mixed = mixed_local + carried_out
    gated, gated_pull = jax.vjp(head_norm, mixed, heads_gain, gate)
    gated_low = gated.astype(jnp.bfloat16)
    hidden_state = inputs + matmul(gated_low, full_out)
    ffn_in, ffn_norm_pull = jax.vjp(rms_norm, hidden_state, gain_two)
    ffn_low = ffn_in.astype(jnp.bfloat16)
    fgate = matmul(ffn_low, full_fgate)
    fup = matmul(ffn_low, full_fup)
    inner, inner_pull = jax.vjp(swiglu, fgate, fup)
    inner_low = inner.astype(jnp.bfloat16)
    block_output = hidden_state + matmul(inner_low, full_fdown)
    regathered = (
        lax.all_gather(norm_gain, "seq", axis=0, tiled=True),
        lax.all_gather(query_weight, "seq", axis=0, tiled=True),
        lax.all_gather(key_weight, "seq", axis=0, tiled=True),
        lax.all_gather(value_weight, "seq", axis=0, tiled=True),
        lax.all_gather(gate_weight, "seq", axis=0, tiled=True),
        lax.all_gather(rank_down, "seq", axis=0, tiled=True),
        lax.all_gather(rank_up, "seq", axis=1, tiled=True),
        lax.all_gather(gate_bias, "seq", axis=0, tiled=True),
        lax.all_gather(head_gain, "seq", axis=0, tiled=True),
        lax.all_gather(out_weight, "seq", axis=0, tiled=True),
        lax.all_gather(ffn_gain, "seq", axis=0, tiled=True),
        lax.all_gather(ffn_gate, "seq", axis=0, tiled=True),
        lax.all_gather(ffn_up, "seq", axis=0, tiled=True),
        lax.all_gather(ffn_down, "seq", axis=0, tiled=True),
    )
    (
        _,
        back_query,
        back_key,
        back_value,
        back_gate,
        back_down_rank,
        back_up_rank,
        _,
        _,
        back_out,
        _,
        back_fgate,
        back_fup,
        back_fdown,
    ) = regathered
    upstream = cotangent.astype(jnp.float32)
    down_grad = left_t(inner_low, cotangent)
    inner_grad = right_t(cotangent, back_fdown)
    fgate_grad, fup_grad = inner_pull(inner_grad)
    fgate_low = fgate_grad.astype(jnp.bfloat16)
    fup_low = fup_grad.astype(jnp.bfloat16)
    fgate_wgrad = left_t(ffn_low, fgate_low)
    fup_wgrad = left_t(ffn_low, fup_low)
    ffn_in_grad = right_t(fgate_low, back_fgate) + right_t(fup_low, back_fup)
    hidden_part, gain_two_grad = ffn_norm_pull(ffn_in_grad)
    hidden_grad = upstream + hidden_part
    hidden_low = hidden_grad.astype(jnp.bfloat16)
    out_wgrad = left_t(gated_low, hidden_low)
    gated_grad = right_t(hidden_low, back_out)
    mixed_grad, heads_gain_grad, gate_grad = gated_pull(gated_grad)
    gate_low = gate_grad.astype(jnp.bfloat16)
    gate_wgrad = left_t(normed_low, gate_low)
    query_part, decay_part, entering_grad = carried_pull(mixed_grad)
    leaving_grad = carried_in(
        (passed, entering_grad * not_first),
        "seq",
        chain,
        (jnp.ones_like(factor), jnp.zeros_like(entering_grad)),
        True,
    )[1]
    log_total_grad = factor * jnp.sum(incoming_state * leaving_grad, axis=-1)
    query_rest, key_grad, value_grad, decay_rest = local_pull(
        (mixed_grad, leaving_grad, log_total_grad)
    )
    query_low_grad = (query_part + query_rest).astype(jnp.bfloat16)
    key_low_grad = key_grad.astype(jnp.bfloat16)
    value_low_grad = value_grad.astype(jnp.bfloat16)
    logit_grad = (decay_part + decay_rest) * jax.nn.sigmoid(-logit) / 16.0
    bias_grad = jnp.sum(logit_grad, axis=0)
    logit_low = logit_grad.astype(jnp.bfloat16)
    up_rank_grad = left_t(rank_mid, logit_low)
    mid_low = right_t(logit_low, back_up_rank).astype(jnp.bfloat16)
    down_rank_grad = left_t(normed_low, mid_low)
    query_wgrad = left_t(normed_low, query_low_grad)
    key_wgrad = left_t(normed_low, key_low_grad)
    value_wgrad = left_t(normed_low, value_low_grad)
    normed_grad = (
        right_t(query_low_grad, back_query)
        + right_t(key_low_grad, back_key)
        + right_t(value_low_grad, back_value)
        + right_t(gate_low, back_gate)
        + right_t(mid_low, back_down_rank)
    )
    input_part, gain_one_grad = jax.vjp(rms_norm, inputs, gain_one)[1](normed_grad)
    tokens_grad = hidden_grad + input_part
    summed = (
        lax.psum_scatter(gain_one_grad, "seq", scatter_dimension=0, tiled=True),
        lax.psum_scatter(query_wgrad, "seq", scatter_dimension=0, tiled=True),
        lax.psum_scatter(key_wgrad, "seq", scatter_dimension=0, tiled=True),
        lax.psum_scatter(value_wgrad, "seq", scatter_dimension=0, tiled=True),
        lax.psum_scatter(gate_wgrad, "seq", scatter_dimension=0, tiled=True),
        lax.psum_scatter(down_rank_grad, "seq", scatter_dimension=0, tiled=True),
        lax.psum_scatter(up_rank_grad, "seq", scatter_dimension=1, tiled=True),
        lax.psum_scatter(bias_grad, "seq", scatter_dimension=0, tiled=True),
        lax.psum_scatter(heads_gain_grad, "seq", scatter_dimension=0, tiled=True),
        lax.psum_scatter(out_wgrad, "seq", scatter_dimension=0, tiled=True),
        lax.psum_scatter(gain_two_grad, "seq", scatter_dimension=0, tiled=True),
        lax.psum_scatter(fgate_wgrad, "seq", scatter_dimension=0, tiled=True),
        lax.psum_scatter(fup_wgrad, "seq", scatter_dimension=0, tiled=True),
        lax.psum_scatter(down_grad, "seq", scatter_dimension=0, tiled=True),
    )
    return (
        block_output,
        tokens_grad,
        summed[0],
        summed[1],
        summed[2],
        summed[3],
        summed[4],
        summed[5],
        summed[6],
        summed[7],
        summed[8],
        summed[9],
        summed[10],
        summed[11],
        summed[12],
        summed[13],
    )


def solution(mesh):
    return jax.shard_map(
        local,
        mesh=mesh,
        in_specs=(
            P("seq", None),
            P("seq"),
            P("seq", None),
            P("seq", None),
            P("seq", None),
            P("seq", None),
            P("seq", None),
            P(None, "seq"),
            P("seq"),
            P("seq"),
            P("seq", None),
            P("seq"),
            P("seq", None),
            P("seq", None),
            P("seq", None),
            P("seq", None),
        ),
        out_specs=(
            P("seq", None),
            P("seq", None),
            P("seq"),
            P("seq", None),
            P("seq", None),
            P("seq", None),
            P("seq", None),
            P("seq", None),
            P(None, "seq"),
            P("seq"),
            P("seq"),
            P("seq", None),
            P("seq"),
            P("seq", None),
            P("seq", None),
            P("seq", None),
        ),
        check_vma=False,
    )
```

profile of v0, /device:TPU:8, one launch (start us, length us, event | category | flops | bytes accessed | tf_op | source)
XLA Modules:
  0.0 2448.2 jit_solution(7890175636859240346)
XLA Ops:
  13.4 40.7 %all-reduce.12 = (bf16[1024]{0:T(1024)(128)(2,1)S(1)}, bf16[512]{0:T(512)(128)(2,1)S(1)}, bf16[1024]{0:T(1024)(128)(2,1)S(1)}, bf16[1024]{0:T(1024)(128)(2,1)S(1)}) all-reduce(bf16[1024]{0:T(1024)(128)(2,1)S(1)} %dynamic-update-slice, bf16[512]{0:T(512)(128)(2,1)S(1)} %dynamic-update-slice.1, ...), channel_id=1, replica_groups=mesh['seq'=32] {'seq'}, use_global_device_ids=true, to_apply=%add.3 | all-reduce | flops 3584 | bytes 14336
  54.1 34.2 %all-gather.3 = bf16[32,32,16]{1,2,0:T(8,128)(2,1)S(1)} all-gather(bf16[1,32,16]{1,2,0:T(8,128)(2,1)S(1)} %bitcast.271), channel_id=1, replica_groups=mesh['seq'=32] {'seq'}, dimensions={0}, use_global_device_ids=true | all-gather | bytes 33792 | tf_op jit(solution)/shard_map/all_gather | solution.py:136
  88.7 37.2 %all_gather.74 = bf16[16,512]{0,1:T(8,128)(2,1)S(1)} all-gather(bf16[16,16]{0,1:T(8,128)(2,1)S(1)} %copy.224), channel_id=1, replica_groups=mesh['seq'=32] {'seq'}, dimensions={1}, use_global_device_ids=true | all-gather | bytes 16896 | tf_op jit(solution)/shard_map/all_gather | solution.py:137
  203.2 52.0 %while.64 = (s32[]{:T(128)}, f32[4,128,256]{2,1,0:T(8,128)S(1)}, f32[16,4,128,256]{3,2,1,0:T(8,128)}, f32[16,4,128]{2,1,0:T(4,128)}, f32[16,4,128,1]{2,1,3,0:T(4...) while((s32[]{:T(128)}, f32[4,128,256]{2,1,0:T(8,128)S(1)}, ...), condition=%wide.region_3.4_spmd.clone, body=%wide.region_2.3_spmd.clone.sunk | while | flops 524291 | bytes 2637956 | solution.py:88
  259.5 34.4 %all-gather.4 = f32[32,4,128]{2,1,0:T(4,128)S(1)} all-gather(f32[1,4,128]{2,1,0:T(4,128)S(1)} %multiply_bitcast_fusion), channel_id=2, replica_groups=mesh['seq'=32] {'seq'}, dimensions={0}, use_global_device_ids=true | all-gather | bytes 67584 | tf_op jit(solution)/shard_map/all_gather | solution.py:15
  316.1 53.8 %all-gather.32.cloned.1.call-done = f32[128,128,256]{2,1,0:T(8,128)} async-done(((f32[4,128,256]{2,1,0:T(8,128)}), f32[128,128,256]{2,1,0:T(8,128)}) %all-gather.32.cloned.1.call-update) | async-done | bytes 16777232 | tf_op jit(solution)/shard_map/all_gather | solution.py:15
  369.8 39.9 %while.65 = (s32[]{:T(128)}, f32[4,128,256]{2,1,0:T(8,128)S(1)}, s32[]{:T(128)}, f32[32,4,128]{2,1,0:T(4,128)S(1)}, f32[32,4,128,256]{3,2,1,0:T(8,128)}, /*index=5*/s32[]{:T(128)}, s32[]{:T(128)}) while((s32[]{:T(128)}, f32[4,128,256]{2,1,0:T(8,128)S(1)}, s32[]{:T(128)}, f32[32,4,128]{2,1,0:T(4,128)S(1)}, ...), condition=%wide.region_6.7_spmd.clone, body=%wide.region_5.6_spmd.clone.sunk | while | flops 524292 | bytes 1579121 | solution.py:27
  446.4 38.9 %all-gather.24.cloned.1.call-done = bf16[1024,1024]{1,0:T(8,128)(2,1)} async-done(((bf16[32,1024]{1,0:T(8,128)(2,1)}), bf16[1024,1024]{1,0:T(8,128)(2,1)}) %all-gather.24.cloned.1.call-update) | async-done | bytes 2097168 | tf_op jit(solution)/shard_map/all_gather | solution.py:140
  492.6 63.1 %all-gather.26.cloned.1.call-done = bf16[1024,2816]{1,0:T(8,128)(2,1)} async-done(((bf16[32,2816]{1,0:T(8,128)(2,1)}), bf16[1024,2816]{1,0:T(8,128)(2,1)}) %all-gather.26.cloned.1.call-update) | async-done | bytes 5767184 | tf_op jit(solution)/shard_map/all_gather | solution.py:142
  567.2 57.6 %all-gather.28.cloned.1.call-done = bf16[1024,2816]{1,0:T(8,128)(2,1)} async-done(((bf16[32,2816]{1,0:T(8,128)(2,1)}), bf16[1024,2816]{1,0:T(8,128)(2,1)}) %all-gather.28.cloned.1.call-update) | async-done | bytes 5767184 | tf_op jit(solution)/shard_map/all_gather | solution.py:143
  636.6 57.3 %all-gather.30.cloned.1.call-done = bf16[2816,1024]{1,0:T(8,128)(2,1)} async-done(((bf16[88,1024]{1,0:T(8,128)(2,1)}), bf16[2816,1024]{1,0:T(8,128)(2,1)}) %all-gather.30.cloned.1.call-update) | async-done | bytes 5767184 | tf_op jit(solution)/shard_map/all_gather | solution.py:144
  818.6 78.6 %all-gather.34.cloned.1.call-done = f32[128,128,256]{2,1,0:T(8,128)} async-done(((f32[4,128,256]{2,1,0:T(8,128)}), f32[128,128,256]{2,1,0:T(8,128)}) %all-gather.34.cloned.1.call-update) | async-done | bytes 16777232 | tf_op jit(solution)/shard_map/all_gather | solution.py:15
  908.8 40.0 %while.66 = (s32[]{:T(128)}, f32[4,128,256]{2,1,0:T(8,128)S(1)}, s32[]{:T(128)}, f32[32,4,128]{2,1,0:T(4,128)S(1)}, f32[32,4,128,256]{3,2,1,0:T(8,128)}, /*index=5*/s32[]{:T(128)}, s32[]{:T(128)}) while((s32[]{:T(128)}, f32[4,128,256]{2,1,0:T(8,128)S(1)}, s32[]{:T(128)}, f32[32,4,128]{2,1,0:T(4,128)S(1)}, ...), condition=%wide.region_13.14_spmd.clone, body=%wide.region_12.13_spmd.clone.sunk | while | flops 524292 | bytes 1579121 | solution.py:27
  953.3 60.5 %while.63 = (s32[]{:T(128)}, f32[4,128,256]{2,1,0:T(8,128)S(1)}, f32[16,4,128]{2,0,1:T(8,128)S(1)}, f32[16,4,128,256]{3,2,1,0:T(8,128)}, f32[16,4,128,256]{3,2,1...) while((s32[]{:T(128)}, f32[4,128,256]{2,1,0:T(8,128)S(1)}, ...), condition=%wide.region_16.17_spmd, body=%wide.region_14.16_spmd.sunk | while | flops 524291 | bytes 3164309 | solution.py:88
  1166.6 39.5 %all-reduce.11 = (f32[1024]{0:T(1024)S(1)}, f32[512]{0:T(512)S(1)}, f32[1024]{0:T(1024)S(1)}, f32[1024]{0:T(1024)S(1)}) all-reduce(f32[1024]{0:T(1024)S(1)} %get-tuple-element.567, f32[512]{0:T(512)S(1)} %get-tuple-element.627, f32[1024]{0:T(1024)S(1)} %copy-done.59, f32[1024]{0:T(1024)S(1)} %copy-done.63), channel_id=5, replica_groups=mesh['seq'=32] {'seq'}, use_global_device_ids=true, to_apply=%region_25.26.clone | all-reduce | flops 3584 | bytes 28672
  1209.7 82.3 %reduce-scatter.31.cloned.1.call-done = f32[32,16]{1,0:T(8,128)} async-done(((f32[1024,16]{1,0:T(8,128)}), f32[32,16]{1,0:T(8,128)}) %reduce-scatter.31.cloned.1.call-update) | async-done | bytes 2064
  1293.4 138.2 %reduce-scatter.21.cloned.1.call-done = f32[32,1024]{1,0:T(8,128)} async-done(((f32[1024,1024]{1,0:T(8,128)}), f32[32,1024]{1,0:T(8,128)}) %reduce-scatter.21.cloned.1.call-update) | async-done | bytes 131088 | tf_op jit(solution)/shard_map/reduce_scatter | solution.py:293
  1431.7 139.5 %reduce-scatter.23.cloned.1.call-done = f32[32,1024]{1,0:T(8,128)} async-done(((f32[1024,1024]{1,0:T(8,128)}), f32[32,1024]{1,0:T(8,128)}) %reduce-scatter.23.cloned.1.call-update) | async-done | bytes 131088 | tf_op jit(solution)/shard_map/reduce_scatter | solution.py:298
  1571.2 162.5 %reduce-scatter.25.cloned.1.call-done = f32[32,2816]{1,0:T(8,128)} async-done(((f32[1024,2816]{1,0:T(8,128)}), f32[32,2816]{1,0:T(8,128)}) %reduce-scatter.25.cloned.1.call-update) | async-done | bytes 360464 | tf_op jit(solution)/shard_map/reduce_scatter | solution.py:300
  1733.7 153.6 %reduce-scatter.27.cloned.1.call-done = f32[32,2816]{1,0:T(8,128)} async-done(((f32[1024,2816]{1,0:T(8,128)}), f32[32,2816]{1,0:T(8,128)}) %reduce-scatter.27.cloned.1.call-update) | async-done | bytes 360464 | tf_op jit(solution)/shard_map/reduce_scatter | solution.py:301
  1887.2 153.5 %reduce-scatter.29.cloned.1.call-done = f32[88,1024]{1,0:T(8,128)} async-done(((f32[2816,1024]{1,0:T(8,128)}), f32[88,1024]{1,0:T(8,128)}) %reduce-scatter.29.cloned.1.call-update) | async-done | bytes 360464 | tf_op jit(solution)/shard_map/reduce_scatter | solution.py:302
  2040.7 126.2 %reduce-scatter.15.cloned.1.call-done = f32[32,512]{1,0:T(8,128)} async-done(((f32[1024,512]{1,0:T(8,128)}), f32[32,512]{1,0:T(8,128)}) %reduce-scatter.15.cloned.1.call-update) | async-done | bytes 65552 | tf_op jit(solution)/shard_map/reduce_scatter | solution.py:290
  2166.9 135.1 %reduce-scatter.17.cloned.1.call-done = f32[32,512]{1,0:T(8,128)} async-done(((f32[1024,512]{1,0:T(8,128)}), f32[32,512]{1,0:T(8,128)}) %reduce-scatter.17.cloned.1.call-update) | async-done | bytes 65552 | tf_op jit(solution)/shard_map/reduce_scatter | solution.py:291
  2302.0 139.0 %reduce-scatter.19.cloned.1.call-done = f32[32,1024]{1,0:T(8,128)} async-done(((f32[1024,1024]{1,0:T(8,128)}), f32[32,1024]{1,0:T(8,128)}) %reduce-scatter.19.cloned.1.call-update) | async-done | bytes 131088 | tf_op jit(solution)/shard_map/reduce_scatter | solution.py:292
  (601 shorter events, 664.3 us)
Async XLA Ops:
  7.2 130.1 %all-gather.18.cloned.1.call-start = ((), (), s32[]{:S(2)}) async-start(), calls=%async_computation.11 | async-start | bytes 1081344 | tf_op jit(solution)/shard_map/all_gather | solution.py:132
  7.9 136.2 %all-gather.20.cloned.1.call-start = ((), (), s32[]{:S(2)}) async-start(), calls=%async_computation.12 | async-start | bytes 1081344 | tf_op jit(solution)/shard_map/all_gather | solution.py:133
  8.7 170.2 %all-gather.16.cloned.1.call-start = ((), (), s32[]{:S(2)}) async-start(), calls=%async_computation.10 | async-start | bytes 2162688 | tf_op jit(solution)/shard_map/all_gather | solution.py:134
  9.4 360.4 %all-gather.32.cloned.1.call-start = ((), (), s32[]{:S(2)}) async-start(), calls=%async_computation.26 | async-start | bytes 17301504 | tf_op jit(solution)/shard_map/all_gather | solution.py:15
  12.4 131.7 %copy-start.5 = (bf16[1024,1024]{0,1:T(8,128)(2,1)}, bf16[1024,1024]{0,1:T(8,128)(2,1)S(1)}, u32[]{:S(2)}) copy-start(bf16[1024,1024]{0,1:T(8,128)(2,1)S(1)} %copy.222) | copy-start | bytes 6291460
  54.1 384.5 %copy-start.49 = (f32[1024]{0:T(1024)}, f32[1024]{0:T(1024)S(1)}, u32[]{:S(2)}) copy-start(f32[1024]{0:T(1024)S(1)} %convert_element_type.99) | copy-start | bytes 12292
  126.3 312.2 %copy-start.51 = (f32[1024]{0:T(1024)}, f32[1024]{0:T(1024)S(1)}, u32[]{:S(2)}) copy-start(f32[1024]{0:T(1024)S(1)} %fusion.125) | copy-start | bytes 12292
  157.8 145.0 %copy-start.3 = (f32[16,64,4,128]{3,1,0,2:T(8,128)}, f32[16,64,4,128]{3,1,0,2:T(8,128)S(1)}, u32[]{:S(2)}) copy-start(f32[16,64,4,128]{3,1,0,2:T(8,128)S(1)} %get-tuple-element.649) | copy-start | bytes 6291460
  256.0 182.6 %all-gather.22.cloned.1.call-start = ((), (), s32[]{:S(2)}) async-start(), calls=%async_computation.13 | async-start | bytes 2162688 | tf_op jit(solution)/shard_map/all_gather | solution.py:135
  256.6 228.7 %all-gather.24.cloned.1.call-start = ((), (), s32[]{:S(2)}) async-start(), calls=%async_computation.14 | async-start | bytes 2162688 | tf_op jit(solution)/shard_map/all_gather | solution.py:140
  257.2 298.5 %all-gather.26.cloned.1.call-start = ((), (), s32[]{:S(2)}) async-start(), calls=%async_computation.15 | async-start | bytes 5947392 | tf_op jit(solution)/shard_map/all_gather | solution.py:142
  257.9 366.9 %all-gather.28.cloned.1.call-start = ((), (), s32[]{:S(2)}) async-start(), calls=%async_computation.16 | async-start | bytes 5947392 | tf_op jit(solution)/shard_map/all_gather | solution.py:143
  258.7 435.3 %all-gather.30.cloned.1.call-start = ((), (), s32[]{:S(2)}) async-start(), calls=%async_computation.17 | async-start | bytes 5947392 | tf_op jit(solution)/shard_map/all_gather | solution.py:144
  259.4 637.8 %all-gather.34.cloned.1.call-start = ((), (), s32[]{:S(2)}) async-start(), calls=%async_computation.27 | async-start | bytes 17301504 | tf_op jit(solution)/shard_map/all_gather | solution.py:15
  784.8 423.5 %reduce-scatter.33.cloned.1.call-start = ((), (), s32[]{:S(2)}) async-start(), calls=%async_computation.29 | async-start | bytes 270336
  1045.3 246.8 %reduce-scatter.31.cloned.1.call-start = ((), (), s32[]{:S(2)}) async-start(), calls=%async_computation.28 | async-start | bytes 540672
  1046.9 384.7 %reduce-scatter.21.cloned.1.call-start = ((), (), s32[]{:S(2)}) async-start(), calls=%async_computation.21 | async-start | bytes 4325376 | tf_op jit(solution)/shard_map/reduce_scatter | solution.py:293
  1053.0 518.2 %reduce-scatter.23.cloned.1.call-start = ((), (), s32[]{:S(2)}) async-start(), calls=%async_computation.22 | async-start | bytes 4325376 | tf_op jit(solution)/shard_map/reduce_scatter | solution.py:298
  1060.2 673.5 %reduce-scatter.25.cloned.1.call-start = ((), (), s32[]{:S(2)}) async-start(), calls=%async_computation.23 | async-start | bytes 11894784 | tf_op jit(solution)/shard_map/reduce_scatter | solution.py:300
  1072.1 815.2 %reduce-scatter.27.cloned.1.call-start = ((), (), s32[]{:S(2)}) async-start(), calls=%async_computation.24 | async-start | bytes 11894784 | tf_op jit(solution)/shard_map/reduce_scatter | solution.py:301
  1084.2 956.5 %reduce-scatter.29.cloned.1.call-start = ((), (), s32[]{:S(2)}) async-start(), calls=%async_computation.25 | async-start | bytes 11894784 | tf_op jit(solution)/shard_map/reduce_scatter | solution.py:302
  1096.3 1070.6 %reduce-scatter.15.cloned.1.call-start = ((), (), s32[]{:S(2)}) async-start(), calls=%async_computation.18 | async-start | bytes 2162688 | tf_op jit(solution)/shard_map/reduce_scatter | solution.py:290
  1101.1 1200.9 %reduce-scatter.17.cloned.1.call-start = ((), (), s32[]{:S(2)}) async-start(), calls=%async_computation.19 | async-start | bytes 2162688 | tf_op jit(solution)/shard_map/reduce_scatter | solution.py:291
  1107.0 1334.1 %reduce-scatter.19.cloned.1.call-start = ((), (), s32[]{:S(2)}) async-start(), calls=%async_computation.20 | async-start | bytes 4325376 | tf_op jit(solution)/shard_map/reduce_scatter | solution.py:292
  (68 other events, 1103.6 us)
Sparse Core Ops, SparseCore 0:
  10.9 54.0 all-gather.17
  67.9 52.6 all-gather.19
  123.4 55.3 all-gather.15
  256.1 113.6 all-gather.31
  372.5 54.7 all-gather.21
  430.0 55.2 all-gather.23
  488.1 67.5 all-gather.25
  558.5 66.2 all-gather.27
  627.7 66.2 all-gather.29
  785.0 112.2 all-gather.33
  1045.4 114.4 reduce-scatter.32
  1162.0 129.9 reduce-scatter.30
  1294.9 136.7 reduce-scatter.20
  1434.4 136.7 reduce-scatter.22
  1573.9 159.6 reduce-scatter.24
  1736.4 150.7 reduce-scatter.26
  1890.0 150.6 reduce-scatter.28
  2043.4 123.4 reduce-scatter.14
  2169.8 132.1 reduce-scatter.16
  2304.7 136.2 reduce-scatter.18
where the time goes:
time: 2480 us; the launch traced here: 2450 us
  waiting for transfers between devices  1610 us (65%)
  matrix products  295 us (12%)
  blocking collectives  186 us (8%)
  other arithmetic  177 us (7%)
  local copies, waits for them, and re-layouts  166 us (7%)
    reduce_scatter x1, waiting for transfers between devices, local(): lax.psum_scatter(fgate_wgrad, 'seq', scatter_dimension=0, tiled=True)  162 us
    reduce_scatter x1, waiting for transfers between devices, local(): lax.psum_scatter(fup_wgrad, 'seq', scatter_dimension=0, tiled=True)  154 us
    reduce_scatter x1, waiting for transfers between devices, local(): lax.psum_scatter(down_grad, 'seq', scatter_dimension=0, tiled=True)  153 us
    reduce_scatter x1, waiting for transfers between devices, local(): lax.psum_scatter(out_wgrad, 'seq', scatter_dimension=0, tiled=True)  140 us
    reduce_scatter x1, waiting for transfers between devices, local(): lax.psum_scatter(value_wgrad, 'seq', scatter_dimension=0, tiled=True)  139 us
    reduce_scatter x1, waiting for transfers between devices, local(): lax.psum_scatter(gate_wgrad, 'seq', scatter_dimension=0, tiled=True)  138 us
    reduce_scatter x1, waiting for transfers between devices, local(): lax.psum_scatter(key_wgrad, 'seq', scatter_dimension=0, tiled=True)  135 us
    all_gather x2, waiting for transfers between devices, carried_in(): pieces = jax.tree.map(lambda part: lax.all_gather(part, axis), value)  132 us
  transfers between devices with their start and end apart: 20, of which 16 were waited for; matrix products, arithmetic and copies ran while one was open for 13% of the time, Pallas kernels for 0%

commit v1 on v0

v1 whole, which is shorter than its diff:
```python
import functools

import jax
import jax.numpy as jnp
from jax import lax
from jax.experimental import pallas as pl
from jax.experimental.pallas import tpu as pltpu
from jax.sharding import PartitionSpec as P

HEADS = 4
HK = 128
HV = 256
GROUP = 64

MESH = pl.DeviceIdType.MESH
LINE = 0
CORE = 3


def grid_of(count):
    core = 2 if count % 2 == 0 else 1
    rest = count // core
    third = max(k for k in range(1, rest + 1) if rest % k == 0 and k**3 <= rest)
    rest //= third
    second = max(k for k in range(1, rest + 1) if rest % k == 0 and k * k <= rest)
    return (rest // second, second, third, core)


class Place:
    def __init__(self, sizes):
        self.sizes = sizes
        rest = lax.axis_index("seq")
        here = []
        for size in sizes[::-1]:
            here.append(lax.rem(rest, size))
            rest = lax.div(rest, size)
        self.here = here[::-1]

    def index(self, **moved):
        out = 0
        for axis, size in enumerate(self.sizes):
            out = out * size + moved.get(f"a{axis}", self.here[axis])
        return out

    def toward(self, axis, step):
        return (self.index(**{f"a{axis}": self.here[axis] + step}),)

    def can(self, axis, step):
        return self.here[axis] > 0 if step < 0 else self.here[axis] < self.sizes[axis] - 1

    def greet(self):
        barrier = pltpu.get_barrier_semaphore()
        total = 0
        for axis, size in enumerate(self.sizes):
            for step in (-1, 1):
                if size == 1:
                    continue
                able = self.can(axis, step)

                @pl.when(able)
                def _(axis=axis, step=step):
                    pl.semaphore_signal(
                        barrier, inc=1, device_id=self.toward(axis, step), device_id_type=MESH
                    )

                total = total + able.astype(jnp.int32)
        pl.semaphore_wait(barrier, total)


def run_all(coroutines):
    active = list(coroutines)
    while active:
        still = []
        for coroutine in active:
            try:
                next(coroutine)
                still.append(coroutine)
            except StopIteration:
                pass
        active = still


class Gather:
    def __init__(self, place, part, order, buffer, columns, send, recv):
        self.place, self.part, self.order = place, part, order + (CORE,)
        self.buffer, self.columns, self.send, self.recv = buffer, columns, send, recv

    def copy(self, stage, line, along, step):
        place, axis = self.place, self.order[stage]
        where = []
        for a in range(4):
            if a == axis:
                where.append(along)
            elif a == LINE and LINE in self.order[:stage]:
                where.append(line)
            elif a in self.order[:stage]:
                where.append(slice(None))
            else:
                where.append(place.here[a])
        first, width = self.columns
        block = self.buffer.at[tuple(where) + (slice(None), pl.ds(first, width))]
        lane = 0 if place.sizes[axis] == 2 and axis != LINE else along
        if axis == LINE:
            line, lane = along, 0
        return pltpu.make_async_remote_copy(
            src_ref=block,
            dst_ref=block,
            send_sem=self.send.at[self.part, stage, line, lane, (step + 1) // 2],
            recv_sem=self.recv.at[self.part, stage, line, lane],
            device_id=place.toward(axis, step),
            device_id_type=MESH,
        )

    def each_step(self, stage, do):
        axis, place = self.order[stage], self.place
        if place.sizes[axis] == 1:
            return
        if place.sizes[axis] == 2 and axis != LINE:
            do(1 - 2 * place.here[axis], None)
            return
        for step in (-1, 1):
            do(step, place.can(axis, step))

    def launch(self, stage, line):
        axis, place = self.order[stage], self.place

        def do(step, able):
            def go():
                self.copy(stage, line, place.here[axis], step).start()

            go() if able is None else pl.when(able)(go)

        self.each_step(stage, do)

    def finish(self, stage, line):
        axis, place = self.order[stage], self.place
        size, here = place.sizes[axis], place.here[axis]
        if size == 1:
            return
        if size == 2:
            self.copy(stage, line, 1 - here, 1 - 2 * here).wait_recv()
            return
        for hop in range(1, size):
            for step in (-1, 1):
                along = here - step * hop
                valid = (along >= 0) & (along < size)

                @pl.when(valid)
                def _(along=along, step=step):
                    self.copy(stage, line, along, step).wait_recv()

                @pl.when(valid & place.can(axis, step))
                def _(along=along, step=step):
                    self.copy(stage, line, along, step).start()

    def steps(self):
        place = self.place
        size, here = place.sizes[LINE], place.here[LINE]
        spot = self.order.index(LINE)
        for stage in range(spot):
            self.launch(stage, here)
            yield
            self.finish(stage, here)
        for step in (-1, 1):

            @pl.when(place.can(LINE, step))
            def _(step=step):
                self.copy(spot, here, here, step).start()

        later = list(range(spot + 1, 4))
        for turn in range(size + len(later)):
            for age in range(min(turn, len(later)), -1, -1):
                far = turn - age
                if far >= size:
                    continue
                for step in (-1, 1) if far else (1,):
                    line = here - step * far
                    valid = (line >= 0) & (line < size)

                    def advance(line=line, step=step, far=far, age=age):
                        if age == 0 and far:
                            self.copy(spot, line, line, step).wait_recv()

                            @pl.when(place.can(LINE, step))
                            def _():
                                self.copy(spot, line, line, step).start()

                        if age:
                            self.finish(later[age - 1], line)
                        if age < len(later):
                            self.launch(later[age], line)

                    pl.when(valid)(advance) if far else advance()
            yield

    def drain(self):
        place = self.place
        size, here = place.sizes[LINE], place.here[LINE]
        spot = self.order.index(LINE)
        for line in range(size):
            for step in (-1, 1):

                @pl.when(place.can(LINE, step) & ((line <= here) if step > 0 else (line >= here)))
                def _(line=line, step=step):
                    self.copy(spot, line, line, step).wait_send()

        for stage in range(4):
            if stage == spot:
                continue
            axis = self.order[stage]
            lines = [here] if stage < spot else list(range(size))
            for line in lines:
                if place.sizes[axis] == 1:
                    continue
                if place.sizes[axis] == 2:
                    self.copy(stage, line, place.here[axis], 1 - 2 * place.here[axis]).wait_send()
                    continue
                for step in (-1, 1):
                    for along in range(place.sizes[axis]):
                        at = place.here[axis]

                        @pl.when(place.can(axis, step) & ((along <= at) if step > 0 else (along >= at)))
                        def _(line=line, step=step, along=along, stage=stage):
                            self.copy(stage, line, along, step).wait_send()


ORDERS = ((2, 0, 1), (1, 0, 2), (0, 2, 1), (0, 1, 2))


def gather_kernel(sizes, parts, count, *refs):
    shards, buffers = refs[:count], refs[count : 2 * count]
    send, recv, own = refs[2 * count :]
    place = Place(sizes)
    locals_ = [
        pltpu.make_async_copy(shard, buffer.at[tuple(place.here)], own.at[k])
        for k, (shard, buffer) in enumerate(zip(shards, buffers))
    ]
    for copy in locals_:
        copy.start()
    place.greet()
    for copy in locals_:
        copy.wait()
    gathers = [
        Gather(place, k, order, buffers[which], columns, send, recv)
        for k, (which, columns, order) in enumerate(parts)
    ]
    run_all([g.steps() for g in gathers])
    for g in gathers:
        g.drain()


def lanes_of(sizes):
    return max([1] + [size for size in sizes[1:] if size > 2])


def gather_all(shards, parts, sizes, collective_id):
    lanes = lanes_of(sizes)
    out = pl.pallas_call(
        functools.partial(gather_kernel, sizes, parts, len(shards)),
        out_shape=[jax.ShapeDtypeStruct(sizes + s.shape, s.dtype) for s in shards],
        in_specs=[pl.BlockSpec(memory_space=pltpu.VMEM)] * len(shards),
        out_specs=[pl.BlockSpec(memory_space=pl.ANY)] * len(shards),
        scratch_shapes=[
            pltpu.SemaphoreType.DMA((len(parts), 4, sizes[0], lanes, 2)),
            pltpu.SemaphoreType.DMA((len(parts), 4, sizes[0], lanes)),
            pltpu.SemaphoreType.DMA((len(shards),)),
        ],
        compiler_params=pltpu.CompilerParams(collective_id=collective_id, has_side_effects=True),
    )(*shards)
    return [o.reshape((-1,) + o.shape[5:]) for o in out]


class Scatter:
    def __init__(self, place, part, order, partial, columns, held, bufs, out, load, send, recv):
        self.place, self.part, self.order = place, part, (CORE,) + order
        self.partial, self.columns, self.held, self.bufs, self.out = partial, columns, held, bufs, out
        self.load, self.send, self.recv = load, send, recv

    def own(self, line):
        first, width = self.columns
        where = (line, slice(None), slice(None), self.place.here[CORE], slice(None), pl.ds(first, width))
        return pltpu.make_async_copy(self.partial.at[where], self.held.at[line], self.load.at[self.part, line])

    def block(self, stage, line, along):
        where, done = [], self.order[:stage]
        for a in range(3):
            if a == self.order[stage]:
                where.append(along)
            elif a in done:
                where.append(self.place.here[a])
            elif a == LINE:
                where.append(line)
            else:
                where.append(slice(None))
        return tuple(where)

    def slot(self, stage, line, slot):
        axis = self.order[stage]
        if axis == LINE:
            return (slot,)
        if LINE in self.order[:stage]:
            line = 0
        return (line, 0 if self.place.sizes[axis] == 2 else slot)

    def copy(self, stage, line, along, step):
        place, axis = self.place, self.order[stage]
        size = place.sizes[axis]
        first, width = self.columns
        if axis == CORE:
            where = (line, slice(None), slice(None), along, slice(None), pl.ds(first, width))
            source = self.partial.at[where]
        else:
            source = self.held.at[self.block(stage, line, along)]
        arrives = place.here[axis] + step == along
        number = jnp.where(arrives & (step < 0), size, along) if size > 2 else 0
        sem = self.slot(stage, line, along)
        if axis == LINE:
            sem = sem + (0,)
        there = self.slot(stage, line, number)
        return pltpu.make_async_remote_copy(
            src_ref=source,
            dst_ref=self.bufs[stage].at[there],
            send_sem=self.send.at[(self.part, stage) + sem],
            recv_sem=self.recv.at[(self.part, stage) + there + ((0,) if axis == LINE else ())],
            device_id=place.toward(axis, step),
            device_id_type=MESH,
        )

    def wait(self, stage, line, number):
        there = self.slot(stage, line, number)
        buf = self.bufs[stage].at[there]
        axis = self.order[stage]
        pltpu.make_async_copy(
            buf, buf, self.recv.at[(self.part, stage) + there + ((0,) if axis == LINE else ())]
        ).wait()
        return self.bufs[stage], there

    def add(self, stage, line, along, number, last=False):
        buf, there = self.wait(stage, line, number)
        if last:
            first, width = self.columns
            self.out[:, pl.ds(first, width)] += buf[there].astype(jnp.float32)
            return
        where = self.block(stage, line, along)
        if self.order[stage] == CORE:
            where = (line, slice(None), slice(None))
        total = self.held[where].astype(jnp.float32) + buf[there].astype(jnp.float32)
        self.held[where] = total.astype(self.held.dtype)

    def launch(self, stage, line):
        axis, place = self.order[stage], self.place
        size, here = place.sizes[axis], place.here[axis]
        if size == 2:
            self.copy(stage, line, 1 - here, 1 - 2 * here).start()
        elif size > 2:
            for turn in range(1, size):
                for step, along in ((1, size - turn), (-1, turn - 1)):

                    @pl.when((here == (0 if step > 0 else size - 1)))
                    def _(step=step, along=along):
                        self.copy(stage, line, along, step).start()

    def pass_on(self, stage, line, turn):
        axis, place = self.order[stage], self.place
        size, here = place.sizes[axis], place.here[axis]
        for step, along in ((1, size - turn), (-1, turn - 1)):
            ahead = (along > here) if step > 0 else (along < here)

            @pl.when(ahead & place.can(axis, -step))
            def _(step=step, along=along):
                self.add(stage, line, along, along)
                self.copy(stage, line, along, step).start()

    def finish(self, stage, line):
        axis, place = self.order[stage], self.place
        size, here = place.sizes[axis], place.here[axis]
        if size == 2:
            self.add(stage, line, here, 0, stage == 3)
        elif size > 2:
            for step, number in ((-1, here), (1, size)):

                @pl.when(place.can(axis, step))
                def _(number=number):
                    self.add(stage, line, here, number, stage == 3)

    def whole(self, stage, line):
        for turn in range(1, self.place.sizes[self.order[stage]]):
            if self.place.sizes[self.order[stage]] > 2:
                self.pass_on(stage, line, turn)
        self.finish(stage, line)

    def line_hop(self, along, hop):
        place, stage = self.place, self.order.index(LINE)
        size, here = place.sizes[LINE], place.here[LINE]
        for step, at, ahead in ((1, hop, along > hop), (-1, size - 1 - hop, along < size - 1 - hop)):
            if not ahead:
                continue

            @pl.when(here == at)
            def _(step=step):
                if hop:
                    self.add(stage, here, along, along)
                self.copy(stage, here, along, step).start()

    def steps(self):
        place = self.place
        size, here = place.sizes[LINE], place.here[LINE]
        lines = []
        for k in range(size):
            lines.append(k // 2 if k % 2 == 0 else size - 1 - k // 2)
        spot = self.order.index(LINE)

        def begin(k):
            self.own(lines[k]).start()
            self.launch(0, lines[k])

        begin(0)
        yield
        for turn in range(2 * size + spot - 2):
            if turn + 1 < size:
                begin(turn + 1)
            for k in range(size):
                hop = turn - k - spot
                if 0 <= hop < size - 1:
                    self.line_hop(lines[k], hop)
            for stage in range(spot - 1, -1, -1):
                k = turn - stage
                if not 0 <= k < size:
                    continue
                if stage == 0:
                    self.own(lines[k]).wait()
                self.whole(stage, lines[k])
                if stage + 1 < spot:
                    self.launch(stage + 1, lines[k])
            yield
        if spot == 3:
            self.begin_out()
        self.finish(spot, here)
        for stage in range(spot + 1, 4):
            if stage == 3:
                self.begin_out()
            self.launch(stage, here)
            yield
            self.whole(stage, here)

    def begin_out(self):
        first, width = self.columns
        mine = self.held[tuple(self.place.here[:3])]
        self.out[:, pl.ds(first, width)] = mine.astype(jnp.float32)

    def drain(self):
        place = self.place
        spot = self.order.index(LINE)
        for stage in range(4):
            axis = self.order[stage]
            size, here = place.sizes[axis], place.here[axis]
            for line in range(place.sizes[LINE]) if stage < spot else [place.here[LINE]]:
                if size == 2:
                    self.copy(stage, line, 1 - here, 1 - 2 * here).wait_send()
                elif size > 2:
                    for along in range(size):
                        for step in (-1, 1):

                            @pl.when((along > here) if step > 0 else (along < here))
                            def _(along=along, step=step, line=line, stage=stage):
                                self.copy(stage, line, along, step).wait_send()


def scatter_kernel(sizes, parts, count, *refs):
    partials, outs = refs[:count], refs[count : 2 * count]
    load, send, recv = refs[2 * count : 2 * count + 3]
    scratch = list(refs[2 * count + 3 :])
    place = Place(sizes)
    place.greet()
    scatters = []
    for k, (which, columns, order) in enumerate(parts):
        held, *bufs = scratch[5 * k : 5 * k + 5]
        scatters.append(
            Scatter(place, k, order, partials[which], columns, held, bufs, outs[which], load, send, recv)
        )
    run_all([s.steps() for s in scatters])
    for s in scatters:
        s.drain()


def scatter_scratch(sizes, parts, shapes, dtype):
    scratch = []
    for which, (_, width), order in parts:
        rows = shapes[which][-2]
        scratch.append(pltpu.VMEM(sizes[:3] + (rows, width), dtype))
        stages = (CORE,) + order
        for stage, axis in enumerate(stages):
            free = tuple(sizes[a] for a in range(1, 3) if a not in stages[: stage + 1])
            slots = 1 if sizes[axis] <= 2 else sizes[axis] + 1
            if axis == LINE:
                lead = (slots,)
            else:
                lead = (1 if LINE in stages[:stage] else sizes[LINE], slots)
            scratch.append(pltpu.VMEM(lead + free + (rows, width), dtype))
    return scratch


def scatter_all(partials, parts, sizes, collective_id):
    count = 1
    for size in sizes:
        count *= size
    partials = [p.reshape(sizes + (p.shape[0] // count, p.shape[1])) for p in partials]
    lanes = max([1] + [size + 1 for size in sizes[1:] if size > 2])
    sems = (len(parts), 4, sizes[0] + 1, lanes)
    return pl.pallas_call(
        functools.partial(scatter_kernel, sizes, parts, len(partials)),
        out_shape=[jax.ShapeDtypeStruct(p.shape[4:], jnp.float32) for p in partials],
        in_specs=[pl.BlockSpec(memory_space=pl.ANY)] * len(partials),
        out_specs=[pl.BlockSpec(memory_space=pltpu.VMEM)] * len(partials),
        scratch_shapes=[
            pltpu.SemaphoreType.DMA((len(parts), sizes[0])),
            pltpu.SemaphoreType.DMA(sems),
            pltpu.SemaphoreType.DMA(sems),
        ]
        + scatter_scratch(sizes, parts, [p.shape for p in partials], partials[0].dtype),
        compiler_params=pltpu.CompilerParams(
            collective_id=collective_id, has_side_effects=True, vmem_limit_bytes=60 << 20
        ),
    )(*partials)


def partners_of(sizes):
    hops = []
    for axis in (2, 1, 0):
        stride = 1
        while stride < sizes[axis]:
            hops.append((axis, stride))
            stride *= 2
    return hops


def scan_kernel(
    sizes, backward, state_ref, logs_ref, out_ref,
    sib, sib_logs, first, first_logs, pre, pre_logs, total, total_logs, wire, wire_logs, got, got_logs, other, send, recv,
):
    place = Place(sizes)
    core = place.here[CORE]
    hops = partners_of(sizes)
    half = HEADS // 2
    mine, theirs = pl.ds(half * core, half), pl.ds(half * (1 - core), half)
    sibling = place.toward(CORE, 1 - 2 * core)

    def bit(axis, stride):
        return lax.rem(lax.div(place.here[axis], stride), 2)

    def partner(axis, stride):
        return place.toward(axis, (1 - 2 * bit(axis, stride)) * stride)

    barrier = pltpu.get_barrier_semaphore()
    for device in [sibling] + [partner(*hop) for hop in hops]:
        pl.semaphore_signal(barrier, inc=1, device_id=device, device_id_type=MESH)
    pl.semaphore_wait(barrier, 1 + len(hops))

    def remote(source, target, number, device):
        return pltpu.make_async_remote_copy(
            src_ref=source, dst_ref=target, send_sem=send.at[number], recv_sem=recv.at[number],
            device_id=device, device_id_type=MESH,
        )

    def scaled(logs, states, added):
        return [jnp.exp(logs[h, 0:1, :]) * states[h] + added[h] for h in range(half)]

    swap = [
        remote(state_ref.at[theirs], sib, 0, sibling),
        remote(logs_ref.at[theirs], sib_logs, 1, sibling),
    ]
    for copy in swap:
        copy.start()
    for copy in swap:
        copy.wait_recv()
    starts = core == (1 if backward else 0)

    @pl.when(starts)
    def _():
        first[...] = state_ref[mine]
        first_logs[...] = logs_ref[mine]
        new = scaled(sib_logs, first, sib)
        for h in range(half):
            total[h] = new[h]

    @pl.when(jnp.logical_not(starts))
    def _():
        first[...] = sib[...]
        first_logs[...] = sib_logs[...]
        new = scaled(logs_ref.at[mine], first, state_ref.at[mine])
        for h in range(half):
            total[h] = new[h]

    total_logs[...] = logs_ref[mine] + sib_logs[...]
    pre[...] = jnp.zeros_like(pre)
    pre_logs[...] = jnp.zeros_like(pre_logs)
    pending = list(swap)
    for k, (axis, stride) in enumerate(hops):
        last = k == len(hops) - 1
        wire[k] = total[...].astype(wire.dtype)
        wire_logs[k] = total_logs[...]
        copies = [
            remote(wire.at[k], got.at[k], 2 + 2 * k, partner(axis, stride)),
            remote(wire_logs.at[k], got_logs.at[k], 3 + 2 * k, partner(axis, stride)),
        ]
        for copy in copies:
            copy.start()
        pending += copies
        for copy in copies:
            copy.wait_recv()
        earlier = bit(axis, stride) == (1 if backward else 0)
        arrived = [got[k, h].astype(jnp.float32) for h in range(half)]

        @pl.when(jnp.logical_not(earlier))
        def _(k=k, arrived=arrived, last=last):
            new = scaled(pre_logs, arrived, pre)
            for h in range(half):
                pre[h] = new[h]
            pre_logs[...] = pre_logs[...] + got_logs[k]
            if not last:
                new = scaled(total_logs, arrived, total)
                for h in range(half):
                    total[h] = new[h]

        if not last:

            @pl.when(earlier)
            def _(k=k, arrived=arrived):
                new = scaled(got_logs.at[k], total, arrived)
                for h in range(half):
                    total[h] = new[h]

            total_logs[...] = total_logs[...] + got_logs[k]
    second = scaled(first_logs, pre, first)

    @pl.when(starts)
    def _():
        for h in range(half):
            other[h] = second[h]
        out_ref[mine] = pre[...]

    @pl.when(jnp.logical_not(starts))
    def _():
        other[...] = pre[...]
        for h in range(half):
            out_ref[half * core + h] = second[h]

    back = remote(other, out_ref.at[mine], 2 + 2 * len(hops), sibling)
    back.start()
    back.wait_recv()
    for copy in pending + [back]:
        copy.wait_send()


def entering(state, logs, sizes, backward, collective_id):
    half, hops = HEADS // 2, len(partners_of(sizes))
    block, tile = (half, HV, HK), (half, 8, HK)
    spread = jnp.broadcast_to(logs[:, None, :], (HEADS, 8, HK))
    return pl.pallas_call(
        functools.partial(scan_kernel, sizes, backward),
        out_shape=jax.ShapeDtypeStruct(state.shape, jnp.float32),
        in_specs=[pl.BlockSpec(memory_space=pltpu.VMEM)] * 2,
        out_specs=pl.BlockSpec(memory_space=pltpu.VMEM),
        scratch_shapes=[
            pltpu.VMEM(block, jnp.float32), pltpu.VMEM(tile, jnp.float32),
            pltpu.VMEM(block, jnp.float32), pltpu.VMEM(tile, jnp.float32),
            pltpu.VMEM(block, jnp.float32), pltpu.VMEM(tile, jnp.float32),
            pltpu.VMEM(block, jnp.float32), pltpu.VMEM(tile, jnp.float32),
            pltpu.VMEM((hops,) + block, jnp.bfloat16), pltpu.VMEM((hops,) + tile, jnp.float32),
            pltpu.VMEM((hops,) + block, jnp.bfloat16), pltpu.VMEM((hops,) + tile, jnp.float32),
            pltpu.VMEM(block, jnp.float32),
            pltpu.SemaphoreType.DMA((3 + 2 * hops,)),
            pltpu.SemaphoreType.DMA((3 + 2 * hops,)),
        ],
        compiler_params=pltpu.CompilerParams(
            collective_id=collective_id, has_side_effects=True, vmem_limit_bytes=32 << 20
        ),
    )(state, spread)


def matmul(left, right):
    return jnp.dot(left, right, preferred_element_type=jnp.float32)


def left_t(left, right):
    return lax.dot_general(
        left, right, (((0,), (0,)), ((), ())), preferred_element_type=jnp.float32
    )


def right_t(left, right):
    return lax.dot_general(
        left, right, (((1,), (1,)), ((), ())), preferred_element_type=jnp.float32
    )


def rms_norm(values, gain):
    return values * lax.rsqrt(jnp.mean(values * values, axis=-1, keepdims=True) + 1e-06) * gain


def head_norm(mixed, gain, gate):
    length = mixed.shape[0]
    shaped = mixed.reshape(length, HEADS, HV)
    headed = shaped * lax.rsqrt(jnp.mean(shaped * shaped, axis=-1, keepdims=True) + 1e-06)
    return headed.reshape(length, HEADS * HV) * gain * jax.nn.silu(gate)


def swiglu(fgate, fup):
    return jax.nn.silu(fgate) * fup


def mixer_local(query, key, value_rows, decay):
    length = query.shape[0]
    blocks = length // GROUP
    q_blocks = query.reshape(blocks, GROUP, HEADS, HK) * HK ** (-0.5)
    k_blocks = key.reshape(blocks, GROUP, HEADS, HK)
    v_blocks = value_rows.reshape(blocks, GROUP, HEADS, HV)
    within = jnp.cumsum(decay.reshape(blocks, GROUP, HEADS, HK), axis=1)
    total = within[:, -1]
    query_with_decay = q_blocks * jnp.exp(within)
    k_decayed = k_blocks * jnp.exp(-within)
    key_to_segment_end = k_blocks * jnp.exp(total[:, None] - within)
    causal = (jnp.arange(GROUP)[:, None] >= jnp.arange(GROUP)[None, :]).astype(jnp.float32)
    scores = (
        jnp.einsum("nihk,njhk->nhij", query_with_decay, k_decayed, precision=lax.Precision.HIGHEST)
        * causal
    )
    segment_result = jnp.einsum(
        "nhij,njhv->nihv", scores, v_blocks, precision=lax.Precision.HIGHEST
    )
    updates = jnp.einsum(
        "njhk,njhv->nhkv", key_to_segment_end, v_blocks, precision=lax.Precision.HIGHEST
    )

    def advance(state_matrix, pair):
        factor, state_increment = pair
        return (jnp.exp(factor)[:, :, None] * state_matrix + state_increment, state_matrix)

    final, starts = lax.scan(advance, jnp.zeros((HEADS, HK, HV), jnp.float32), (total, updates))
    segment_result = segment_result + jnp.einsum(
        "nihk,nhkv->nihv", query_with_decay, starts, precision=lax.Precision.HIGHEST
    )
    return (segment_result.reshape(length, HEADS * HV), final, jnp.sum(total, axis=0))


def mixer_carried(query, decay, incoming_state):
    length = query.shape[0]
    blocks = length // GROUP
    q_blocks = query.reshape(blocks, GROUP, HEADS, HK) * HK ** (-0.5)
    within = jnp.cumsum(decay.reshape(blocks, GROUP, HEADS, HK), axis=1)
    before = jnp.cumsum(within[:, -1], axis=0) - within[:, -1]
    weighted_scores = q_blocks * jnp.exp(within + before[:, None])
    segment_result = jnp.einsum(
        "blfs,fsq->blfq", weighted_scores, incoming_state, precision=lax.Precision.HIGHEST
    )
    return segment_result.reshape(length, HEADS * HV)


PARTS = (
    (0, (0, 128), ORDERS[0]),
    (1, (0, 1024), ORDERS[0]),
    (1, (1024, 1024), ORDERS[1]),
    (1, (2048, 1024), ORDERS[2]),
    (2, (0, 1024), ORDERS[3]),
    (3, (0, 2816), ORDERS[0]),
    (4, (0, 2816), ORDERS[1]),
    (5, (0, 512), ORDERS[2]),
    (5, (512, 512), ORDERS[3]),
)
BACK_PARTS = tuple((which, columns, order[::-1]) for which, columns, order in PARTS)
TILE = (16, 128)


def packed(pieces):
    count = pieces[0].shape[0]
    flat = jnp.concatenate([p.reshape(count, -1) for p in pieces], axis=1)
    flat = jnp.pad(flat, ((0, 0), (0, TILE[0] * TILE[1] - flat.shape[1])))
    return flat.reshape(count * TILE[0], TILE[1])


def unpacked(tiles, shapes):
    count = tiles.shape[0] // TILE[0]
    flat = tiles.reshape(count, TILE[0] * TILE[1])
    out, at = [], 0
    for shape in shapes:
        size = 1
        for extent in shape:
            size *= extent
        out.append(flat[:, at : at + size].reshape((count,) + shape))
        at += size
    return out


def local(
    tokens,
    norm_gain,
    query_weight,
    key_weight,
    value_weight,
    gate_weight,
    rank_down,
    rank_up,
    gate_bias,
    head_gain,
    out_weight,
    ffn_gain,
    ffn_gate,
    ffn_up,
    ffn_down,
    cotangent,
):
    count = lax.axis_size("seq")
    sizes = grid_of(count)
    small = (norm_gain, rank_down, rank_up, gate_bias, head_gain, ffn_gain)
    shapes = [s.shape for s in small]
    projections = jnp.concatenate([query_weight, key_weight, value_weight, gate_weight], axis=1)
    tiles, full_proj, full_out, full_fgate, full_fup, full_fdown = gather_all(
        [packed([s[None] for s in small]), projections, out_weight, ffn_gate, ffn_up, ffn_down], PARTS, sizes, 0
    )
    pieces = unpacked(tiles, shapes)
    full_gain, full_bias, full_head_gain, full_ffn_gain = (pieces[k].reshape(-1) for k in (0, 3, 4, 5))
    full_down_rank = pieces[1].reshape(-1, rank_down.shape[1])
    full_up_rank = pieces[2].transpose(1, 0, 2).reshape(rank_up.shape[0], -1)
    full_query, full_key = full_proj[:, :512], full_proj[:, 512:1024]
    full_value, full_gate = full_proj[:, 1024:2048], full_proj[:, 2048:]
    gain_one = full_gain.astype(jnp.float32)
    gain_two = full_ffn_gain.astype(jnp.float32)
    heads_gain = full_head_gain.astype(jnp.float32)
    inputs = tokens.astype(jnp.float32)
    normed = rms_norm(inputs, gain_one)
    normed_low = normed.astype(jnp.bfloat16)
    query_low = matmul(normed_low, full_query).astype(jnp.bfloat16)
    key_low = matmul(normed_low, full_key).astype(jnp.bfloat16)
    value_low = matmul(normed_low, full_value).astype(jnp.bfloat16)
    rank_mid = matmul(normed_low, full_down_rank).astype(jnp.bfloat16)
    logit = matmul(rank_mid, full_up_rank) + full_bias.astype(jnp.float32)
    decay = jax.nn.log_sigmoid(logit) / 16.0
    gate = matmul(normed_low, full_gate)
    query_f = query_low.astype(jnp.float32)
    key_f = key_low.astype(jnp.float32)
    value_f = value_low.astype(jnp.float32)
    local_out, local_pull = jax.vjp(mixer_local, query_f, key_f, value_f, decay)
    mixed_local, final_state, log_total = local_out
    factor = jnp.exp(log_total)
    incoming_state = entering(final_state.transpose(0, 2, 1), log_total, sizes, False, 2).transpose(0, 2, 1)
    carried_out, carried_pull = jax.vjp(mixer_carried, query_f, decay, incoming_state)
    mixed = mixed_local + carried_out
    gated, gated_pull = jax.vjp(head_norm, mixed, heads_gain, gate)
    gated_low = gated.astype(jnp.bfloat16)
    hidden_state = inputs + matmul(gated_low, full_out)
    ffn_in, ffn_norm_pull = jax.vjp(rms_norm, hidden_state, gain_two)
    ffn_low = ffn_in.astype(jnp.bfloat16)
    fgate = matmul(ffn_low, full_fgate)
    fup = matmul(ffn_low, full_fup)
    inner, inner_pull = jax.vjp(swiglu, fgate, fup)
    inner_low = inner.astype(jnp.bfloat16)
    block_output = hidden_state + matmul(inner_low, full_fdown)
    upstream = cotangent.astype(jnp.float32)
    down_grad = left_t(inner_low, cotangent)
    inner_grad = right_t(cotangent, full_fdown)
    fgate_grad, fup_grad = inner_pull(inner_grad)
    fgate_low = fgate_grad.astype(jnp.bfloat16)
    fup_low = fup_grad.astype(jnp.bfloat16)
    fgate_wgrad = left_t(ffn_low, fgate_low)
    fup_wgrad = left_t(ffn_low, fup_low)
    ffn_in_grad = right_t(fgate_low, full_fgate) + right_t(fup_low, full_fup)
    hidden_part, gain_two_grad = ffn_norm_pull(ffn_in_grad)
    hidden_grad = upstream + hidden_part
    hidden_low = hidden_grad.astype(jnp.bfloat16)
    out_wgrad = left_t(gated_low, hidden_low)
    gated_grad = right_t(hidden_low, full_out)
    mixed_grad, heads_gain_grad, gate_grad = gated_pull(gated_grad)
    gate_low = gate_grad.astype(jnp.bfloat16)
    gate_wgrad = left_t(normed_low, gate_low)
    query_part, decay_part, entering_grad = carried_pull(mixed_grad)
    leaving_grad = entering(entering_grad.transpose(0, 2, 1), log_total, sizes, True, 3).transpose(0, 2, 1)
    log_total_grad = factor * jnp.sum(incoming_state * leaving_grad, axis=-1)
    query_rest, key_grad, value_grad, decay_rest = local_pull(
        (mixed_grad, leaving_grad, log_total_grad)
    )
    query_low_grad = (query_part + query_rest).astype(jnp.bfloat16)
    key_low_grad = key_grad.astype(jnp.bfloat16)
    value_low_grad = value_grad.astype(jnp.bfloat16)
    logit_grad = (decay_part + decay_rest) * jax.nn.sigmoid(-logit) / 16.0
    bias_grad = jnp.sum(logit_grad, axis=0)
    logit_low = logit_grad.astype(jnp.bfloat16)
    up_rank_grad = left_t(rank_mid, logit_low)
    mid_low = right_t(logit_low, full_up_rank).astype(jnp.bfloat16)
    down_rank_grad = left_t(normed_low, mid_low)
    query_wgrad = left_t(normed_low, query_low_grad)
    key_wgrad = left_t(normed_low, key_low_grad)
    value_wgrad = left_t(normed_low, value_low_grad)
    normed_grad = (
        right_t(query_low_grad, full_query)
        + right_t(key_low_grad, full_key)
        + right_t(value_low_grad, full_value)
        + right_t(gate_low, full_gate)
        + right_t(mid_low, full_down_rank)
    )
    input_part, gain_one_grad = jax.vjp(rms_norm, inputs, gain_one)[1](normed_grad)
    tokens_grad = hidden_grad + input_part
    tiles = packed(
        [
            gain_one_grad.reshape(count, -1),
            down_rank_grad.reshape(count, -1),
            up_rank_grad.reshape(rank_up.shape[0], count, -1).transpose(1, 0, 2),
            bias_grad.reshape(count, -1),
            heads_gain_grad.reshape(count, -1),
            gain_two_grad.reshape(count, -1),
        ]
    ).astype(jnp.bfloat16)
    proj_wgrad = jnp.concatenate([query_wgrad, key_wgrad, value_wgrad, gate_wgrad], axis=1)
    summed = scatter_all(
        [tiles] + [g.astype(jnp.bfloat16) for g in (proj_wgrad, out_wgrad, fgate_wgrad, fup_wgrad, down_grad)],
        BACK_PARTS, sizes, 1,
    )
    gain_sum, down_sum, up_sum, bias_sum, head_sum, ffn_sum = [p[0] for p in unpacked(summed[0], shapes)]
    proj_sum = summed[1]
    return (
        block_output,
        tokens_grad,
        gain_sum,
        proj_sum[:, :512],
        proj_sum[:, 512:1024],
        proj_sum[:, 1024:2048],
        proj_sum[:, 2048:],
        down_sum,
        up_sum,
        bias_sum,
        head_sum,
        summed[2],
        ffn_sum,
        summed[3],
        summed[4],
        summed[5],
    )


def solution(mesh):
    return jax.shard_map(
        local,
        mesh=mesh,
        in_specs=(
            P("seq", None),
            P("seq"),
            P("seq", None),
            P("seq", None),
            P("seq", None),
            P("seq", None),
            P("seq", None),
            P(None, "seq"),
            P("seq"),
            P("seq"),
            P("seq", None),
            P("seq"),
            P("seq", None),
            P("seq", None),
            P("seq", None),
            P("seq", None),
        ),
        out_specs=(
            P("seq", None),
            P("seq", None),
            P("seq"),
            P("seq", None),
            P("seq", None),
            P("seq", None),
            P("seq", None),
            P("seq", None),
            P(None, "seq"),
            P("seq"),
            P("seq"),
            P("seq", None),
            P("seq"),
            P("seq", None),
            P("seq", None),
            P("seq", None),
        ),
        check_vma=False,
    )
```

time: 2480 us -> 875 us (0.35); the launches traced: 2450 us -> 868 us
  waiting for transfers between devices: 1610 us -> 0 us
  Pallas kernels: 0 us -> 298 us
  blocking collectives: 186 us -> 0 us
  other arithmetic: 177 us -> 115 us
    reduce_scatter x8 -> x0, waiting for transfers between devices: 1150 us -> none  [the longest x1 162 us: local(): lax.psum_scatter(fgate_wgrad, 'seq', scatter_dimension=0, tiled=True)]
    all_gather x10 -> x0, waiting for transfers between devices: 370 us -> none  [the longest x2 132 us: carried_in(): pieces = jax.tree.map(lambda part: lax.all_gather(part, axis), value)]
    pallas_call x0 -> x4, Pallas kernels: none -> 298 us  [the longest x1 143 us: scatter_all(): pl.pallas_call(functools.partial(scatter_kernel, sizes, parts, len(partia...]
    all_gather x3 -> x0, blocking collectives: 106 us -> none  [the longest x1 37.2 us: local(): lax.all_gather(rank_up, 'seq', axis=1, tiled=True)]
    unnamed x22 -> x0, waiting for transfers between devices: 87.7 us -> none
    unnamed x2 -> x0, blocking collectives: 80.1 us -> none
    select_n x62 -> x0, other arithmetic: 77 us -> none  [hop(): jnp.where(position < mine, new, old)]
    dot_general x8 -> x10, matrix products: 58.7 us -> 48.9 us  [left_t(): lax.dot_general(left, right, (((0,), (0,)), ((), ())), preferred_element_...]
  transfers between devices with their start and end apart: 20 -> 0, of which waited for: 16 -> 0; matrix products, arithmetic and copies ran while one was open for 13% -> 0% of each run, Pallas kernels for 0% -> 0%
where the time goes in v1:
time: 875 us; the launch traced here: 868 us
  Pallas kernels  298 us (34%)
  matrix products  285 us (33%)
  local copies, waits for them, and re-layouts  168 us (19%)
  other arithmetic  115 us (13%)
    pallas_call x1, Pallas kernels, scatter_all(): pl.pallas_call(functools.partial(scatter_kernel, sizes, parts, len(partia...  143 us
    pallas_call x1, Pallas kernels, gather_all(): pl.pallas_call(functools.partial(gather_kernel, sizes, parts, len(shards)...  99.3 us
    dot_general x10, matrix products, matmul(): return jnp.dot(left, right, preferred_element_type=jnp.float32)  65.1 us
    dot_general x10, matrix products, right_t(): lax.dot_general(left, right, (((1,), (1,)), ((), ())), preferred_element_...  61.9 us
    pallas_call x2, Pallas kernels, entering(): pl.pallas_call(functools.partial(scan_kernel, sizes, backward), out_shape...  56.4 us
    dot_general x10, matrix products, left_t(): lax.dot_general(left, right, (((0,), (0,)), ((), ())), preferred_element_...  48.9 us
    unnamed x181, local copies, waits for them, and re-layouts  34.9 us
    dynamic_update_slice x64, local copies, waits for them, and re-layouts, mixer_local(): lax.scan(advance, jnp.zeros((HEADS, HK, HV), jnp.float32), (total, updates))  33 us

profile of v1, /device:TPU:8, one launch (start us, length us, event | category | flops | bytes accessed | tf_op | source)
XLA Modules:
  0.0 868.3 jit_solution(9639237638036542705)
XLA Ops:
  5.3 99.3 %shard_map.279 = (bf16[4,2,2,2,16,128]{5,4,3,2,1,0:T(8,128)(2,1)}, bf16[4,2,2,2,32,3072]{5,4,3,2,1,0:T(8,128)(2,1)}, bf16[4,2,2,2,32,1024]{5,4,3,2,1,0:T(8,128)(...) custom-call(bf16[16,128]{1,0:T(8,128)(2,1)} %bitcast.327, ...), custom_call_target="tpu_custom_call" | custom-call | tf_op jit(solution)/shard_map/pallas_call | solution.py:258
  153.7 9.1 %fusion.63 = f32[16,4,128,256]{3,2,1,0:T(8,128)} fusion(f32[16,64,4,128]{3,1,0,2:T(8,128)} %get-tuple-element.458, bf16[16,64,4,256]{3,2,1,0:T(4,128)(2,1)} %reshape.335), kind=kOutput, calls=%fused_computation.121 | convolution fusion | flops 1610612736 | bytes 12582912 | tf_op jit(solution)/shard_map/jvp(njhk,njhv->nhkv)/dot_general | solution.py:731
  167.2 52.2 %while.36 = (s32[]{:T(128)}, f32[4,128,256]{2,1,0:T(8,128)S(1)}, f32[16,4,128,256]{3,2,1,0:T(8,128)}, f32[16,4,128]{2,1,0:T(4,128)}, f32[16,4,128,1]{2,1,3,0:T(4...) while((s32[]{:T(128)}, f32[4,128,256]{2,1,0:T(8,128)S(1)}, ...), condition=%wide.region_3.4_spmd.clone, body=%wide.region_2.3_spmd.clone.sunk | while | flops 524291 | bytes 2639472 | solution.py:739
  219.3 8.9 %fusion.80 = f32[16,4,256,64]{2,3,1,0:T(8,128)} fusion(f32[16,4,128,256]{3,2,1,0:T(8,128)} %get-tuple-element.616, f32[16,64,4,128]{3,1,0,2:T(8,128)S(1)} %get-tuple-element.451), kind=kOutput, calls=%fused_computation.141 | convolution fusion | flops 1610612736 | bytes 14680064 | tf_op jit(solution)/shard_map/jvp(nihk,nhkv->nihv)/dot_general | solution.py:740
  235.9 30.8 %shard_map.280 = f32[4,256,128]{2,1,0:T(8,128)S(1)} custom-call(f32[4,256,128]{2,1,0:T(8,128)S(1)} %bitcast.283, f32[4,8,128]{2,1,0:T(8,128)S(1)} %broadcast_in_dim.83.logs_ref), custom_call_target="tpu_custom_call" | custom-call | tf_op jit(solution)/shard_map/pallas_call | solution.py:659
  266.8 10.2 %multiply_reduce_fusion.4 = (f32[16,64,4]{1,2,0:T(4,128)S(1)}, f32[16,64,4,256]{3,1,2,0:T(8,128)}) fusion(f32[16,64,4,128]{3,1,0,2:T(8,128)} %get-tuple-element.450, f32[4,256,128]{2,1,0:T(8,128)S(1)} %shard_map.280, f32[16,4,256,64]{2,3,1,0:T(8,128)} %fusion.66, f32[16,4,256,64]{2,3,1,0:T(8,128)} %fusion.80), kind=kOutput, calls=%fused_computation.68 | convolution fusion | flops 1614802944 | bytes 15220736 | tf_op jit(solution)/shard_map/jvp(blfs,fsq->blfq)/dot_general | solution.py:753
  277.0 8.3 copy.346
  293.1 8.9 %multiply_convert_fusion.2 = (bf16[1024,1024]{0,1:T(8,128)(2,1)S(1)}, f32[1024,1024]{0,1:T(8,128)}) fusion(f32[1024,1024]{0,1:T(8,128)} %reshape.370, f32[1024]{0:T(1024)S(1)} %reshape.363, f32[1024,4]{0,1:T(4,128)S(1)} %rsqrt.38, bf16[1024,1024]{0,1:T(8,128)(2,1)} %fusion.12, bf16[1024,3072]{1,0:T(8,128)(2,1)} %bitcast.305), kind=kOutput, calls=%fused_computation.65 | convolution fusion | flops 2155872256 | bytes 14700544 | tf_op jit(solution)/shard_map/dot_general | solution.py:682
  309.6 12.4 %fusion.139 = f32[1024,2816]{1,0:T(8,128)} fusion(bf16[1024,1024]{0,1:T(8,128)(2,1)S(1)} %multiply_convert_fusion.1, bf16[1024,2816]{1,0:T(8,128)(2,1)} %bitcast.338), kind=kOutput, calls=%fused_computation.232 | convolution fusion | flops 5905580032 | bytes 19398656 | tf_op jit(solution)/shard_map/dot_general | solution.py:682
  322.1 9.4 %fusion.138 = f32[1024,2816]{1,0:T(8,128)} fusion(bf16[1024,1024]{0,1:T(8,128)(2,1)S(1)} %multiply_convert_fusion.1, bf16[1024,2816]{1,0:T(8,128)(2,1)S(1)} %bitcast.343), kind=kOutput, calls=%fused_computation.231 | convolution fusion | flops 5905580032 | bytes 19398656 | tf_op jit(solution)/shard_map/dot_general | solution.py:682
  331.5 21.5 %fusion.4 = (bf16[1024,2816]{1,0:T(8,128)(2,1)}, bf16[1024,2816]{1,0:T(8,128)(2,1)}, bf16[1024,2816]{1,0:T(8,128)(2,1)}) fusion(f32[1024,2816]{1,0:T(8,128)} %fusion.138, f32[1024,2816]{1,0:T(8,128)} %fusion.139, bf16[2816,1024]{1,0:T(8,128)(2,1)} %bitcast.336, bf16[1024,1024]{1,0:T(8,128)(2,1)} %param.35), kind=kOutput, calls=%fused_computation.18 | convolution fusion | flops 5951717376 | bytes 48234496 | tf_op jit(solution)/shard_map/dot_general | solution.py:692
  352.9 10.0 %fusion.140 = f32[1024,1024]{0,1:T(8,128)S(1)} fusion(bf16[1024,2816]{1,0:T(8,128)(2,1)} %get-tuple-element.438, bf16[1024,2816]{1,0:T(8,128)(2,1)} %bitcast.340), kind=kOutput, calls=%fused_computation.233 | convolution fusion | flops 5905580032 | bytes 15728640 | tf_op jit(solution)/shard_map/dot_general | solution.py:692
  363.0 10.2 %multiply_reduce_fusion = (bf16[1024]{0:T(1024)(128)(2,1)S(1)}, f32[1024]{0:T(1024)S(1)}, f32[1024,1024]{0,1:T(8,128)}) fusion(f32[1024,1024]{0,1:T(8,128)S(1)} %copy-done.30, f32[1024]{0:T(1024)S(1)} %fusion.130, f32[1024]{0:T(1024)S(1)} %reshape.364, f32[1024,1024]{0,1:T(8,128)S(1)} %fusion.140, bf16[1024,2816]{1,0:T(8,128)(2,1)S(1)} %copy-done.72, ...), kind=kOutput, calls=%fused_computation.58 | convolution fusion | flops 5912918016 | bytes 24131584 | tf_op jit(solution)/shard_map/dot_general | solution.py:692
  420.7 9.5 %fusion.78 = f32[16,4,128,256]{3,2,1,0:T(8,128)} fusion(f32[16,4,256,64]{2,3,1,0:T(8,128)S(1)} %get-tuple-element.442, f32[16,64,4,128]{3,1,0,2:T(8,128)S(1)} %get-tuple-element.451), kind=kOutput, calls=%fused_computation.139 | convolution fusion | flops 1610612736 | bytes 14680064 | tf_op jit(solution)/shard_map/transpose(jvp(nihk,nhkv->nihv))/dot_general | solution.py:740
  437.0 25.5 %shard_map.281 = f32[4,256,128]{2,1,0:T(8,128)S(1)} custom-call(f32[4,256,128]{2,1,0:T(8,128)S(1)} %fusion.94.state_ref, f32[4,8,128]{2,1,0:T(8,128)S(1)} %broadcast_in_dim.83.logs_ref), custom_call_target="tpu_custom_call" | custom-call | tf_op jit(solution)/shard_map/pallas_call | solution.py:659
  467.0 60.4 %while.35 = (s32[]{:T(128)}, f32[4,128,256]{2,1,0:T(8,128)S(1)}, f32[16,4,128]{2,0,1:T(8,128)S(1)}, f32[16,4,128,256]{3,2,1,0:T(8,128)}, f32[16,4,128,256]{3,2,1...) while((s32[]{:T(128)}, f32[4,128,256]{2,1,0:T(8,128)S(1)}, ...), condition=%wide.region_12.13_spmd, body=%wide.region_10.12_spmd.sunk | while | flops 524291 | bytes 3164301 | solution.py:739
  553.8 12.1 %fusion.93 = (f32[16,4,128]{2,0,1:T(8,128)S(1)}, f32[16,4,128,64]{2,3,0,1:T(8,128)}) fusion(f32[16,64,4,128]{3,2,1,0:T(4,128)} %reshape.362, f32[16,64,4,128]{3,0,1,2:T(8,128)} %copy-done.13, f32[16,4,128]{2,0,1:T(8,128)S(1)} %copy-done.49, bf16[16,64,4,256]{3,2,1,0:T(4,128)(2,1)} %reshape.335, f32[16,4,128,256]{3,2,1,0:T(8,128)} %get-tuple-element.239), kind=kOutput, calls=%fused_computation.159 | convolution fusion | flops 1612701696 | bytes 16842752 | tf_op jit(solution)/shard_map/transpose(jvp(njhk,njhv->nhkv))/dot_general | solution.py:731
  576.3 10.2 %fusion.8 = f32[16,4,64,128]{3,2,0,1:T(8,128)} fusion(f32[16,4,128,256]{3,2,1,0:T(8,128)S(1)} %bitcast.285, f32[16,4,256,64]{2,3,1,0:T(8,128)S(1)} %copy-done.4), kind=kOutput, calls=%fused_computation.24 | convolution fusion | flops 1610612736 | bytes 14680064 | tf_op jit(solution)/shard_map/transpose(jvp(nihk,nhkv->nihv))/dot_general | solution.py:740
  590.7 9.4 %fusion.133 = (f32[16,4,128]{2,0,1:T(8,128)S(1)}, f32[16,64,4,128]{3,1,0,2:T(8,128)}, bf16[16,64,4,128]{3,1,0,2:T(8,128)(2,1)S(1)}, bf16[16,64,4,128]{3,1,0,2:T(8,128)(2,1)S(1)}, f32[16,64,4,128]{3,1,0,2:T(8,128)}) fusion(f32[16,4,128]{2,0,1:T(8,128)S(1)} %copy-done.56, f32[16,64,4,128]{3,0,1,2:T(8,128)S(1)} %copy-done.14, ...), kind=kOutput, calls=%fused_computation.227 | convolution fusion | flops 1624236032 | bytes 23724032 | tf_op jit(solution)/shard_map/transpose(jvp(blfs,fsq->blfq))/dot_general | solution.py:753
  657.8 10.7 %convolution_convert_fusion.2 = bf16[1024,2816]{1,0:T(8,128)(2,1)} fusion(bf16[1024,1024]{0,1:T(8,128)(2,1)S(1)} %copy-done.41, bf16[1024,2816]{1,0:T(8,128)(2,1)} %get-tuple-element.438), kind=kOutput, calls=%fused_computation.39 | convolution fusion | flops 5908463616 | bytes 13631488 | tf_op jit(solution)/shard_map/dot_general | solution.py:686
  668.5 7.9 convolution_convert_fusion.1
  676.5 8.1 convolution_convert_fusion
  684.6 142.7 %shard_map.282 = (f32[16,128]{1,0:T(8,128)}, f32[32,3072]{1,0:T(8,128)}, f32[32,1024]{1,0:T(8,128)}, f32[32,2816]{1,0:T(8,128)}, f32[32,2816]{1,0:T(8,128)}, /*index=5*/f32[88,1024]{1,0:T(8,128)}) custom-call(bf16[4,2,2,2,16,128]{5,4,3,2,1,0:T(8,128)(2,1)} %bitcast.312, bf16[4,2,2,2,32,3072]{5,4,3,2,1,0:T(8,128)(2,1)} %pad_maximum_fusion.refs_1_, ...), custom_call_target="tpu_custom_call" | custom-call | tf_op jit(solution)/shard_map/pallas_call | solution.py:510
  847.8 11.9 %convolution_add_fusion.1 = f32[1024,1024]{0,1:T(8,128)} fusion(f32[1024,1024]{0,1:T(8,128)} %get-tuple-element.476, bf16[1024,2816]{1,0:T(8,128)(2,1)} %get-tuple-element.439, bf16[2816,1024]{1,0:T(8,128)(2,1)} %bitcast.337), kind=kOutput, calls=%fused_computation.127 | convolution fusion | flops 5906628608 | bytes 19922944 | tf_op jit(solution)/shard_map/dot_general | solution.py:682
  (467 shorter events, 378.7 us)
Async XLA Ops:
  123.3 13.5 %copy-start.55 = (f32[16,4,128]{2,0,1:T(8,128)}, f32[16,4,128]{2,0,1:T(8,128)S(1)}, u32[]{:S(2)}) copy-start(f32[16,4,128]{2,0,1:T(8,128)S(1)} %get-tuple-element.456) | copy-start | bytes 98308
  123.3 112.6 %copy-start.68 = (f32[4,128]{1,0:T(4,128)}, f32[4,128]{1,0:T(4,128)S(1)}, u32[]{:S(2)}) copy-start(f32[4,128]{1,0:T(4,128)S(1)} %get-tuple-element.454) | copy-start | bytes 6148
  266.8 10.2 %copy-start = (f32[4,256,128]{2,1,0:T(8,128)}, f32[4,256,128]{2,1,0:T(8,128)S(1)}, u32[]{:S(2)}) copy-start(f32[4,256,128]{2,1,0:T(8,128)S(1)} %shard_map.280) | copy-start | bytes 1572868
  293.1 8.9 %copy-start.45 = (bf16[4,2,2,2,32,1024]{5,4,3,2,1,0:T(8,128)(2,1)S(1)}, bf16[4,2,2,2,32,1024]{5,4,3,2,1,0:T(8,128)(2,1)}, u32[]{:S(2)}) copy-start(bf16[4,2,2,2,32,1024]{5,4,3,2,1,0:T(8,128)(2,1)} %get-tuple-element.233) | copy-start | bytes 6291460
  306.8 15.2 %slice-start.4 = ((s8[5767168]{0:T(1024)(128)(4,1)}), s8[4194304]{0:T(1024)(128)(4,1)S(1)}, s32[]{:S(2)}) async-start(s8[5767168]{0:T(1024)(128)(4,1)} %bitcast.341), calls=%async_computation.4 | async-start | bytes 8388608
  309.6 12.5 %copy-start.40 = (bf16[1024,1024]{0,1:T(8,128)(2,1)}, bf16[1024,1024]{0,1:T(8,128)(2,1)S(1)}, u32[]{:S(2)}) copy-start(bf16[1024,1024]{0,1:T(8,128)(2,1)S(1)} %multiply_convert_fusion.1) | copy-start | bytes 6291460
  309.6 12.5 %slice-start.5 = ((s8[5767168]{0:T(1024)(128)(4,1)}), s8[1572864]{0:T(1024)(128)(4,1)S(1)}, s32[]{:S(2)}) async-start(s8[5767168]{0:T(1024)(128)(4,1)} %bitcast.341), calls=%async_computation.5 | async-start | bytes 3145728
  352.9 10.0 %copy-start.30 = (f32[1024,1024]{0,1:T(8,128)S(1)}, f32[1024,1024]{0,1:T(8,128)}, u32[]{:S(2)}) copy-start(f32[1024,1024]{0,1:T(8,128)} %get-tuple-element.476) | copy-start | bytes 12582916
  352.9 10.1 %copy-start.72 = (bf16[1024,2816]{1,0:T(8,128)(2,1)S(1)}, bf16[1024,2816]{1,0:T(8,128)(2,1)}, u32[]{:S(2)}) copy-start(bf16[1024,2816]{1,0:T(8,128)(2,1)} %get-tuple-element.437) | copy-start | bytes 17301508
  382.8 9.6 %copy-start.10 = (f32[1024,1024]{0,1:T(8,128)}, f32[1024,1024]{0,1:T(8,128)S(1)}, u32[]{:S(2)}) copy-start(f32[1024,1024]{0,1:T(8,128)S(1)} %fusion.14) | copy-start | bytes 12582916
  420.6 9.5 %copy-start.2 = (f32[16,4,256,64]{2,3,1,0:T(8,128)}, f32[16,4,256,64]{2,3,1,0:T(8,128)S(1)}, u32[]{:S(2)}) copy-start(f32[16,4,256,64]{2,3,1,0:T(8,128)S(1)} %get-tuple-element.442) | copy-start | bytes 12582916
  420.7 9.5 %copy-start.11 = (f32[4,256,16,64]{1,3,0,2:T(8,128)}, f32[4,256,16,64]{1,3,0,2:T(8,128)S(1)}, u32[]{:S(2)}) copy-start(f32[4,256,16,64]{1,3,0,2:T(8,128)S(1)} %get-tuple-element.443) | copy-start | bytes 12582916
  420.7 9.5 %copy-start.27 = (f32[16,64,4,128]{3,1,0,2:T(8,128)S(1)}, f32[16,64,4,128]{3,1,0,2:T(8,128)}, u32[]{:S(2)}) copy-start(f32[16,64,4,128]{3,1,0,2:T(8,128)} %get-tuple-element.450) | copy-start | bytes 6291460
  553.6 22.7 %slice-start = ((s8[8388608]{0:T(1024)(128)(4,1)}), s8[4194304]{0:T(1024)(128)(4,1)S(1)}, s32[]{:S(2)}) async-start(s8[8388608]{0:T(1024)(128)(4,1)} %bitcast.284), calls=%async_computation | async-start | bytes 8388608
  553.7 12.1 %copy-start.4 = (f32[16,4,256,64]{2,3,1,0:T(8,128)S(1)}, f32[16,4,256,64]{2,3,1,0:T(8,128)}, u32[]{:S(2)}) copy-start(f32[16,4,256,64]{2,3,1,0:T(8,128)} %copy-done.2) | copy-start | bytes 12582916
  553.8 22.6 %slice-start.1 = ((s8[8388608]{0:T(1024)(128)(4,1)}), s8[4194304]{0:T(1024)(128)(4,1)S(1)}, s32[]{:S(2)}) async-start(s8[8388608]{0:T(1024)(128)(4,1)} %bitcast.284), calls=%async_computation.1 | async-start | bytes 8388608
  576.3 10.3 %copy-start.21 = (f32[16,64,4,128]{3,1,0,2:T(8,128)S(1)}, f32[16,64,4,128]{3,1,0,2:T(8,128)}, u32[]{:S(2)}) copy-start(f32[16,64,4,128]{3,1,0,2:T(8,128)} %get-tuple-element.457) | copy-start | bytes 6291460
  576.3 10.2 %copy-start.26 = (f32[16,4,64,64]{3,2,1,0:T(8,128)S(1)}, f32[16,4,64,64]{3,2,1,0:T(8,128)}, u32[]{:S(2)}) copy-start(f32[16,4,64,64]{3,2,1,0:T(8,128)} %copy-done.25) | copy-start | bytes 3145732
  576.3 14.4 %copy-start.19 = (f32[16,64,4,128]{3,2,1,0:T(4,128)S(1)}, f32[16,64,4,128]{3,2,1,0:T(4,128)}, u32[]{:S(2)}) copy-start(f32[16,64,4,128]{3,2,1,0:T(4,128)} %mul.382) | copy-start | bytes 6291460
  576.3 14.4 %copy-start.56 = (f32[16,4,128]{2,0,1:T(8,128)S(1)}, f32[16,4,128]{2,0,1:T(8,128)}, u32[]{:S(2)}) copy-start(f32[16,4,128]{2,0,1:T(8,128)} %copy-done.55) | copy-start | bytes 98308
  651.1 17.4 %slice-start.6 = ((s8[5767168]{0:T(1024)(128)(4,1)}), s8[4194304]{0:T(1024)(128)(4,1)S(1)}, s32[]{:S(2)}) async-start(s8[5767168]{0:T(1024)(128)(4,1)} %bitcast.344), calls=%async_computation.6 | async-start | bytes 8388608
  657.8 10.7 %slice-start.7 = ((s8[5767168]{0:T(1024)(128)(4,1)}), s8[1572864]{0:T(1024)(128)(4,1)S(1)}, s32[]{:S(2)}) async-start(s8[5767168]{0:T(1024)(128)(4,1)} %bitcast.344), calls=%async_computation.7 | async-start | bytes 3145728
  657.8 18.7 %slice-start.8 = ((s8[5767168]{0:T(1024)(128)(4,1)}), s8[4194304]{0:T(1024)(128)(4,1)S(1)}, s32[]{:S(2)}) async-start(s8[5767168]{0:T(1024)(128)(4,1)} %bitcast.346), calls=%async_computation.8 | async-start | bytes 8388608
  684.6 151.3 %copy-start.67 = (f32[1024]{0:T(1024)S(1)}, f32[1024]{0:T(1024)}, u32[]{:S(2)}) copy-start(f32[1024]{0:T(1024)} %copy-done.66) | copy-start | bytes 12292
  (59 other events, 258.7 us)

commit v2 on v1

--- a/solution.py
+++ b/solution.py
@@ -10,7 +10,6 @@
 HEADS = 4
 HK = 128
 HV = 256
-GROUP = 64
 
 MESH = pl.DeviceIdType.MESH
 LINE = 0
@@ -655,7 +654,6 @@
 def entering(state, logs, sizes, backward, collective_id):
     half, hops = HEADS // 2, len(partners_of(sizes))
     block, tile = (half, HV, HK), (half, 8, HK)
-    spread = jnp.broadcast_to(logs[:, None, :], (HEADS, 8, HK))
     return pl.pallas_call(
         functools.partial(scan_kernel, sizes, backward),
         out_shape=jax.ShapeDtypeStruct(state.shape, jnp.float32),
@@ -675,85 +673,380 @@
         compiler_params=pltpu.CompilerParams(
             collective_id=collective_id, has_side_effects=True, vmem_limit_bytes=32 << 20
         ),
-    )(state, spread)
-
-
-def matmul(left, right):
-    return jnp.dot(left, right, preferred_element_type=jnp.float32)
-
-
-def left_t(left, right):
-    return lax.dot_general(
-        left, right, (((0,), (0,)), ((), ())), preferred_element_type=jnp.float32
+    )(state, logs)
+
+
+CHUNK = 128
+ROWS = 256
+FTILE = 256
+F32, BF16 = jnp.float32, jnp.bfloat16
+
+
+def nn(left, right):
+    return jnp.dot(left, right, preferred_element_type=F32)
+
+
+def nt(left, right):
+    return lax.dot_general(left, right, (((1,), (1,)), ((), ())), preferred_element_type=F32)
+
+
+def tn(left, right):
+    return lax.dot_general(left, right, (((0,), (0,)), ((), ())), preferred_element_type=F32)
+
+
+def sigmoid(v):
+    return 1.0 / (1.0 + jnp.exp(-v))
+
+
+def causal_mask(size):
+    return lax.broadcasted_iota(jnp.int32, (size, size), 0) >= lax.broadcasted_iota(jnp.int32, (size, size), 1)
+
+
+def triangle(upper):
+    rows = lax.broadcasted_iota(jnp.int32, (CHUNK, CHUNK), 0)
+    columns = lax.broadcasted_iota(jnp.int32, (CHUNK, CHUNK), 1)
+    kept = (columns >= rows) if upper else (columns <= rows)
+    return jnp.where(kept, 1.0, 0.0).astype(BF16)
+
+
+def running(matrix, values):
+    high = values.astype(BF16)
+    low = (values - high.astype(F32)).astype(BF16)
+    return nn(matrix, high) + nn(matrix, low)
+
+
+def inverse_rms(values):
+    return lax.rsqrt(jnp.mean(values * values, axis=-1, keepdims=True) + 1e-06)
+
+
+def heads_of(width):
+    return [slice(h * width, (h + 1) * width) for h in range(HEADS)]
+
+
+def project_kernel(
+    tokens, gain, weights, down, up, bias,
+    normed_ref, query_ref, key_ref, value_ref, gate_ref, mid_ref, logit_ref, within_ref, update_ref, final_ref, logs_ref,
+):
+    @pl.when(pl.program_id(0) == 0)
+    def _():
+        final_ref[...] = jnp.zeros_like(final_ref)
+        logs_ref[...] = jnp.zeros_like(logs_ref)
+
+    inputs = tokens[...].astype(F32)
+    normed = (inputs * inverse_rms(inputs) * gain[...]).astype(BF16)
+    normed_ref[...] = normed
+    keys = HEADS * HK
+    values = HEADS * HV
+    mid = nn(normed, down[...]).astype(BF16)
+    mid_ref[...] = mid
+    logit = nn(mid, up[...]) + bias[...]
+    logit_ref[...] = logit
+    query_ref[...] = nn(normed, weights[:, :keys]).astype(BF16)
+    key_ref[...] = nn(normed, weights[:, keys : 2 * keys]).astype(BF16)
+    value_ref[...] = nn(normed, weights[:, 2 * keys : 2 * keys + values]).astype(BF16)
+    gate_ref[...] = nn(normed, weights[:, 2 * keys + values :]).astype(BF16)
+    decay = (jnp.minimum(logit, 0.0) - jnp.log1p(jnp.exp(-jnp.abs(logit)))) * (1.0 / 16.0)
+    lower = triangle(False)
+    for c in range(ROWS // CHUNK):
+        rows = slice(c * CHUNK, (c + 1) * CHUNK)
+        within = running(lower, decay[rows])
+        within_ref[rows] = within
+        total = within[CHUNK - 1 : CHUNK]
+        ending = (key_ref[rows].astype(F32) * jnp.exp(total - within)).astype(BF16)
+        for h, (ks, vs) in enumerate(zip(heads_of(HK), heads_of(HV))):
+            update = tn(value_ref[rows, vs], ending[:, ks])
+            update_ref[c, h] = update.astype(BF16)
+            final_ref[h] = final_ref[h] * jnp.exp(total[:, ks]) + update
+            logs_ref[h] = logs_ref[h] + total[:, ks]
+
+
+def mix_kernel(
+    tokens, query, key, value, gate, within_all, update, entering_ref, head_gain, out_weight, ffn_gain,
+    mixed_ref, gated_ref, hidden_ref, ffn_ref, starts_ref, state,
+):
+    @pl.when(pl.program_id(0) == 0)
+    def _():
+        state[...] = entering_ref[...]
+
+    mask = causal_mask(CHUNK)
+    for c in range(ROWS // CHUNK):
+        rows = slice(c * CHUNK, (c + 1) * CHUNK)
+        within = within_all[rows]
+        middle = within[CHUNK // 2 - 1 : CHUNK // 2]
+        total = within[CHUNK - 1 : CHUNK]
+        scaled = query[rows].astype(F32) * HK**-0.5
+        from_start = (scaled * jnp.exp(within)).astype(BF16)
+        left = (scaled * jnp.exp(within - middle)).astype(BF16)
+        right = (key[rows].astype(F32) * jnp.exp(middle - within)).astype(BF16)
+        for h, (ks, vs) in enumerate(zip(heads_of(HK), heads_of(HV))):
+            start = state[h].astype(BF16)
+            starts_ref[c, h] = start
+            scores = jnp.where(mask, nt(left[:, ks], right[:, ks]), 0.0).astype(BF16)
+            mixed = nn(scores, value[rows, vs]) + nt(from_start[:, ks], start)
+            state[h] = state[h] * jnp.exp(total[:, ks]) + update[c, h].astype(F32)
+            mixed_ref[rows, vs] = mixed.astype(BF16)
+            gates = gate[rows, vs].astype(F32)
+            gated = mixed * inverse_rms(mixed) * head_gain[:, vs] * (gates * sigmoid(gates))
+            gated_ref[rows, vs] = gated.astype(BF16)
+    hidden = tokens[...].astype(F32) + nn(gated_ref[...], out_weight[...])
+    hidden_ref[...] = hidden
+    ffn_ref[...] = (hidden * inverse_rms(hidden) * ffn_gain[...]).astype(BF16)
+
+
+def ffn_kernel(
+    ffn_in, ffn_in_t, cotangent, hidden, gate_weight, up_weight, down_weight,
+    out_ref, back_ref, gate_grad, up_grad, down_grad,
+):
+    @pl.when(pl.program_id(0) == 0)
+    def _():
+        out_ref[...] = hidden[...]
+        back_ref[...] = jnp.zeros_like(back_ref)
+
+    gate, up = nn(ffn_in[...], gate_weight[...]), nn(ffn_in[...], up_weight[...])
+    back = nt(cotangent[...], down_weight[...])
+    share = sigmoid(gate)
+    passed = gate * share
+    inner = (passed * up).astype(BF16)
+    d_up = (back * passed).astype(BF16)
+    d_gate = (back * up * (share * (1.0 + gate * (1.0 - share)))).astype(BF16)
+    out_ref[...] += nn(inner, down_weight[...])
+    back_ref[...] += nt(d_gate, gate_weight[...]) + nt(d_up, up_weight[...])
+    gate_grad[...] = nn(ffn_in_t[...], d_gate).astype(BF16)
+    up_grad[...] = nn(ffn_in_t[...], d_up).astype(BF16)
+    down_grad[...] = tn(inner, cotangent[...]).astype(BF16)
+
+
+def norm_back(values, gain, grad):
+    scale = inverse_rms(values)
+    inner = grad * gain
+    along = jnp.mean(inner * values, axis=-1, keepdims=True)
+    return scale * inner - values * (scale * scale * scale * along), grad * values * scale
+
+
+def unmix_kernel(
+    ffn_back, hidden, cotangent, gate, mixed, query, within_all, head_gain, out_weight, ffn_gain,
+    d_hidden_ref, low_ref, d_gate_ref, d_mixed_ref, update_ref, enters_ref, ffn_gain_ref, head_gain_ref,
+):
+    @pl.when(pl.program_id(0) == 0)
+    def _():
+        enters_ref[...] = jnp.zeros_like(enters_ref)
+        ffn_gain_ref[...] = jnp.zeros_like(ffn_gain_ref)
+        head_gain_ref[...] = jnp.zeros_like(head_gain_ref)
+
+    through, terms = norm_back(hidden[...], ffn_gain[...], ffn_back[...])
+    ffn_gain_ref[...] += jnp.sum(terms, axis=0, keepdims=True)
+    d_hidden = cotangent[...].astype(F32) + through
+    d_hidden_ref[...] = d_hidden
+    low = d_hidden.astype(BF16)
+    low_ref[...] = low
+    d_gated = nt(low, out_weight[...])
+    for vs in heads_of(HV):
+        value = mixed[:, vs].astype(F32)
+        scale = inverse_rms(value)
+        headed = value * scale
+        gates = gate[:, vs].astype(F32)
+        share = sigmoid(gates)
+        passed = gates * share
+        grad, gain = d_gated[:, vs], head_gain[:, vs]
+        head_gain_ref[:, vs] += jnp.sum(grad * headed * passed, axis=0, keepdims=True)
+        d_gate_ref[:, vs] = (grad * headed * gain * (share * (1.0 + gates * (1.0 - share)))).astype(BF16)
+        d_headed = grad * gain * passed
+        along = jnp.mean(d_headed * headed, axis=-1, keepdims=True)
+        d_mixed_ref[:, vs] = (scale * (d_headed - headed * along)).astype(BF16)
+    for c in reversed(range(ROWS // CHUNK)):
+        rows = slice(c * CHUNK, (c + 1) * CHUNK)
+        within = within_all[rows]
+        total = within[CHUNK - 1 : CHUNK]
+        from_start = (query[rows].astype(F32) * HK**-0.5 * jnp.exp(within)).astype(BF16)
+        for h, (ks, vs) in enumerate(zip(heads_of(HK), heads_of(HV))):
+            update = tn(d_mixed_ref[rows, vs], from_start[:, ks])
+            update_ref[c, h] = update.astype(BF16)
+            enters_ref[h] = enters_ref[h] * jnp.exp(total[:, ks]) + update
+
+
+def back_kernel(
+    tokens, query, key, value, logit, within_all, d_mixed, starts, update, leaving_ref, d_gate, d_hidden,
+    gain, weights, down, up,
+    d_qkv_ref, d_logit_ref, d_mid_ref, tokens_grad_ref, gain_ref, bias_ref, state,
+):
+    @pl.when(pl.program_id(0) == 0)
+    def _():
+        state[...] = leaving_ref[...]
+        gain_ref[...] = jnp.zeros_like(gain_ref)
+        bias_ref[...] = jnp.zeros_like(bias_ref)
+
+    mask = causal_mask(CHUNK)
+    upper = triangle(True)
+    keys = HEADS * HK
+    for c in reversed(range(ROWS // CHUNK)):
+        rows = slice(c * CHUNK, (c + 1) * CHUNK)
+        within = within_all[rows]
+        middle = within[CHUNK // 2 - 1 : CHUNK // 2]
+        total = within[CHUNK - 1 : CHUNK]
+        factor = jnp.exp(total)
+        queries, keys_f = query[rows].astype(F32), key[rows].astype(F32)
+        q_start, q_middle = jnp.exp(within) * HK**-0.5, jnp.exp(within - middle) * HK**-0.5
+        k_middle, k_end = jnp.exp(middle - within), jnp.exp(total - within)
+        left = (queries * q_middle).astype(BF16)
+        right = (keys_f * k_middle).astype(BF16)
+        ending = (keys_f * k_end).astype(BF16)
+        moves, extras = [], []
+        for h, (ks, vs) in enumerate(zip(heads_of(HK), heads_of(HV))):
+            start, after = starts[c, h], state[h].astype(BF16)
+            grad, values = d_mixed[rows, vs], value[rows, vs]
+            scores = jnp.where(mask, nt(left[:, ks], right[:, ks]), 0.0).astype(BF16)
+            d_scores = jnp.where(mask, nt(grad, values), 0.0).astype(BF16)
+            d_value = tn(scores, grad) + nt(ending[:, ks], after)
+            d_query = nn(d_scores, right[:, ks]) * q_middle[:, ks] + nn(grad, start) * q_start[:, ks]
+            d_end = nn(values, after) * k_end[:, ks]
+            d_key = tn(d_scores, left[:, ks]) * k_middle[:, ks] + d_end
+            d_qkv_ref[rows, ks] = d_query.astype(BF16)
+            d_qkv_ref[rows, slice(keys + ks.start, keys + ks.stop)] = d_key.astype(BF16)
+            d_qkv_ref[rows, slice(2 * keys + vs.start, 2 * keys + vs.stop)] = d_value.astype(BF16)
+            moves.append(queries[:, ks] * d_query - keys_f[:, ks] * d_key)
+            extras.append(
+                jnp.sum(keys_f[:, ks] * d_end, axis=0, keepdims=True)
+                + factor[:, ks] * jnp.sum(start.astype(F32) * state[h], axis=0, keepdims=True)
+            )
+            state[h] = state[h] * factor[:, ks] + update[c, h].astype(F32)
+        d_decay = running(upper, jnp.concatenate(moves, axis=1)) + jnp.concatenate(extras, axis=1)
+        d_logit = d_decay * sigmoid(-logit[rows]) * (1.0 / 16.0)
+        bias_ref[...] += jnp.sum(d_logit, axis=0, keepdims=True)
+        d_logit_ref[rows] = d_logit.astype(BF16)
+    d_mid = nt(d_logit_ref[...], up[...]).astype(BF16)
+    d_mid_ref[...] = d_mid
+    inner = 2 * keys + HEADS * HV
+    d_normed = (
+        nt(d_qkv_ref[...], weights[:, :inner]) + nt(d_gate[...], weights[:, inner:]) + nt(d_mid, down[...])
     )
-
-
-def right_t(left, right):
-    return lax.dot_general(
-        left, right, (((1,), (1,)), ((), ())), preferred_element_type=jnp.float32
+    through, terms = norm_back(tokens[...].astype(F32), gain[...], d_normed)
+    gain_ref[...] += jnp.sum(terms, axis=0, keepdims=True)
+    tokens_grad_ref[...] = d_hidden[...] + through
+
+
+def rows_spec(width, steps, backward):
+    return pl.BlockSpec((ROWS, width), (lambda i: (steps - 1 - i, 0)) if backward else (lambda i: (i, 0)))
+
+
+def chunks_spec(steps, backward):
+    return pl.BlockSpec(
+        (ROWS // CHUNK, HEADS, HV, HK),
+        (lambda i: (steps - 1 - i, 0, 0, 0)) if backward else (lambda i: (i, 0, 0, 0)),
     )
 
 
-def rms_norm(values, gain):
-    return values * lax.rsqrt(jnp.mean(values * values, axis=-1, keepdims=True) + 1e-06) * gain
-
-
-def head_norm(mixed, gain, gate):
-    length = mixed.shape[0]
-    shaped = mixed.reshape(length, HEADS, HV)
-    headed = shaped * lax.rsqrt(jnp.mean(shaped * shaped, axis=-1, keepdims=True) + 1e-06)
-    return headed.reshape(length, HEADS * HV) * gain * jax.nn.silu(gate)
-
-
-def swiglu(fgate, fup):
-    return jax.nn.silu(fgate) * fup
-
-
-def mixer_local(query, key, value_rows, decay):
-    length = query.shape[0]
-    blocks = length // GROUP
-    q_blocks = query.reshape(blocks, GROUP, HEADS, HK) * HK ** (-0.5)
-    k_blocks = key.reshape(blocks, GROUP, HEADS, HK)
-    v_blocks = value_rows.reshape(blocks, GROUP, HEADS, HV)
-    within = jnp.cumsum(decay.reshape(blocks, GROUP, HEADS, HK), axis=1)
-    total = within[:, -1]
-    query_with_decay = q_blocks * jnp.exp(within)
-    k_decayed = k_blocks * jnp.exp(-within)
-    key_to_segment_end = k_blocks * jnp.exp(total[:, None] - within)
-    causal = (jnp.arange(GROUP)[:, None] >= jnp.arange(GROUP)[None, :]).astype(jnp.float32)
-    scores = (
-        jnp.einsum("nihk,njhk->nhij", query_with_decay, k_decayed, precision=lax.Precision.HIGHEST)
-        * causal
-    )
-    segment_result = jnp.einsum(
-        "nhij,njhv->nihv", scores, v_blocks, precision=lax.Precision.HIGHEST
-    )
-    updates = jnp.einsum(
-        "njhk,njhv->nhkv", key_to_segment_end, v_blocks, precision=lax.Precision.HIGHEST
-    )
-
-    def advance(state_matrix, pair):
-        factor, state_increment = pair
-        return (jnp.exp(factor)[:, :, None] * state_matrix + state_increment, state_matrix)
-
-    final, starts = lax.scan(advance, jnp.zeros((HEADS, HK, HV), jnp.float32), (total, updates))
-    segment_result = segment_result + jnp.einsum(
-        "nihk,nhkv->nihv", query_with_decay, starts, precision=lax.Precision.HIGHEST
-    )
-    return (segment_result.reshape(length, HEADS * HV), final, jnp.sum(total, axis=0))
-
-
-def mixer_carried(query, decay, incoming_state):
-    length = query.shape[0]
-    blocks = length // GROUP
-    q_blocks = query.reshape(blocks, GROUP, HEADS, HK) * HK ** (-0.5)
-    within = jnp.cumsum(decay.reshape(blocks, GROUP, HEADS, HK), axis=1)
-    before = jnp.cumsum(within[:, -1], axis=0) - within[:, -1]
-    weighted_scores = q_blocks * jnp.exp(within + before[:, None])
-    segment_result = jnp.einsum(
-        "blfs,fsq->blfq", weighted_scores, incoming_state, precision=lax.Precision.HIGHEST
-    )
-    return segment_result.reshape(length, HEADS * HV)
+def kept_spec(shape):
+    return pl.BlockSpec(shape, lambda i: (0,) * len(shape), pipeline_mode=pl.Buffered(1))
+
+
+def kept_out(shape):
+    return pl.BlockSpec(shape, lambda i: (0,) * len(shape))
+
+
+PARAMS = dict(vmem_limit_bytes=60 << 20)
+STATE = (HEADS, HV, HK)
+
+
+def project(tokens, gain, weights, down, up, bias):
+    length, width = tokens.shape
+    steps, keys, values = length // ROWS, HEADS * HK, HEADS * HV
+    row = lambda w: rows_spec(w, steps, False)
+    chunks = (length // CHUNK,) + STATE
+    shape = jax.ShapeDtypeStruct
+    return pl.pallas_call(
+        project_kernel,
+        grid=(steps,),
+        in_specs=[row(width)] + [kept_spec(a.shape) for a in (gain, weights, down, up, bias)],
+        out_specs=[row(w) for w in (width, keys, keys, values, values, down.shape[1], keys, keys)]
+        + [chunks_spec(steps, False), kept_out(STATE), kept_out((HEADS, 8, HK))],
+        out_shape=[shape((length, w), BF16) for w in (width, keys, keys, values, values, down.shape[1])]
+        + [shape((length, keys), F32)] * 2
+        + [shape(chunks, BF16), shape(STATE, F32), shape((HEADS, 8, HK), F32)],
+        compiler_params=pltpu.CompilerParams(**PARAMS),
+    )(tokens, gain, weights, down, up, bias)
+
+
+def mix(tokens, query, key, value, gate, within, update, entered, head_gain, out_weight, ffn_gain):
+    length, width = tokens.shape
+    steps, keys, values = length // ROWS, HEADS * HK, HEADS * HV
+    row = lambda w: rows_spec(w, steps, False)
+    shape = jax.ShapeDtypeStruct
+    return pl.pallas_call(
+        mix_kernel,
+        grid=(steps,),
+        in_specs=[row(w) for w in (width, keys, keys, values, values, keys)]
+        + [chunks_spec(steps, False)]
+        + [kept_spec(a.shape) for a in (entered, head_gain, out_weight, ffn_gain)],
+        out_specs=[row(w) for w in (values, values, width, width)] + [chunks_spec(steps, False)],
+        out_shape=[
+            shape((length, values), BF16), shape((length, values), BF16),
+            shape((length, width), F32), shape((length, width), BF16), shape(update.shape, BF16),
+        ],
+        scratch_shapes=[pltpu.VMEM(STATE, F32)],
+        compiler_params=pltpu.CompilerParams(**PARAMS),
+    )(tokens, query, key, value, gate, within, update, entered, head_gain, out_weight, ffn_gain)
+
+
+def feed_forward(ffn_in, cotangent, hidden, gate_weight, up_weight, down_weight):
+    length, width = ffn_in.shape
+    inner = gate_weight.shape[1]
+    whole = [ffn_in, ffn_in.T, cotangent, hidden]
+    wide = pl.BlockSpec((width, FTILE), lambda i: (0, i))
+    tall = pl.BlockSpec((FTILE, width), lambda i: (i, 0))
+    shape = jax.ShapeDtypeStruct
+    return pl.pallas_call(
+        ffn_kernel,
+        grid=(inner // FTILE,),
+        in_specs=[kept_spec(a.shape) for a in whole] + [wide, wide, tall],
+        out_specs=[kept_out((length, width))] * 2 + [wide, wide, tall],
+        out_shape=[shape((length, width), F32)] * 2
+        + [shape((width, inner), BF16)] * 2 + [shape((inner, width), BF16)],
+        compiler_params=pltpu.CompilerParams(**PARAMS),
+    )(*whole, gate_weight, up_weight, down_weight)
+
+
+def unmix(ffn_back, hidden, cotangent, gate, mixed, query, within, head_gain, out_weight, ffn_gain):
+    length, width = hidden.shape
+    steps, keys, values = length // ROWS, HEADS * HK, HEADS * HV
+    row = lambda w: rows_spec(w, steps, True)
+    chunks = (length // CHUNK,) + STATE
+    shape = jax.ShapeDtypeStruct
+    return pl.pallas_call(
+        unmix_kernel,
+        grid=(steps,),
+        in_specs=[row(w) for w in (width, width, width, values, values, keys, keys)]
+        + [kept_spec(a.shape) for a in (head_gain, out_weight, ffn_gain)],
+        out_specs=[row(w) for w in (width, width, values, values)]
+        + [chunks_spec(steps, True), kept_out(STATE), kept_out((1, width)), kept_out((1, values))],
+        out_shape=[
+            shape((length, width), F32), shape((length, width), BF16), shape((length, values), BF16),
+            shape((length, values), BF16), shape(chunks, BF16), shape(STATE, F32),
+            shape((1, width), F32), shape((1, values), F32),
+        ],
+        compiler_params=pltpu.CompilerParams(**PARAMS),
+    )(ffn_back, hidden, cotangent, gate, mixed, query, within, head_gain, out_weight, ffn_gain)
+
+
+def back(tokens, query, key, value, logit, within, d_mixed, starts, update, leaving, d_gate, d_hidden, gain, weights, down, up):
+    length, width = tokens.shape
+    steps, keys, values = length // ROWS, HEADS * HK, HEADS * HV
+    row = lambda w: rows_spec(w, steps, True)
+    shape = jax.ShapeDtypeStruct
+    inner = 2 * keys + values
+    return pl.pallas_call(
+        back_kernel,
+        grid=(steps,),
+        in_specs=[row(w) for w in (width, keys, keys, values, keys, keys, values)]
+        + [chunks_spec(steps, True)] * 2 + [kept_spec(leaving.shape), row(values), row(width)]
+        + [kept_spec(a.shape) for a in (gain, weights, down, up)],
+        out_specs=[row(w) for w in (inner, keys, down.shape[1], width)] + [kept_out((1, width)), kept_out((1, keys))],
+        out_shape=[
+            shape((length, inner), BF16), shape((length, keys), BF16), shape((length, down.shape[1]), BF16),
+            shape((length, width), F32), shape((1, width), F32), shape((1, keys), F32),
+        ],
+        scratch_shapes=[pltpu.VMEM(STATE, F32)],
+        compiler_params=pltpu.CompilerParams(**PARAMS),
+    )(tokens, query, key, value, logit, within, d_mixed, starts, update, leaving, d_gate, d_hidden, gain, weights, down, up)
 
 
 PARTS = (
@@ -821,109 +1114,57 @@
     full_gain, full_bias, full_head_gain, full_ffn_gain = (pieces[k].reshape(-1) for k in (0, 3, 4, 5))
     full_down_rank = pieces[1].reshape(-1, rank_down.shape[1])
     full_up_rank = pieces[2].transpose(1, 0, 2).reshape(rank_up.shape[0], -1)
-    full_query, full_key = full_proj[:, :512], full_proj[:, 512:1024]
-    full_value, full_gate = full_proj[:, 1024:2048], full_proj[:, 2048:]
-    gain_one = full_gain.astype(jnp.float32)
-    gain_two = full_ffn_gain.astype(jnp.float32)
-    heads_gain = full_head_gain.astype(jnp.float32)
-    inputs = tokens.astype(jnp.float32)
-    normed = rms_norm(inputs, gain_one)
-    normed_low = normed.astype(jnp.bfloat16)
-    query_low = matmul(normed_low, full_query).astype(jnp.bfloat16)
-    key_low = matmul(normed_low, full_key).astype(jnp.bfloat16)
-    value_low = matmul(normed_low, full_value).astype(jnp.bfloat16)
-    rank_mid = matmul(normed_low, full_down_rank).astype(jnp.bfloat16)
-    logit = matmul(rank_mid, full_up_rank) + full_bias.astype(jnp.float32)
-    decay = jax.nn.log_sigmoid(logit) / 16.0
-    gate = matmul(normed_low, full_gate)
-    query_f = query_low.astype(jnp.float32)
-    key_f = key_low.astype(jnp.float32)
-    value_f = value_low.astype(jnp.float32)
-    local_out, local_pull = jax.vjp(mixer_local, query_f, key_f, value_f, decay)
-    mixed_local, final_state, log_total = local_out
-    factor = jnp.exp(log_total)
-    incoming_state = entering(final_state.transpose(0, 2, 1), log_total, sizes, False, 2).transpose(0, 2, 1)
-    carried_out, carried_pull = jax.vjp(mixer_carried, query_f, decay, incoming_state)
-    mixed = mixed_local + carried_out
-    gated, gated_pull = jax.vjp(head_norm, mixed, heads_gain, gate)
-    gated_low = gated.astype(jnp.bfloat16)
-    hidden_state = inputs + matmul(gated_low, full_out)
-    ffn_in, ffn_norm_pull = jax.vjp(rms_norm, hidden_state, gain_two)
-    ffn_low = ffn_in.astype(jnp.bfloat16)
-    fgate = matmul(ffn_low, full_fgate)
-    fup = matmul(ffn_low, full_fup)
-    inner, inner_pull = jax.vjp(swiglu, fgate, fup)
-    inner_low = inner.astype(jnp.bfloat16)
-    block_output = hidden_state + matmul(inner_low, full_fdown)
-    upstream = cotangent.astype(jnp.float32)
-    down_grad = left_t(inner_low, cotangent)
-    inner_grad = right_t(cotangent, full_fdown)
-    fgate_grad, fup_grad = inner_pull(inner_grad)
-    fgate_low = fgate_grad.astype(jnp.bfloat16)
-    fup_low = fup_grad.astype(jnp.bfloat16)
-    fgate_wgrad = left_t(ffn_low, fgate_low)
-    fup_wgrad = left_t(ffn_low, fup_low)
-    ffn_in_grad = right_t(fgate_low, full_fgate) + right_t(fup_low, full_fup)
-    hidden_part, gain_two_grad = ffn_norm_pull(ffn_in_grad)
-    hidden_grad = upstream + hidden_part
-    hidden_low = hidden_grad.astype(jnp.bfloat16)
-    out_wgrad = left_t(gated_low, hidden_low)
-    gated_grad = right_t(hidden_low, full_out)
-    mixed_grad, heads_gain_grad, gate_grad = gated_pull(gated_grad)
-    gate_low = gate_grad.astype(jnp.bfloat16)
-    gate_wgrad = left_t(normed_low, gate_low)
-    query_part, decay_part, entering_grad = carried_pull(mixed_grad)
-    leaving_grad = entering(entering_grad.transpose(0, 2, 1), log_total, sizes, True, 3).transpose(0, 2, 1)
-    log_total_grad = factor * jnp.sum(incoming_state * leaving_grad, axis=-1)
-    query_rest, key_grad, value_grad, decay_rest = local_pull(
-        (mixed_grad, leaving_grad, log_total_grad)
+    gain, heads_gain, ffn_gains, bias = (
+        v.astype(F32).reshape(1, -1) for v in (full_gain, full_head_gain, full_ffn_gain, full_bias)
     )
-    query_low_grad = (query_part + query_rest).astype(jnp.bfloat16)
-    key_low_grad = key_grad.astype(jnp.bfloat16)
-    value_low_grad = value_grad.astype(jnp.bfloat16)
-    logit_grad = (decay_part + decay_rest) * jax.nn.sigmoid(-logit) / 16.0
-    bias_grad = jnp.sum(logit_grad, axis=0)
-    logit_low = logit_grad.astype(jnp.bfloat16)
-    up_rank_grad = left_t(rank_mid, logit_low)
-    mid_low = right_t(logit_low, full_up_rank).astype(jnp.bfloat16)
-    down_rank_grad = left_t(normed_low, mid_low)
-    query_wgrad = left_t(normed_low, query_low_grad)
-    key_wgrad = left_t(normed_low, key_low_grad)
-    value_wgrad = left_t(normed_low, value_low_grad)
-    normed_grad = (
-        right_t(query_low_grad, full_query)
-        + right_t(key_low_grad, full_key)
-        + right_t(value_low_grad, full_value)
-        + right_t(gate_low, full_gate)
-        + right_t(mid_low, full_down_rank)
+    rank = rank_down.shape[1]
+    down = jnp.pad(full_down_rank, ((0, 0), (0, 128 - rank)))
+    up = jnp.pad(full_up_rank, ((0, 128 - rank), (0, 0)))
+    normed, query, key, value, gate, mid, logit, within, update, final, logs = project(
+        tokens, gain, full_proj, down, up, bias
     )
-    input_part, gain_one_grad = jax.vjp(rms_norm, inputs, gain_one)[1](normed_grad)
-    tokens_grad = hidden_grad + input_part
+    incoming = entering(final, logs, sizes, False, 2)
+    mixed, gated, hidden, ffn_in, starts = mix(
+        tokens, query, key, value, gate, within, update, incoming, heads_gain, full_out, ffn_gains
+    )
+    block_output, ffn_back, fgate_wgrad, fup_wgrad, fdown_wgrad = feed_forward(
+        ffn_in, cotangent, hidden, full_fgate, full_fup, full_fdown
+    )
+    d_hidden, hidden_low, d_gate, d_mixed, back_update, enters, ffn_gain_grad, head_gain_grad = unmix(
+        ffn_back, hidden, cotangent, gate, mixed, query, within, heads_gain, full_out, ffn_gains
+    )
+    leaving = entering(enters, logs, sizes, True, 3)
+    d_qkv, d_logit, d_mid, tokens_grad, gain_grad, bias_grad = back(
+        tokens, query, key, value, logit, within, d_mixed, starts, back_update, leaving, d_gate, d_hidden,
+        gain, full_proj, down, up,
+    )
+    proj_wgrad = jnp.concatenate([tn(normed, d_qkv).astype(BF16), tn(normed, d_gate).astype(BF16)], axis=1)
+    out_wgrad = tn(gated, hidden_low).astype(BF16)
+    down_rank_grad = tn(normed, d_mid)[:, :rank]
+    up_rank_grad = tn(mid, d_logit)[:rank]
     tiles = packed(
         [
-            gain_one_grad.reshape(count, -1),
+            gain_grad.reshape(count, -1),
             down_rank_grad.reshape(count, -1),
-            up_rank_grad.reshape(rank_up.shape[0], count, -1).transpose(1, 0, 2),
+            up_rank_grad.reshape(rank, count, -1).transpose(1, 0, 2),
             bias_grad.reshape(count, -1),
-            heads_gain_grad.reshape(count, -1),
-            gain_two_grad.reshape(count, -1),
+            head_gain_grad.reshape(count, -1),
+            ffn_gain_grad.reshape(count, -1),
         ]
-    ).astype(jnp.bfloat16)
-    proj_wgrad = jnp.concatenate([query_wgrad, key_wgrad, value_wgrad, gate_wgrad], axis=1)
+    ).astype(BF16)
     summed = scatter_all(
-        [tiles] + [g.astype(jnp.bfloat16) for g in (proj_wgrad, out_wgrad, fgate_wgrad, fup_wgrad, down_grad)],
-        BACK_PARTS, sizes, 1,
+        [tiles, proj_wgrad, out_wgrad, fgate_wgrad, fup_wgrad, fdown_wgrad], BACK_PARTS, sizes, 1
     )
     gain_sum, down_sum, up_sum, bias_sum, head_sum, ffn_sum = [p[0] for p in unpacked(summed[0], shapes)]
-    proj_sum = summed[1]
+    proj_sum, keys = summed[1], HEADS * HK
     return (
         block_output,
         tokens_grad,
         gain_sum,
-        proj_sum[:, :512],
-        proj_sum[:, 512:1024],
-        proj_sum[:, 1024:2048],
-        proj_sum[:, 2048:],
+        proj_sum[:, :keys],
+        proj_sum[:, keys : 2 * keys],
+        proj_sum[:, 2 * keys : 2 * keys + HEADS * HV],
+        proj_sum[:, 2 * keys + HEADS * HV :],
         down_sum,
         up_sum,
         bias_sum,

time: 875 us -> 498 us (0.57)
  matrix products: 285 us -> 20 us
  local copies, waits for them, and re-layouts: 168 us -> 32.5 us
  Pallas kernels: 298 us -> 433 us
  other arithmetic: 115 us -> 5 us
    dot_general x45 -> x5, matrix products: 285 us -> 20 us  [tn(): lax.dot_general(left, right, (((0,), (0,)), ((), ())), preferred_element_...]
    pallas_call x0 -> x5, Pallas kernels: none -> 134 us  [the longest x1 64.6 us: feed_forward(): pl.pallas_call(ffn_kernel, grid=(inner // FTILE,), in_specs=[kept_spec(a....]
    dynamic_update_slice x64 -> x0, local copies, waits for them, and re-layouts: 33 us -> none  [mixer_local(): lax.scan(advance, jnp.zeros((HEADS, HK, HV), jnp.float32), (total, updates))]
    add x18 -> x0, other arithmetic: 31 us -> none  [the longest x16 19.3 us: advance(): jnp.exp(factor)[:, :, None] * state_matrix + state_increment]
    reshape x10 -> x4, local copies, waits for them, and re-layouts: 29.3 us -> 0.39 us  [the longest x1 0.15 us: local(): up_rank_grad.reshape(rank, count, -1).transpose(1, 0, 2)]
    reduce_sum x21 -> x0, other arithmetic: 26.4 us -> none  [the longest x16 24.1 us: advance(): jnp.exp(factor)[:, :, None] * state_matrix + state_increment]
    unnamed x181 -> x50, local copies, waits for them, and re-layouts: 34.9 us -> 12 us
    add x4 -> x0, local copies, waits for them, and re-layouts: 20.1 us -> none  [the longest x3 18.8 us: local(): mixed = mixed_local + carried_out]
where the time goes in v2:
time: 498 us; the launch traced here: 491 us
  Pallas kernels  433 us (87%)
  local copies, waits for them, and re-layouts  32.5 us (7%)
  matrix products  20 us (4%)
  other arithmetic  5 us (1%)
    pallas_call x1, Pallas kernels, scatter_all(): pl.pallas_call(functools.partial(scatter_kernel, sizes, parts, len(partia...  142 us
    pallas_call x1, Pallas kernels, gather_all(): pl.pallas_call(functools.partial(gather_kernel, sizes, parts, len(shards)...  99.3 us
    pallas_call x1, Pallas kernels, feed_forward(): pl.pallas_call(ffn_kernel, grid=(inner // FTILE,), in_specs=[kept_spec(a....  64.6 us
    pallas_call x2, Pallas kernels, entering(): pl.pallas_call(functools.partial(scan_kernel, sizes, backward), out_shape...  56.7 us
    pallas_call x1, Pallas kernels, back(): pl.pallas_call(back_kernel, grid=(steps,), in_specs=[row(w) for w in (wid...  25.4 us
    dot_general x5, matrix products, tn(): lax.dot_general(left, right, (((0,), (0,)), ((), ())), preferred_element_...  20 us
    pallas_call x1, Pallas kernels, project(): pl.pallas_call(project_kernel, grid=(steps,), in_specs=[row(width)] + [ke...  15.9 us
    pallas_call x1, Pallas kernels, unmix(): pl.pallas_call(unmix_kernel, grid=(steps,), in_specs=[row(w) for w in (wi...  14.9 us

profile of v2, /device:TPU:8, one launch (start us, length us, event | category | flops | bytes accessed | tf_op | source)
XLA Modules:
  0.0 491.5 jit_solution(4717780935718538712)
XLA Ops:
  3.7 1.6 pad_maximum_fusion.1.refs_1_
  5.3 99.3 %shard_map.279 = (bf16[4,2,2,2,16,128]{5,4,3,2,1,0:T(8,128)(2,1)}, bf16[4,2,2,2,32,3072]{5,4,3,2,1,0:T(8,128)(2,1)}, bf16[4,2,2,2,32,1024]{5,4,3,2,1,0:T(8,128)(...) custom-call(bf16[16,128]{1,0:T(8,128)(2,1)} %bitcast.71, ...), custom_call_target="tpu_custom_call" | custom-call | tf_op jit(solution)/shard_map/pallas_call | solution.py:257
  104.6 0.9 copy.49
  110.6 15.9 %shard_map.280 = (bf16[1024,1024]{1,0:T(8,128)(2,1)}, bf16[1024,512]{1,0:T(8,128)(2,1)}, bf16[1024,512]{1,0:T(8,128)(2,1)}, bf16[1024,1024]{1,0:T(8,128)(2,1)}, ...) custom-call(bf16[1024,1024]{1,0:T(8,128)(2,1)} %tokens.5, ...), custom_call_target="tpu_custom_call" | custom-call | tf_op jit(solution)/shard_map/pallas_call | solution.py:956
  126.5 1.0 copy-done.3
  128.2 31.0 %shard_map.281.entering_ref = f32[4,256,128]{2,1,0:T(8,128)S(1)} custom-call(f32[4,256,128]{2,1,0:T(8,128)S(1)} %copy-done.3, f32[4,8,128]{2,1,0:T(8,128)S(1)} %copy-done.4), custom_call_target="tpu_custom_call" | custom-call | tf_op jit(solution)/shard_map/pallas_call | solution.py:657
  160.0 13.2 %shard_map.282 = (bf16[1024,1024]{1,0:T(8,128)(2,1)}, bf16[1024,1024]{1,0:T(8,128)(2,1)}, f32[1024,1024]{1,0:T(8,128)}, bf16[1024,1024]{1,0:T(8,128)(2,1)}, bf16[8,4,256,128]{3,2,1,0:T(8,128)(2,1)}) custom-call(bf16[1024,1024]{1,0:T(8,128)(2,1)} %tokens.5, bf16[1024,512]{1,0:T(8,128)(2,1)} %get-tuple-element.65.query, ...), custom_call_target="tpu_custom_call" | custom-call | tf_op jit(solution)/shard_map/pallas_call | solution.py:974
  173.2 3.9 copy.38
  177.2 64.6 %shard_map.283 = (f32[1024,1024]{1,0:T(8,128)}, f32[1024,1024]{1,0:T(8,128)}, bf16[1024,2816]{1,0:T(8,128)(2,1)}, bf16[1024,2816]{1,0:T(8,128)(2,1)}, bf16[2816,1024]{1,0:T(8,128)(2,1)}) custom-call(bf16[1024,1024]{1,0:T(8,128)(2,1)} %get-tuple-element.74.ffn_in, bf16[1024,1024]{1,0:T(8,128)(2,1)} %bitcast.54, bf16[1024,1024]{1,0:T(8,128)(2,1)} %cotangent.3, ...), custom_call_target="tpu_custom_call" | custom-call | tf_op jit(solution)/shard_map/pallas_call | solution.py:997
  241.8 14.9 %shard_map.284 = (f32[1024,1024]{1,0:T(8,128)}, bf16[1024,1024]{1,0:T(8,128)(2,1)}, bf16[1024,1024]{1,0:T(8,128)(2,1)}, bf16[1024,1024]{1,0:T(8,128)(2,1)}, bf16...) custom-call(f32[1024,1024]{1,0:T(8,128)} %get-tuple-element.81.ffn_back, ...), custom_call_target="tpu_custom_call" | custom-call | tf_op jit(solution)/shard_map/pallas_call | solution.py:1014
  256.8 5.4 %convolution_convert_fusion.1 = bf16[1024,1024]{1,0:T(8,128)(2,1)} fusion(bf16[1024,1024]{1,0:T(8,128)(2,1)S(1)} %copy-done.18, bf16[1024,1024]{1,0:T(8,128)(2,1)} %get-tuple-element.100), kind=kOutput, calls=%fused_computation.2 | convolution fusion | flops 2148532224 | bytes 6291456 | tf_op jit(solution)/shard_map/dot_general | solution.py:694
  262.4 25.7 %shard_map.285.leaving_ref = f32[4,256,128]{2,1,0:T(8,128)S(1)} custom-call(f32[4,256,128]{2,1,0:T(8,128)S(1)} %copy-done.2, f32[4,8,128]{2,1,0:T(8,128)S(1)} %copy-done.5), custom_call_target="tpu_custom_call" | custom-call | tf_op jit(solution)/shard_map/pallas_call | solution.py:657
  289.0 25.4 %shard_map.286 = (bf16[1024,2048]{1,0:T(8,128)(2,1)}, bf16[1024,512]{1,0:T(8,128)(2,1)}, bf16[1024,128]{1,0:T(8,128)(2,1)}, f32[1024,1024]{1,0:T(8,128)}, f32[1,1024]{1,0:T(1,128)}, /*index=5*/f32[1,512]{1,0:T(1,128)}) custom-call(bf16[1024,1024]{1,0:T(8,128)(2,1)} %tokens.5, bf16[1024,512]{1,0:T(8,128)(2,1)} %get-tuple-element.65.query, ...), custom_call_target="tpu_custom_call" | custom-call | tf_op jit(solution)/shard_map/pallas_call | solution.py:1036
  314.5 5.5 %convolution_convert_fusion.2 = bf16[1024,1024]{1,0:T(8,128)(2,1)} fusion(bf16[1024,1024]{1,0:T(8,128)(2,1)} %get-tuple-element.91, bf16[1024,1024]{1,0:T(8,128)(2,1)S(1)} %copy-done.6), kind=kOutput, calls=%fused_computation.3 | convolution fusion | flops 2148532224 | bytes 6291456 | tf_op jit(solution)/shard_map/dot_general | solution.py:694
  320.9 2.2 fusion.2
  323.7 6.6 %convolution_convert_fusion = bf16[1024,2048]{1,0:T(8,128)(2,1)S(1)} fusion(bf16[1024,1024]{1,0:T(8,128)(2,1)} %get-tuple-element.91, bf16[1024,2048]{1,0:T(8,128)(2,1)S(1)} %copy-done.17), kind=kOutput, calls=%fused_computation.1 | convolution fusion | flops 4297064448 | bytes 10485760 | tf_op jit(solution)/shard_map/dot_general | solution.py:694
  330.4 3.2 pad_maximum_fusion
  334.9 142.5 %shard_map.287 = (f32[16,128]{1,0:T(8,128)}, f32[32,3072]{1,0:T(8,128)}, f32[32,1024]{1,0:T(8,128)}, f32[32,2816]{1,0:T(8,128)}, f32[32,2816]{1,0:T(8,128)}, /*index=5*/f32[88,1024]{1,0:T(8,128)}) custom-call(bf16[4,2,2,2,16,128]{5,4,3,2,1,0:T(8,128)(2,1)} %bitcast.62, bf16[4,2,2,2,32,3072]{5,4,3,2,1,0:T(8,128)(2,1)} %bitcast.49, ...), custom_call_target="tpu_custom_call" | custom-call | tf_op jit(solution)/shard_map/pallas_call | solution.py:509
  477.4 1.3 slice_bitcast_fusion.2
  479.5 1.3 slice_bitcast_fusion
  483.0 1.5 fusion.1
  484.6 1.7 fusion
  486.2 1.6 copy.54
  487.8 1.7 copy.55
  (84 shorter events, 17.9 us)
Async XLA Ops:
  126.5 1.0 copy-start.3
  127.5 0.7 copy-start.4
  159.2 0.8 copy-start.1
  241.8 15.0 %copy-start.18 = (bf16[1024,1024]{1,0:T(8,128)(2,1)S(1)}, bf16[1024,1024]{1,0:T(8,128)(2,1)}, u32[]{:S(2)}) copy-start(bf16[1024,1024]{1,0:T(8,128)(2,1)} %get-tuple-element.99) | copy-start | bytes 6291460
  256.8 5.4 %copy-start.13 = (f32[1,1024]{1,0:T(1,128)S(1)}, f32[1,1024]{1,0:T(1,128)}, u32[]{:S(2)}) copy-start(f32[1,1024]{1,0:T(1,128)} %get-tuple-element.97) | copy-start | bytes 12292
  256.8 5.4 %copy-start.14 = (f32[1,1024]{1,0:T(1,128)S(1)}, f32[1,1024]{1,0:T(1,128)}, u32[]{:S(2)}) copy-start(f32[1,1024]{1,0:T(1,128)} %get-tuple-element.96) | copy-start | bytes 12292
  256.8 5.6 %copy-start.2 = (f32[4,256,128]{2,1,0:T(8,128)S(1)}, f32[4,256,128]{2,1,0:T(8,128)}, u32[]{:S(2)}) copy-start(f32[4,256,128]{2,1,0:T(8,128)} %get-tuple-element.86.state_ref) | copy-start | bytes 1572868
  256.8 5.6 %copy-start.5 = (f32[4,8,128]{2,1,0:T(8,128)S(1)}, f32[4,8,128]{2,1,0:T(8,128)}, u32[]{:S(2)}) copy-start(f32[4,8,128]{2,1,0:T(8,128)} %get-tuple-element.72.logs_ref) | copy-start | bytes 49156
  288.2 0.8 copy-start
  289.0 25.4 %copy-start.6 = (bf16[1024,1024]{1,0:T(8,128)(2,1)S(1)}, bf16[1024,1024]{1,0:T(8,128)(2,1)}, u32[]{:S(2)}) copy-start(bf16[1024,1024]{1,0:T(8,128)(2,1)} %get-tuple-element.87.d_gate) | copy-start | bytes 6291460
  314.4 5.5 %copy-start.8 = (bf16[1024,512]{1,0:T(8,128)(2,1)S(1)}, bf16[1024,512]{1,0:T(8,128)(2,1)}, u32[]{:S(2)}) copy-start(bf16[1024,512]{1,0:T(8,128)(2,1)} %get-tuple-element.94) | copy-start | bytes 3145732
  314.4 5.5 %copy-start.11 = (bf16[1024,128]{1,0:T(8,128)(2,1)S(1)}, bf16[1024,128]{1,0:T(8,128)(2,1)}, u32[]{:S(2)}) copy-start(bf16[1024,128]{1,0:T(8,128)(2,1)} %get-tuple-element.93) | copy-start | bytes 786436
  314.4 5.9 %copy-start.16 = (f32[1,512]{1,0:T(1,128)S(1)}, f32[1,512]{1,0:T(1,128)}, u32[]{:S(2)}) copy-start(f32[1,512]{1,0:T(1,128)} %get-tuple-element.95) | copy-start | bytes 6148
  314.4 5.9 %copy-start.15 = (f32[1,1024]{1,0:T(1,128)S(1)}, f32[1,1024]{1,0:T(1,128)}, u32[]{:S(2)}) copy-start(f32[1,1024]{1,0:T(1,128)} %get-tuple-element.90) | copy-start | bytes 12292
  314.5 6.4 %copy-start.19 = (bf16[1024,128]{1,0:T(8,128)(2,1)S(1)}, bf16[1024,128]{1,0:T(8,128)(2,1)}, u32[]{:S(2)}) copy-start(bf16[1024,128]{1,0:T(8,128)(2,1)} %get-tuple-element.92) | copy-start | bytes 786436
  320.9 2.8 copy-start.17
  323.7 6.6 %copy-start.12 = (bf16[1024,128]{0,1:T(8,128)(2,1)}, bf16[1024,128]{0,1:T(8,128)(2,1)S(1)}, u32[]{:S(2)}) copy-start(bf16[1024,128]{0,1:T(8,128)(2,1)S(1)} %fusion.2) | copy-start | bytes 786436
  323.7 6.7 %copy-start.7 = (bf16[1024,1024]{1,0:T(8,128)(2,1)S(1)}, bf16[1024,1024]{1,0:T(8,128)(2,1)}, u32[]{:S(2)}) copy-start(bf16[1024,1024]{1,0:T(8,128)(2,1)} %convolution_convert_fusion.2) | copy-start | bytes 6291460
  330.4 3.2 slice-start
  477.4 12.2 %copy-start.10 = (f32[32,2816]{1,0:T(8,128)S(1)}, f32[32,2816]{1,0:T(8,128)}, u32[]{:S(2)}) copy-start(f32[32,2816]{1,0:T(8,128)} %get-tuple-element.168) | copy-start | bytes 1081348
  477.4 12.9 %copy-start.9 = (f32[88,1024]{1,0:T(8,128)S(1)}, f32[88,1024]{1,0:T(8,128)}, u32[]{:S(2)}) copy-start(f32[88,1024]{1,0:T(8,128)} %get-tuple-element.169) | copy-start | bytes 1081348

commit v3 on v2

--- a/solution.py
+++ b/solution.py
@@ -10,6 +10,7 @@
 HEADS = 4
 HK = 128
 HV = 256
+RANK = 16
 
 MESH = pl.DeviceIdType.MESH
 LINE = 0
@@ -47,9 +48,19 @@
     def can(self, axis, step):
         return self.here[axis] > 0 if step < 0 else self.here[axis] < self.sizes[axis] - 1
 
-    def greet(self):
+    def bit(self, axis, stride):
+        return lax.rem(lax.div(self.here[axis], stride), 2)
+
+    def partner(self, axis, stride):
+        return self.toward(axis, (1 - 2 * self.bit(axis, stride)) * stride)
+
+    def greet(self, hops=()):
         barrier = pltpu.get_barrier_semaphore()
         total = 0
+        for axis, stride in hops:
+            if stride > 1:
+                pl.semaphore_signal(barrier, inc=1, device_id=self.partner(axis, stride), device_id_type=MESH)
+                total = total + 1
         for axis, size in enumerate(self.sizes):
             for step in (-1, 1):
                 if size == 1:
@@ -533,27 +544,22 @@
     return hops
 
 
-def scan_kernel(
-    sizes, backward, state_ref, logs_ref, out_ref,
+def scan_kernel(sizes, backward, *refs):
+    place = Place(sizes)
+    place.greet(partners_of(sizes))
+    scan_states(place, backward, lambda hop: None, *refs)
+
+
+def scan_states(
+    place, backward, between, state_ref, logs_ref, out_ref,
     sib, sib_logs, first, first_logs, pre, pre_logs, total, total_logs, wire, wire_logs, got, got_logs, other, send, recv,
 ):
-    place = Place(sizes)
     core = place.here[CORE]
-    hops = partners_of(sizes)
+    hops = partners_of(place.sizes)
     half = HEADS // 2
     mine, theirs = pl.ds(half * core, half), pl.ds(half * (1 - core), half)
     sibling = place.toward(CORE, 1 - 2 * core)
-
-    def bit(axis, stride):
-        return lax.rem(lax.div(place.here[axis], stride), 2)
-
-    def partner(axis, stride):
-        return place.toward(axis, (1 - 2 * bit(axis, stride)) * stride)
-
-    barrier = pltpu.get_barrier_semaphore()
-    for device in [sibling] + [partner(*hop) for hop in hops]:
-        pl.semaphore_signal(barrier, inc=1, device_id=device, device_id_type=MESH)
-    pl.semaphore_wait(barrier, 1 + len(hops))
+    bit, partner = place.bit, place.partner
 
     def remote(source, target, number, device):
         return pltpu.make_async_remote_copy(
@@ -595,6 +601,7 @@
     pre_logs[...] = jnp.zeros_like(pre_logs)
     pending = list(swap)
     for k, (axis, stride) in enumerate(hops):
+        between(k)
         last = k == len(hops) - 1
         wire[k] = total[...].astype(wire.dtype)
         wire_logs[k] = total_logs[...]
@@ -651,25 +658,29 @@
         copy.wait_send()
 
 
-def entering(state, logs, sizes, backward, collective_id):
+def scan_scratch(sizes):
     half, hops = HEADS // 2, len(partners_of(sizes))
     block, tile = (half, HV, HK), (half, 8, HK)
+    return [
+        pltpu.VMEM(block, jnp.float32), pltpu.VMEM(tile, jnp.float32),
+        pltpu.VMEM(block, jnp.float32), pltpu.VMEM(tile, jnp.float32),
+        pltpu.VMEM(block, jnp.float32), pltpu.VMEM(tile, jnp.float32),
+        pltpu.VMEM(block, jnp.float32), pltpu.VMEM(tile, jnp.float32),
+        pltpu.VMEM((hops,) + block, jnp.bfloat16), pltpu.VMEM((hops,) + tile, jnp.float32),
+        pltpu.VMEM((hops,) + block, jnp.bfloat16), pltpu.VMEM((hops,) + tile, jnp.float32),
+        pltpu.VMEM(block, jnp.float32),
+        pltpu.SemaphoreType.DMA((3 + 2 * hops,)),
+        pltpu.SemaphoreType.DMA((3 + 2 * hops,)),
+    ]
+
+
+def entering(state, logs, sizes, backward, collective_id):
     return pl.pallas_call(
         functools.partial(scan_kernel, sizes, backward),
         out_shape=jax.ShapeDtypeStruct(state.shape, jnp.float32),
         in_specs=[pl.BlockSpec(memory_space=pltpu.VMEM)] * 2,
         out_specs=pl.BlockSpec(memory_space=pltpu.VMEM),
-        scratch_shapes=[
-            pltpu.VMEM(block, jnp.float32), pltpu.VMEM(tile, jnp.float32),
-            pltpu.VMEM(block, jnp.float32), pltpu.VMEM(tile, jnp.float32),
-            pltpu.VMEM(block, jnp.float32), pltpu.VMEM(tile, jnp.float32),
-            pltpu.VMEM(block, jnp.float32), pltpu.VMEM(tile, jnp.float32),
-            pltpu.VMEM((hops,) + block, jnp.bfloat16), pltpu.VMEM((hops,) + tile, jnp.float32),
-            pltpu.VMEM((hops,) + block, jnp.bfloat16), pltpu.VMEM((hops,) + tile, jnp.float32),
-            pltpu.VMEM(block, jnp.float32),
-            pltpu.SemaphoreType.DMA((3 + 2 * hops,)),
-            pltpu.SemaphoreType.DMA((3 + 2 * hops,)),
-        ],
+        scratch_shapes=scan_scratch(sizes),
         compiler_params=pltpu.CompilerParams(
             collective_id=collective_id, has_side_effects=True, vmem_limit_bytes=32 << 20
         ),
@@ -715,6 +726,16 @@
     return nn(matrix, high) + nn(matrix, low)
 
 
+def halves(values):
+    high = values.astype(BF16)
+    return high, (values - high.astype(F32)).astype(BF16)
+
+
+def fine_nt(left, right):
+    (high, low), (other, rest) = left, right
+    return nt(high, other) + (nt(high, rest) + nt(low, other))
+
+
 def inverse_rms(values):
     return lax.rsqrt(jnp.mean(values * values, axis=-1, keepdims=True) + 1e-06)
 
@@ -723,36 +744,40 @@
     return [slice(h * width, (h + 1) * width) for h in range(HEADS)]
 
 
-def project_kernel(
-    tokens, gain, weights, down, up, bias,
-    normed_ref, query_ref, key_ref, value_ref, gate_ref, mid_ref, logit_ref, within_ref, update_ref, final_ref, logs_ref,
-):
-    @pl.when(pl.program_id(0) == 0)
-    def _():
-        final_ref[...] = jnp.zeros_like(final_ref)
-        logs_ref[...] = jnp.zeros_like(logs_ref)
-
+def small_rows(extra):
+    lanes = lax.broadcasted_iota(jnp.int32, (8, extra.shape[1]), 1)
+    rows = lax.broadcasted_iota(jnp.int32, (8, extra.shape[1]), 0)
+    return nt(jnp.where(lanes == rows + RANK, 1.0, 0.0).astype(BF16), extra)
+
+
+def with_one(mid):
+    lanes = lax.broadcasted_iota(jnp.int32, mid.shape, 1)
+    return jnp.where(lanes < RANK, mid, jnp.where(lanes == RANK, 1.0, 0.0)).astype(BF16)
+
+
+def project_rows(tokens, gain, weight, up, outs, final_ref, logs_ref):
+    normed_ref, query_ref, key_ref, value_ref, gate_ref, mid_ref, logit_ref, within_ref, update_ref = outs
     inputs = tokens[...].astype(F32)
-    normed = (inputs * inverse_rms(inputs) * gain[...]).astype(BF16)
+    normed = (inputs * inverse_rms(inputs) * gain).astype(BF16)
     normed_ref[...] = normed
     keys = HEADS * HK
     values = HEADS * HV
-    mid = nn(normed, down[...]).astype(BF16)
+    mid = with_one(nn(normed, weight(2 * keys + 2 * values, 128)))
     mid_ref[...] = mid
-    logit = nn(mid, up[...]) + bias[...]
+    logit = nt(mid, up)
     logit_ref[...] = logit
-    query_ref[...] = nn(normed, weights[:, :keys]).astype(BF16)
-    key_ref[...] = nn(normed, weights[:, keys : 2 * keys]).astype(BF16)
-    value_ref[...] = nn(normed, weights[:, 2 * keys : 2 * keys + values]).astype(BF16)
-    gate_ref[...] = nn(normed, weights[:, 2 * keys + values :]).astype(BF16)
+    query_ref[...] = nn(normed, weight(0, keys)).astype(BF16)
+    key_ref[...] = nn(normed, weight(keys, keys)).astype(BF16)
+    value_ref[...] = nn(normed, weight(2 * keys, values)).astype(BF16)
+    gate_ref[...] = nn(normed, weight(2 * keys + values, values)).astype(BF16)
     decay = (jnp.minimum(logit, 0.0) - jnp.log1p(jnp.exp(-jnp.abs(logit)))) * (1.0 / 16.0)
     lower = triangle(False)
     for c in range(ROWS // CHUNK):
-        rows = slice(c * CHUNK, (c + 1) * CHUNK)
-        within = running(lower, decay[rows])
-        within_ref[rows] = within
+        rows = pl.ds(c * CHUNK, CHUNK)
+        within = running(lower, decay[c * CHUNK : (c + 1) * CHUNK])
+        within_ref[rows, :] = within
         total = within[CHUNK - 1 : CHUNK]
-        ending = (key_ref[rows].astype(F32) * jnp.exp(total - within)).astype(BF16)
+        ending = (key_ref[rows, :].astype(F32) * jnp.exp(total - within)).astype(BF16)
         for h, (ks, vs) in enumerate(zip(heads_of(HK), heads_of(HV))):
             update = tn(value_ref[rows, vs], ending[:, ks])
             update_ref[c, h] = update.astype(BF16)
@@ -760,37 +785,56 @@
             logs_ref[h] = logs_ref[h] + total[:, ks]
 
 
-def mix_kernel(
-    tokens, query, key, value, gate, within_all, update, entering_ref, head_gain, out_weight, ffn_gain,
-    mixed_ref, gated_ref, hidden_ref, ffn_ref, starts_ref, state,
-):
+def project_kernel(tokens, gains, weights, up, *refs):
+    outs, (final_ref, logs_ref) = refs[:9], refs[9:]
+
+    @pl.when(pl.program_id(0) == 0)
+    def _():
+        final_ref[...] = jnp.zeros_like(final_ref)
+        logs_ref[...] = jnp.zeros_like(logs_ref)
+
+    project_rows(
+        tokens, gains[0:1], lambda first, width: weights[:, first : first + width], up[...], outs, final_ref, logs_ref
+    )
+
+
+def mix_rows(tokens, query, key, value, gate, within_all, update, state, head_gain, out_weight, ffn_gain, outs):
+    mixed_ref, gated_ref, hidden_ref, ffn_ref, starts_ref = outs
+    mask = causal_mask(CHUNK)
+    for c in range(ROWS // CHUNK):
+        rows = pl.ds(c * CHUNK, CHUNK)
+        within = within_all[rows, :]
+        middle = within[CHUNK // 2 - 1 : CHUNK // 2]
+        total = within[CHUNK - 1 : CHUNK]
+        scaled = query[rows, :].astype(F32) * HK**-0.5
+        from_start = (scaled * jnp.exp(within)).astype(BF16)
+        left = halves(scaled * jnp.exp(within - middle))
+        right = halves(key[rows, :].astype(F32) * jnp.exp(middle - within))
+        for h, (ks, vs) in enumerate(zip(heads_of(HK), heads_of(HV))):
+            start = state[h].astype(BF16)
+            starts_ref[c, h] = start
+            scores = jnp.where(mask, fine_nt([p[:, ks] for p in left], [p[:, ks] for p in right]), 0.0).astype(BF16)
+            mixed = nn(scores, value[rows, vs]) + nt(from_start[:, ks], start)
+            state[h] = state[h] * jnp.exp(total[:, ks]) + update[c, h].astype(F32)
+            mixed_ref[rows, vs] = mixed
+            gates = gate[rows, vs].astype(F32)
+            gated = mixed * inverse_rms(mixed) * head_gain[:, vs] * (gates * sigmoid(gates))
+            gated_ref[rows, vs] = gated.astype(BF16)
+    hidden = tokens[...].astype(F32) + nn(gated_ref[...], out_weight)
+    hidden_ref[...] = hidden
+    ffn_ref[...] = (hidden * inverse_rms(hidden) * ffn_gain).astype(BF16)
+
+
+def mix_kernel(tokens, query, key, value, gate, within_all, update, entering_ref, gains, out_weight, *refs):
+    outs, state = refs[:5], refs[5]
+
     @pl.when(pl.program_id(0) == 0)
     def _():
         state[...] = entering_ref[...]
 
-    mask = causal_mask(CHUNK)
-    for c in range(ROWS // CHUNK):
-        rows = slice(c * CHUNK, (c + 1) * CHUNK)
-        within = within_all[rows]
-        middle = within[CHUNK // 2 - 1 : CHUNK // 2]
-        total = within[CHUNK - 1 : CHUNK]
-        scaled = query[rows].astype(F32) * HK**-0.5
-        from_start = (scaled * jnp.exp(within)).astype(BF16)
-        left = (scaled * jnp.exp(within - middle)).astype(BF16)
-        right = (key[rows].astype(F32) * jnp.exp(middle - within)).astype(BF16)
-        for h, (ks, vs) in enumerate(zip(heads_of(HK), heads_of(HV))):
-            start = state[h].astype(BF16)
-            starts_ref[c, h] = start
-            scores = jnp.where(mask, nt(left[:, ks], right[:, ks]), 0.0).astype(BF16)
-            mixed = nn(scores, value[rows, vs]) + nt(from_start[:, ks], start)
-            state[h] = state[h] * jnp.exp(total[:, ks]) + update[c, h].astype(F32)
-            mixed_ref[rows, vs] = mixed.astype(BF16)
-            gates = gate[rows, vs].astype(F32)
-            gated = mixed * inverse_rms(mixed) * head_gain[:, vs] * (gates * sigmoid(gates))
-            gated_ref[rows, vs] = gated.astype(BF16)
-    hidden = tokens[...].astype(F32) + nn(gated_ref[...], out_weight[...])
-    hidden_ref[...] = hidden
-    ffn_ref[...] = (hidden * inverse_rms(hidden) * ffn_gain[...]).astype(BF16)
+    mix_rows(
+        tokens, query, key, value, gate, within_all, update, state, gains[1:2], out_weight[...], gains[2:3], outs
+    )
 
 
 def ffn_kernel(
@@ -824,7 +868,7 @@
 
 
 def unmix_kernel(
-    ffn_back, hidden, cotangent, gate, mixed, query, within_all, head_gain, out_weight, ffn_gain,
+    ffn_back, hidden, cotangent, gate, mixed, query, within_all, gains, out_weight,
     d_hidden_ref, low_ref, d_gate_ref, d_mixed_ref, update_ref, enters_ref, ffn_gain_ref, head_gain_ref,
 ):
     @pl.when(pl.program_id(0) == 0)
@@ -833,7 +877,7 @@
         ffn_gain_ref[...] = jnp.zeros_like(ffn_gain_ref)
         head_gain_ref[...] = jnp.zeros_like(head_gain_ref)
 
-    through, terms = norm_back(hidden[...], ffn_gain[...], ffn_back[...])
+    through, terms = norm_back(hidden[...], gains[2:3], ffn_back[...])
     ffn_gain_ref[...] += jnp.sum(terms, axis=0, keepdims=True)
     d_hidden = cotangent[...].astype(F32) + through
     d_hidden_ref[...] = d_hidden
@@ -841,39 +885,38 @@
     low_ref[...] = low
     d_gated = nt(low, out_weight[...])
     for vs in heads_of(HV):
-        value = mixed[:, vs].astype(F32)
+        value = mixed[:, vs]
         scale = inverse_rms(value)
         headed = value * scale
         gates = gate[:, vs].astype(F32)
         share = sigmoid(gates)
         passed = gates * share
-        grad, gain = d_gated[:, vs], head_gain[:, vs]
+        grad, gain = d_gated[:, vs], gains[1:2, vs]
         head_gain_ref[:, vs] += jnp.sum(grad * headed * passed, axis=0, keepdims=True)
         d_gate_ref[:, vs] = (grad * headed * gain * (share * (1.0 + gates * (1.0 - share)))).astype(BF16)
         d_headed = grad * gain * passed
         along = jnp.mean(d_headed * headed, axis=-1, keepdims=True)
-        d_mixed_ref[:, vs] = (scale * (d_headed - headed * along)).astype(BF16)
+        d_mixed_ref[:, vs] = scale * (d_headed - headed * along)
     for c in reversed(range(ROWS // CHUNK)):
         rows = slice(c * CHUNK, (c + 1) * CHUNK)
         within = within_all[rows]
         total = within[CHUNK - 1 : CHUNK]
         from_start = (query[rows].astype(F32) * HK**-0.5 * jnp.exp(within)).astype(BF16)
         for h, (ks, vs) in enumerate(zip(heads_of(HK), heads_of(HV))):
-            update = tn(d_mixed_ref[rows, vs], from_start[:, ks])
+            update = tn(d_mixed_ref[rows, vs].astype(BF16), from_start[:, ks])
             update_ref[c, h] = update.astype(BF16)
             enters_ref[h] = enters_ref[h] * jnp.exp(total[:, ks]) + update
 
 
 def back_kernel(
     tokens, query, key, value, logit, within_all, d_mixed, starts, update, leaving_ref, d_gate, d_hidden,
-    gain, weights, down, up,
-    d_qkv_ref, d_logit_ref, d_mid_ref, tokens_grad_ref, gain_ref, bias_ref, state,
+    gains, weights, up,
+    d_qkv_ref, d_logit_ref, d_mid_ref, tokens_grad_ref, gain_ref, state,
 ):
     @pl.when(pl.program_id(0) == 0)
     def _():
         state[...] = leaving_ref[...]
         gain_ref[...] = jnp.zeros_like(gain_ref)
-        bias_ref[...] = jnp.zeros_like(bias_ref)
 
     mask = causal_mask(CHUNK)
     upper = triangle(True)
@@ -887,15 +930,15 @@
         queries, keys_f = query[rows].astype(F32), key[rows].astype(F32)
         q_start, q_middle = jnp.exp(within) * HK**-0.5, jnp.exp(within - middle) * HK**-0.5
         k_middle, k_end = jnp.exp(middle - within), jnp.exp(total - within)
-        left = (queries * q_middle).astype(BF16)
-        right = (keys_f * k_middle).astype(BF16)
+        lefts, rights = halves(queries * q_middle), halves(keys_f * k_middle)
+        left, right = lefts[0], rights[0]
         ending = (keys_f * k_end).astype(BF16)
         moves, extras = [], []
         for h, (ks, vs) in enumerate(zip(heads_of(HK), heads_of(HV))):
             start, after = starts[c, h], state[h].astype(BF16)
-            grad, values = d_mixed[rows, vs], value[rows, vs]
-            scores = jnp.where(mask, nt(left[:, ks], right[:, ks]), 0.0).astype(BF16)
-            d_scores = jnp.where(mask, nt(grad, values), 0.0).astype(BF16)
+            (grad, rest), values = halves(d_mixed[rows, vs]), value[rows, vs]
+            scores = jnp.where(mask, fine_nt([p[:, ks] for p in lefts], [p[:, ks] for p in rights]), 0.0).astype(BF16)
+            d_scores = jnp.where(mask, nt(grad, values) + nt(rest, values), 0.0).astype(BF16)
             d_value = tn(scores, grad) + nt(ending[:, ks], after)
             d_query = nn(d_scores, right[:, ks]) * q_middle[:, ks] + nn(grad, start) * q_start[:, ks]
             d_end = nn(values, after) * k_end[:, ks]
@@ -911,15 +954,16 @@
             state[h] = state[h] * factor[:, ks] + update[c, h].astype(F32)
         d_decay = running(upper, jnp.concatenate(moves, axis=1)) + jnp.concatenate(extras, axis=1)
         d_logit = d_decay * sigmoid(-logit[rows]) * (1.0 / 16.0)
-        bias_ref[...] += jnp.sum(d_logit, axis=0, keepdims=True)
         d_logit_ref[rows] = d_logit.astype(BF16)
-    d_mid = nt(d_logit_ref[...], up[...]).astype(BF16)
+    d_mid = nn(d_logit_ref[...], up[...])
+    d_mid = jnp.where(lax.broadcasted_iota(jnp.int32, d_mid.shape, 1) < RANK, d_mid, 0.0).astype(BF16)
     d_mid_ref[...] = d_mid
     inner = 2 * keys + HEADS * HV
+    outer = inner + HEADS * HV
     d_normed = (
-        nt(d_qkv_ref[...], weights[:, :inner]) + nt(d_gate[...], weights[:, inner:]) + nt(d_mid, down[...])
+        nt(d_qkv_ref[...], weights[:, :inner]) + nt(d_gate[...], weights[:, inner:outer]) + nt(d_mid, weights[:, outer:])
     )
-    through, terms = norm_back(tokens[...].astype(F32), gain[...], d_normed)
+    through, terms = norm_back(tokens[...].astype(F32), gains[0:1], d_normed)
     gain_ref[...] += jnp.sum(terms, axis=0, keepdims=True)
     tokens_grad_ref[...] = d_hidden[...] + through
 
@@ -947,7 +991,7 @@
 STATE = (HEADS, HV, HK)
 
 
-def project(tokens, gain, weights, down, up, bias):
+def project(tokens, gains, weights, up):
     length, width = tokens.shape
     steps, keys, values = length // ROWS, HEADS * HK, HEADS * HV
     row = lambda w: rows_spec(w, steps, False)
@@ -956,17 +1000,17 @@
     return pl.pallas_call(
         project_kernel,
         grid=(steps,),
-        in_specs=[row(width)] + [kept_spec(a.shape) for a in (gain, weights, down, up, bias)],
-        out_specs=[row(w) for w in (width, keys, keys, values, values, down.shape[1], keys, keys)]
+        in_specs=[row(width)] + [kept_spec(a.shape) for a in (gains, weights, up)],
+        out_specs=[row(w) for w in (width, keys, keys, values, values, 128, keys, keys)]
         + [chunks_spec(steps, False), kept_out(STATE), kept_out((HEADS, 8, HK))],
-        out_shape=[shape((length, w), BF16) for w in (width, keys, keys, values, values, down.shape[1])]
+        out_shape=[shape((length, w), BF16) for w in (width, keys, keys, values, values, 128)]
         + [shape((length, keys), F32)] * 2
         + [shape(chunks, BF16), shape(STATE, F32), shape((HEADS, 8, HK), F32)],
         compiler_params=pltpu.CompilerParams(**PARAMS),
-    )(tokens, gain, weights, down, up, bias)
-
-
-def mix(tokens, query, key, value, gate, within, update, entered, head_gain, out_weight, ffn_gain):
+    )(tokens, gains, weights, up)
+
+
+def mix(tokens, query, key, value, gate, within, update, entered, gains, out_weight):
     length, width = tokens.shape
     steps, keys, values = length // ROWS, HEADS * HK, HEADS * HV
     row = lambda w: rows_spec(w, steps, False)
@@ -976,15 +1020,163 @@
         grid=(steps,),
         in_specs=[row(w) for w in (width, keys, keys, values, values, keys)]
         + [chunks_spec(steps, False)]
-        + [kept_spec(a.shape) for a in (entered, head_gain, out_weight, ffn_gain)],
+        + [kept_spec(a.shape) for a in (entered, gains, out_weight)],
         out_specs=[row(w) for w in (values, values, width, width)] + [chunks_spec(steps, False)],
         out_shape=[
-            shape((length, values), BF16), shape((length, values), BF16),
+            shape((length, values), F32), shape((length, values), BF16),
             shape((length, width), F32), shape((length, width), BF16), shape(update.shape, BF16),
         ],
         scratch_shapes=[pltpu.VMEM(STATE, F32)],
         compiler_params=pltpu.CompilerParams(**PARAMS),
-    )(tokens, query, key, value, gate, within, update, entered, head_gain, out_weight, ffn_gain)
+    )(tokens, query, key, value, gate, within, update, entered, gains, out_weight)
+
+
+FRONT_PARTS = (
+    (0, (0, 128), ORDERS[0]),
+    (1, (0, 1024), ORDERS[0]),
+    (1, (1024, 1024), ORDERS[1]),
+    (1, (2048, 1152), ORDERS[2]),
+    (2, (0, 1024), ORDERS[3]),
+    (3, (0, 2816), ORDERS[0]),
+    (4, (0, 2816), ORDERS[1]),
+    (5, (0, 512), ORDERS[2]),
+    (5, (512, 512), ORDERS[3]),
+)
+FIRST_PARTS = 5
+FRONT_TURNS = (1, 2, (2,), 1)
+
+
+def front_kernel(sizes, steps, *refs):
+    tokens, shards, refs = refs[0], refs[1:7], refs[7:]
+    buffers, refs = refs[:6], refs[6:]
+    outs, mixed_outs, (logs_out, gains_out), refs = refs[:8], refs[8:13], refs[13:15], refs[15:]
+    up_all, proj_all, out_all, query, key, value, gate, within, update, state, final, logs, gains, refs = *refs[:13], refs[13:]
+    send, recv, own, flush = refs[:4]
+    scan = refs[4:]
+    place = Place(sizes)
+    step = pl.program_id(0)
+    here = tuple(place.here)
+    held = (up_all, proj_all, out_all) + tuple(buffers[3:])
+    gathers = [
+        Gather(place, k, order, held[which], columns, send, recv)
+        for k, (which, columns, order) in enumerate(FRONT_PARTS)
+    ]
+    owned = [pltpu.make_async_copy(shards[k], buffers[k].at[here], own.at[k]) for k in (3, 4, 5)]
+    flushes = [pltpu.make_async_copy(held[k], buffers[k], flush.at[k]) for k in range(3)]
+    later = [g.steps() for g in gathers[FIRST_PARTS:]]
+
+    def turn():
+        for g in later:
+            next(g, None)
+
+    def during(hop):
+        if hop in FRONT_TURNS[2]:
+            turn()
+
+    @pl.when(step == 0)
+    def _():
+        for copy in owned:
+            copy.start()
+        for k in range(3):
+            held[k][here] = shards[k][...]
+        place.greet(partners_of(sizes))
+        for copy in owned:
+            copy.wait()
+        run_all([g.steps() for g in gathers[:FIRST_PARTS]])
+        turn()
+        flushes[0].start()
+        flushes[1].start()
+        flushes[2].start()
+        extra = 2 * HEADS * (HK + HV)
+        gains[...] = small_rows(proj_all[..., pl.ds(extra, 128)].reshape(-1, 128))
+        gains_out[...] = gains[...]
+        final[...] = jnp.zeros_like(final)
+        logs[...] = jnp.zeros_like(logs)
+        for _ in range(FRONT_TURNS[0]):
+            turn()
+
+    @pl.when(step < steps)
+    def _():
+        rows = pl.ds(pl.multiple_of(step * ROWS, ROWS), ROWS)
+        chunks = pl.ds(step * (ROWS // CHUNK), ROWS // CHUNK)
+        normed_ref, query_ref, key_ref, value_ref, gate_ref, mid_ref, logit_ref, within_ref = outs
+        kept = (query, key, value, gate, within)
+        tiles = (query_ref, key_ref, value_ref, gate_ref, within_ref)
+        project_rows(
+            tokens, gains[0:1],
+            lambda first, width: proj_all[..., pl.ds(first, width)].reshape(-1, width),
+            up_all[...].reshape(-1, 128),
+            (normed_ref, query_ref, key_ref, value_ref, gate_ref, mid_ref, logit_ref, within_ref, update.at[chunks]),
+            final, logs,
+        )
+        for whole, tile in zip(kept, tiles):
+            whole[rows, :] = tile[...]
+
+    @pl.when(step == steps)
+    def _():
+        for _ in range(FRONT_TURNS[1]):
+            turn()
+        logs_out[...] = logs[...]
+        scan_states(place, False, during, final, logs, state, *scan)
+        for _ in range(FRONT_TURNS[3]):
+            turn()
+
+    @pl.when(step >= steps)
+    def _():
+        at = step - steps
+        rows = pl.ds(pl.multiple_of(at * ROWS, ROWS), ROWS)
+        chunks = pl.ds(at * (ROWS // CHUNK), ROWS // CHUNK)
+        mix_rows(
+            tokens, query.at[rows], key.at[rows], value.at[rows], gate.at[rows], within.at[rows], update.at[chunks], state,
+            gains[1:2], out_all[...].reshape(-1, out_all.shape[-1]), gains[2:3], mixed_outs,
+        )
+
+    @pl.when(step == 2 * steps - 1)
+    def _():
+        run_all(later)
+        for g in gathers:
+            g.drain()
+        for copy in flushes:
+            copy.wait()
+
+
+def front(tokens, shards, sizes, collective_id):
+    length, width = tokens.shape
+    steps, keys, values = length // ROWS, HEADS * HK, HEADS * HV
+    shape, chunks = jax.ShapeDtypeStruct, (length // CHUNK,) + STATE
+    first = lambda w: pl.BlockSpec((ROWS, w), lambda i: (jnp.minimum(i, steps - 1), 0))
+    second = lambda w: pl.BlockSpec((ROWS, w), lambda i: (jnp.maximum(i - steps, 0), 0))
+    lanes = lanes_of(sizes)
+    parts = len(FRONT_PARTS)
+    one = lambda w, t: ((length, w), t)
+    results = [one(width, BF16), one(keys, BF16), one(keys, BF16), one(values, BF16), one(values, BF16), one(128, BF16), one(keys, F32), one(keys, F32)]
+    mixes = [one(values, F32), one(values, BF16), one(width, F32), one(width, BF16)]
+    out = pl.pallas_call(
+        functools.partial(front_kernel, sizes, steps),
+        grid=(2 * steps,),
+        in_specs=[pl.BlockSpec((ROWS, width), lambda i: (lax.rem(i, steps), 0))] + [kept_spec(s.shape) for s in shards],
+        out_specs=[pl.BlockSpec(memory_space=pl.ANY)] * len(shards)
+        + [first(s[1]) for s, _ in results]
+        + [second(s[1]) for s, _ in mixes]
+        + [pl.BlockSpec((ROWS // CHUNK,) + STATE, lambda i: (jnp.maximum(i - steps, 0), 0, 0, 0))]
+        + [kept_out((HEADS, 8, HK)), kept_out((8, width))],
+        out_shape=[shape(sizes + s.shape, s.dtype) for s in shards]
+        + [shape(s, t) for s, t in results + mixes]
+        + [shape(chunks, BF16), shape((HEADS, 8, HK), F32), shape((8, width), F32)],
+        scratch_shapes=[pltpu.VMEM(sizes + s.shape, s.dtype) for s in shards[:3]]
+        + [pltpu.VMEM((length, w), t) for w, t in ((keys, BF16), (keys, BF16), (values, BF16), (values, BF16), (keys, F32))]
+        + [pltpu.VMEM(chunks, BF16), pltpu.VMEM(STATE, F32), pltpu.VMEM(STATE, F32), pltpu.VMEM((HEADS, 8, HK), F32), pltpu.VMEM((8, width), F32)]
+        + [
+            pltpu.SemaphoreType.DMA((parts, 4, sizes[0], lanes, 2)),
+            pltpu.SemaphoreType.DMA((parts, 4, sizes[0], lanes)),
+            pltpu.SemaphoreType.DMA((len(shards),)),
+            pltpu.SemaphoreType.DMA((3,)),
+        ]
+        + scan_scratch(sizes),
+        compiler_params=pltpu.CompilerParams(collective_id=collective_id, has_side_effects=True, **PARAMS),
+    )(tokens, *shards)
+    weights = [o.reshape(-1, o.shape[-1]) for o in out[: len(shards)]]
+    return weights, out[len(shards) :]
 
 
 def feed_forward(ffn_in, cotangent, hidden, gate_weight, up_weight, down_weight):
@@ -1005,7 +1197,7 @@
     )(*whole, gate_weight, up_weight, down_weight)
 
 
-def unmix(ffn_back, hidden, cotangent, gate, mixed, query, within, head_gain, out_weight, ffn_gain):
+def unmix(ffn_back, hidden, cotangent, gate, mixed, query, within, gains, out_weight):
     length, width = hidden.shape
     steps, keys, values = length // ROWS, HEADS * HK, HEADS * HV
     row = lambda w: rows_spec(w, steps, True)
@@ -1015,19 +1207,19 @@
         unmix_kernel,
         grid=(steps,),
         in_specs=[row(w) for w in (width, width, width, values, values, keys, keys)]
-        + [kept_spec(a.shape) for a in (head_gain, out_weight, ffn_gain)],
+        + [kept_spec(a.shape) for a in (gains, out_weight)],
         out_specs=[row(w) for w in (width, width, values, values)]
         + [chunks_spec(steps, True), kept_out(STATE), kept_out((1, width)), kept_out((1, values))],
         out_shape=[
             shape((length, width), F32), shape((length, width), BF16), shape((length, values), BF16),
-            shape((length, values), BF16), shape(chunks, BF16), shape(STATE, F32),
+            shape((length, values), F32), shape(chunks, BF16), shape(STATE, F32),
             shape((1, width), F32), shape((1, values), F32),
         ],
         compiler_params=pltpu.CompilerParams(**PARAMS),
-    )(ffn_back, hidden, cotangent, gate, mixed, query, within, head_gain, out_weight, ffn_gain)
-
-
-def back(tokens, query, key, value, logit, within, d_mixed, starts, update, leaving, d_gate, d_hidden, gain, weights, down, up):
+    )(ffn_back, hidden, cotangent, gate, mixed, query, within, gains, out_weight)
+
+
+def back(tokens, query, key, value, logit, within, d_mixed, starts, update, leaving, d_gate, d_hidden, gains, weights, up):
     length, width = tokens.shape
     steps, keys, values = length // ROWS, HEADS * HK, HEADS * HV
     row = lambda w: rows_spec(w, steps, True)
@@ -1038,50 +1230,23 @@
         grid=(steps,),
         in_specs=[row(w) for w in (width, keys, keys, values, keys, keys, values)]
         + [chunks_spec(steps, True)] * 2 + [kept_spec(leaving.shape), row(values), row(width)]
-        + [kept_spec(a.shape) for a in (gain, weights, down, up)],
-        out_specs=[row(w) for w in (inner, keys, down.shape[1], width)] + [kept_out((1, width)), kept_out((1, keys))],
+        + [kept_spec(a.shape) for a in (gains, weights, up)],
+        out_specs=[row(w) for w in (inner, keys, 128, width)] + [kept_out((1, width))],
         out_shape=[
-            shape((length, inner), BF16), shape((length, keys), BF16), shape((length, down.shape[1]), BF16),
-            shape((length, width), F32), shape((1, width), F32), shape((1, keys), F32),
+            shape((length, inner), BF16), shape((length, keys), BF16), shape((length, 128), BF16),
+            shape((length, width), F32), shape((1, width), F32),
         ],
         scratch_shapes=[pltpu.VMEM(STATE, F32)],
         compiler_params=pltpu.CompilerParams(**PARAMS),
-    )(tokens, query, key, value, logit, within, d_mixed, starts, update, leaving, d_gate, d_hidden, gain, weights, down, up)
-
-
-PARTS = (
-    (0, (0, 128), ORDERS[0]),
-    (1, (0, 1024), ORDERS[0]),
-    (1, (1024, 1024), ORDERS[1]),
-    (1, (2048, 1024), ORDERS[2]),
-    (2, (0, 1024), ORDERS[3]),
-    (3, (0, 2816), ORDERS[0]),
-    (4, (0, 2816), ORDERS[1]),
-    (5, (0, 512), ORDERS[2]),
-    (5, (512, 512), ORDERS[3]),
-)
-BACK_PARTS = tuple((which, columns, order[::-1]) for which, columns, order in PARTS)
-TILE = (16, 128)
-
-
-def packed(pieces):
-    count = pieces[0].shape[0]
-    flat = jnp.concatenate([p.reshape(count, -1) for p in pieces], axis=1)
-    flat = jnp.pad(flat, ((0, 0), (0, TILE[0] * TILE[1] - flat.shape[1])))
-    return flat.reshape(count * TILE[0], TILE[1])
-
-
-def unpacked(tiles, shapes):
-    count = tiles.shape[0] // TILE[0]
-    flat = tiles.reshape(count, TILE[0] * TILE[1])
-    out, at = [], 0
-    for shape in shapes:
-        size = 1
-        for extent in shape:
-            size *= extent
-        out.append(flat[:, at : at + size].reshape((count,) + shape))
-        at += size
-    return out
+    )(tokens, query, key, value, logit, within, d_mixed, starts, update, leaving, d_gate, d_hidden, gains, weights, up)
+
+
+BACK_PARTS = tuple((which, columns, order[::-1]) for which, columns, order in FRONT_PARTS)
+
+
+def beside(pieces):
+    rows, used = pieces[0].shape[0], sum(p.shape[1] for p in pieces)
+    return jnp.concatenate(pieces + [jnp.zeros((rows, 128 - used), pieces[0].dtype)], axis=1)
 
 
 def local(
@@ -1102,78 +1267,63 @@
     ffn_down,
     cotangent,
 ):
-    count = lax.axis_size("seq")
-    sizes = grid_of(count)
-    small = (norm_gain, rank_down, rank_up, gate_bias, head_gain, ffn_gain)
-    shapes = [s.shape for s in small]
-    projections = jnp.concatenate([query_weight, key_weight, value_weight, gate_weight], axis=1)
-    tiles, full_proj, full_out, full_fgate, full_fup, full_fdown = gather_all(
-        [packed([s[None] for s in small]), projections, out_weight, ffn_gate, ffn_up, ffn_down], PARTS, sizes, 0
-    )
-    pieces = unpacked(tiles, shapes)
-    full_gain, full_bias, full_head_gain, full_ffn_gain = (pieces[k].reshape(-1) for k in (0, 3, 4, 5))
-    full_down_rank = pieces[1].reshape(-1, rank_down.shape[1])
-    full_up_rank = pieces[2].transpose(1, 0, 2).reshape(rank_up.shape[0], -1)
-    gain, heads_gain, ffn_gains, bias = (
-        v.astype(F32).reshape(1, -1) for v in (full_gain, full_head_gain, full_ffn_gain, full_bias)
-    )
-    rank = rank_down.shape[1]
-    down = jnp.pad(full_down_rank, ((0, 0), (0, 128 - rank)))
-    up = jnp.pad(full_up_rank, ((0, 128 - rank), (0, 0)))
-    normed, query, key, value, gate, mid, logit, within, update, final, logs = project(
-        tokens, gain, full_proj, down, up, bias
-    )
-    incoming = entering(final, logs, sizes, False, 2)
-    mixed, gated, hidden, ffn_in, starts = mix(
-        tokens, query, key, value, gate, within, update, incoming, heads_gain, full_out, ffn_gains
-    )
+    sizes = grid_of(lax.axis_size("seq"))
+    extra = beside([rank_down] + [g[:, None] for g in (norm_gain, head_gain, ffn_gain)])
+    projections = jnp.concatenate([query_weight, key_weight, value_weight, gate_weight, extra], axis=1)
+    shards = [beside([rank_up.T, gate_bias[:, None]]), projections, out_weight, ffn_gate, ffn_up, ffn_down]
+    if rank_up.shape[1] % 16 == 0:
+        weights, kept = front(tokens, shards, sizes, 0)
+        up, proj, out, full_fgate, full_fup, full_fdown = weights
+        normed, query, key, value, gate, mid, logit, within, mixed, gated, hidden, ffn_in, starts, logs, gains = kept
+    else:
+        up, proj, out, full_fgate, full_fup, full_fdown = gather_all(shards, FRONT_PARTS, sizes, 0)
+        gains = jnp.pad(proj[:, -128 + RANK : -128 + RANK + 3].astype(F32).T, ((0, 5), (0, 0)))
+        normed, query, key, value, gate, mid, logit, within, update, final, logs = project(tokens, gains, proj, up)
+        incoming = entering(final, logs, sizes, False, 2)
+        mixed, gated, hidden, ffn_in, starts = mix(
+            tokens, query, key, value, gate, within, update, incoming, gains, out
+        )
     block_output, ffn_back, fgate_wgrad, fup_wgrad, fdown_wgrad = feed_forward(
         ffn_in, cotangent, hidden, full_fgate, full_fup, full_fdown
     )
     d_hidden, hidden_low, d_gate, d_mixed, back_update, enters, ffn_gain_grad, head_gain_grad = unmix(
-        ffn_back, hidden, cotangent, gate, mixed, query, within, heads_gain, full_out, ffn_gains
+        ffn_back, hidden, cotangent, gate, mixed, query, within, gains, out
     )
     leaving = entering(enters, logs, sizes, True, 3)
-    d_qkv, d_logit, d_mid, tokens_grad, gain_grad, bias_grad = back(
+    d_qkv, d_logit, d_mid, tokens_grad, gain_grad = back(
         tokens, query, key, value, logit, within, d_mixed, starts, back_update, leaving, d_gate, d_hidden,
-        gain, full_proj, down, up,
+        gains, proj, up,
     )
-    proj_wgrad = jnp.concatenate([tn(normed, d_qkv).astype(BF16), tn(normed, d_gate).astype(BF16)], axis=1)
+    rank_grad = tn(normed, d_mid)[:, :RANK]
+    extra_grad = beside([rank_grad] + [g.reshape(-1, 1) for g in (gain_grad, head_gain_grad, ffn_gain_grad)])
+    proj_wgrad = jnp.concatenate(
+        [tn(normed, d_qkv).astype(BF16), tn(normed, d_gate).astype(BF16), extra_grad.astype(BF16)], axis=1
+    )
     out_wgrad = tn(gated, hidden_low).astype(BF16)
-    down_rank_grad = tn(normed, d_mid)[:, :rank]
-    up_rank_grad = tn(mid, d_logit)[:rank]
-    tiles = packed(
-        [
-            gain_grad.reshape(count, -1),
-            down_rank_grad.reshape(count, -1),
-            up_rank_grad.reshape(rank, count, -1).transpose(1, 0, 2),
-            bias_grad.reshape(count, -1),
-            head_gain_grad.reshape(count, -1),
-            ffn_gain_grad.reshape(count, -1),
-        ]
-    ).astype(BF16)
-    summed = scatter_all(
-        [tiles, proj_wgrad, out_wgrad, fgate_wgrad, fup_wgrad, fdown_wgrad], BACK_PARTS, sizes, 1
+    up_wgrad = tn(d_logit, mid).astype(BF16)
+    up_sum, proj_sum, out_sum, fgate_sum, fup_sum, fdown_sum = scatter_all(
+        [up_wgrad, proj_wgrad, out_wgrad, fgate_wgrad, fup_wgrad, fdown_wgrad], BACK_PARTS, sizes, 1
     )
-    gain_sum, down_sum, up_sum, bias_sum, head_sum, ffn_sum = [p[0] for p in unpacked(summed[0], shapes)]
-    proj_sum, keys = summed[1], HEADS * HK
+    keys, values = HEADS * HK, HEADS * HV
+    last = 2 * (keys + values)
+    gain_sum, head_sum, ffn_sum = (proj_sum[:, last + RANK + k] for k in range(3))
     return (
         block_output,
         tokens_grad,
         gain_sum,
         proj_sum[:, :keys],
         proj_sum[:, keys : 2 * keys],
-        proj_sum[:, 2 * keys : 2 * keys + HEADS * HV],
-        proj_sum[:, 2 * keys + HEADS * HV :],
-        down_sum,
-        up_sum,
-        bias_sum,
+        proj_sum[:, 2 * keys : 2 * keys + values],
+        proj_sum[:, 2 * keys + values : last],
+        proj_sum[:, last : last + RANK],
+        up_sum[:, :RANK].T,
+        up_sum[:, RANK],
         head_sum,
-        summed[2],
+        out_sum,
         ffn_sum,
-        summed[3],
-        summed[4],
-        summed[5],
+        fgate_sum,
+        fup_sum,
+        fdown_sum,
     )
 
 

time: 498 us -> 481 us (0.966)
  Pallas kernels: 433 us -> 417 us
    pallas_call x2 -> x1, Pallas kernels: 56.7 us -> 23.6 us  [entering(): pl.pallas_call(functools.partial(scan_kernel, sizes, backward), out_shape...]
    concatenate x2 -> x3, local copies, waits for them, and re-layouts: 0.93 us -> 12.7 us  [the longest x1 10.9 us: local(): jnp.concatenate([tn(normed, d_qkv).astype(BF16), tn(normed, d_gate).astyp...]
    pallas_call x3 -> x1, Pallas kernels: 128 us -> 138 us  [front(): pl.pallas_call(functools.partial(front_kernel, sizes, steps), grid=(2 * s...]
    unnamed x50 -> x36, local copies, waits for them, and re-layouts: 12 us -> 8.51 us
where the time goes in v3:
time: 481 us; the launch traced here: 474 us
  Pallas kernels  417 us (87%)
  local copies, waits for them, and re-layouts  36.5 us (8%)
  matrix products  18.5 us (4%)
    pallas_call x1, Pallas kernels, scatter_all(): pl.pallas_call(functools.partial(scatter_kernel, sizes, parts, len(partia...  146 us
    pallas_call x1, Pallas kernels, front(): pl.pallas_call(functools.partial(front_kernel, sizes, steps), grid=(2 * s...  138 us
    pallas_call x1, Pallas kernels, feed_forward(): pl.pallas_call(ffn_kernel, grid=(inner // FTILE,), in_specs=[kept_spec(a....  64.8 us
    pallas_call x1, Pallas kernels, back(): pl.pallas_call(back_kernel, grid=(steps,), in_specs=[row(w) for w in (wid...  27.5 us
    pallas_call x1, Pallas kernels, entering(): pl.pallas_call(functools.partial(scan_kernel, sizes, backward), out_shape...  23.6 us
    dot_general x5, matrix products, tn(): lax.dot_general(left, right, (((0,), (0,)), ((), ())), preferred_element_...  18.5 us
    pallas_call x1, Pallas kernels, unmix(): pl.pallas_call(unmix_kernel, grid=(steps,), in_specs=[row(w) for w in (wi...  16.9 us
    concatenate x1, local copies, waits for them, and re-layouts, local(): jnp.concatenate([tn(normed, d_qkv).astype(BF16), tn(normed, d_gate).astyp...  10.9 us

profile of v3, /device:TPU:8, one launch (start us, length us, event | category | flops | bytes accessed | tf_op | source)
XLA Modules:
  0.0 473.8 jit_solution(7829638073625730869)
XLA Ops:
  0.6 0.8 copy.45
  1.4 0.8 copy.46
  3.7 1.7 concatenate.13.refs_2_
  5.4 0.8 copy.43
  7.6 138.2 %shard_map.279 = (bf16[4,2,2,2,16,128]{5,4,3,2,1,0:T(8,128)(2,1)}, bf16[4,2,2,2,32,3200]{5,4,3,2,1,0:T(8,128)(2,1)}, bf16[4,2,2,2,32,1024]{5,4,3,2,1,0:T(8,128)(...) custom-call(bf16[1024,1024]{1,0:T(8,128)(2,1)} %tokens.1, ...), custom_call_target="tpu_custom_call" | custom-call | tf_op jit(solution)/shard_map/pallas_call | solution.py:1154
  145.8 3.9 copy.49
  149.8 64.8 %shard_map.280 = (f32[1024,1024]{1,0:T(8,128)}, f32[1024,1024]{1,0:T(8,128)}, bf16[1024,2816]{1,0:T(8,128)(2,1)}, bf16[1024,2816]{1,0:T(8,128)(2,1)}, bf16[2816,1024]{1,0:T(8,128)(2,1)}) custom-call(bf16[1024,1024]{1,0:T(8,128)(2,1)} %get-tuple-element.61.ffn_in, bf16[1024,1024]{1,0:T(8,128)(2,1)} %bitcast.38, bf16[1024,1024]{1,0:T(8,128)(2,1)} %cotangent.3, ...), custom_call_target="tpu_custom_call" | custom-call | tf_op jit(solution)/shard_map/pallas_call | solution.py:1189
  214.6 16.9 %shard_map.281 = (f32[1024,1024]{1,0:T(8,128)}, bf16[1024,1024]{1,0:T(8,128)(2,1)}, bf16[1024,1024]{1,0:T(8,128)(2,1)}, f32[1024,1024]{1,0:T(8,128)}, bf16[8,4,2...) custom-call(f32[1024,1024]{1,0:T(8,128)} %get-tuple-element.72.ffn_back, ...), custom_call_target="tpu_custom_call" | custom-call | tf_op jit(solution)/shard_map/pallas_call | solution.py:1206
  231.6 5.4 %convolution_convert_fusion.1 = bf16[1024,1024]{1,0:T(8,128)(2,1)} fusion(bf16[1024,1024]{1,0:T(8,128)(2,1)S(1)} %copy-done.13, bf16[1024,1024]{1,0:T(8,128)(2,1)} %get-tuple-element.96), kind=kOutput, calls=%fused_computation.1 | convolution fusion | flops 2148532224 | bytes 6291456 | tf_op jit(solution)/shard_map/dot_general | solution.py:705
  237.4 23.6 %shard_map.282.leaving_ref = f32[4,256,128]{2,1,0:T(8,128)S(1)} custom-call(f32[4,256,128]{2,1,0:T(8,128)S(1)} %copy-done.1, f32[4,8,128]{2,1,0:T(8,128)S(1)} %copy-done.2), custom_call_target="tpu_custom_call" | custom-call | tf_op jit(solution)/shard_map/pallas_call | solution.py:678
  261.0 0.8 copy-done
  261.8 27.5 %shard_map.283 = (bf16[1024,2048]{1,0:T(8,128)(2,1)}, bf16[1024,512]{1,0:T(8,128)(2,1)}, bf16[1024,128]{1,0:T(8,128)(2,1)}, f32[1024,1024]{1,0:T(8,128)}, f32[1,1024]{1,0:T(1,128)}) custom-call(bf16[1024,1024]{1,0:T(8,128)(2,1)} %tokens.1, bf16[1024,512]{1,0:T(8,128)(2,1)} %get-tuple-element.67.query, bf16[1024,512]{1,0:T(8,128)(2,1)} %get-tuple-element.68.key, ...), custom_call_target="tpu_custom_call" | custom-call | tf_op jit(solution)/shard_map/pallas_call | solution.py:1228
  289.3 1.9 fusion.2
  291.2 3.8 convolution_convert_fusion.2
  295.0 6.3 %convolution_convert_fusion = bf16[1024,2048]{1,0:T(8,128)(2,1)} fusion(bf16[1024,1024]{1,0:T(8,128)(2,1)S(1)} %copy-done.3, bf16[1024,2048]{1,0:T(8,128)(2,1)S(1)} %copy-done.12), kind=kOutput, calls=%fused_computation | convolution fusion | flops 4297064448 | bytes 10485760 | tf_op jit(solution)/shard_map/dot_general | solution.py:705
  301.6 10.9 %concatenate.14 = bf16[1024,3200]{1,0:T(8,128)(2,1)} concatenate(bf16[1024,2048]{1,0:T(8,128)(2,1)} %convolution_convert_fusion, bf16[1024,1024]{1,0:T(8,128)(2,1)} %convolution_convert_fusion.2, bf16[1024,16]{1,0:T(8,128)(2,1)S(1)} %bitcast.48, bf16[1024,1]{1,0:T(8,128)(2,1)S(1)} %copy.52, bf16[1024,1]{1,0:T(8,128)(2,1)S(1)} %copy.53, bf16[1024,1]{1,0:T(8,128)(2,1)S(1)} %copy.54, ...), dimensions={1} | concatenate | bytes 13107200 | tf_op jit(solution)/shard_map/concatenate | solution.py:1299
  312.6 1.1 convolution_convert_fusion.3
  313.7 145.8 %shard_map.284 = (f32[16,128]{1,0:T(8,128)}, f32[32,3200]{1,0:T(8,128)}, f32[32,1024]{1,0:T(8,128)}, f32[32,2816]{1,0:T(8,128)}, f32[32,2816]{1,0:T(8,128)}, /*index=5*/f32[88,1024]{1,0:T(8,128)}) custom-call(bf16[4,2,2,2,16,128]{5,4,3,2,1,0:T(8,128)(2,1)} %bitcast.49, bf16[4,2,2,2,32,3200]{5,4,3,2,1,0:T(8,128)(2,1)} %bitcast.37, ...), custom_call_target="tpu_custom_call" | custom-call | tf_op jit(solution)/shard_map/pallas_call | solution.py:520
  459.5 1.8 fusion
  461.3 1.5 fusion.1
  465.6 1.6 slice_reduce_fusion
  467.2 1.4 slice_reduce_fusion.3
  468.6 1.6 copy.63
  470.1 1.7 copy.64
  (46 shorter events, 8.0 us)
Async XLA Ops:
  214.6 17.0 %copy-start.13 = (bf16[1024,1024]{1,0:T(8,128)(2,1)S(1)}, bf16[1024,1024]{1,0:T(8,128)(2,1)}, u32[]{:S(2)}) copy-start(bf16[1024,1024]{1,0:T(8,128)(2,1)} %get-tuple-element.95) | copy-start | bytes 6291460
  231.5 5.5 %copy-start.10 = (f32[1,1024]{1,0:T(1,128)S(1)}, f32[1,1024]{1,0:T(1,128)}, u32[]{:S(2)}) copy-start(f32[1,1024]{1,0:T(1,128)} %get-tuple-element.94) | copy-start | bytes 12292
  231.6 5.4 %copy-start.11 = (f32[1,1024]{1,0:T(1,128)S(1)}, f32[1,1024]{1,0:T(1,128)}, u32[]{:S(2)}) copy-start(f32[1,1024]{1,0:T(1,128)} %get-tuple-element.93) | copy-start | bytes 12292
  231.6 5.9 %copy-start.1 = (f32[4,256,128]{2,1,0:T(8,128)S(1)}, f32[4,256,128]{2,1,0:T(8,128)}, u32[]{:S(2)}) copy-start(f32[4,256,128]{2,1,0:T(8,128)} %get-tuple-element.80.refs_0_) | copy-start | bytes 1572868
  231.6 5.9 %copy-start.2 = (f32[4,8,128]{2,1,0:T(8,128)S(1)}, f32[4,8,128]{2,1,0:T(8,128)}, u32[]{:S(2)}) copy-start(f32[4,8,128]{2,1,0:T(8,128)} %get-tuple-element.81.refs_1_) | copy-start | bytes 49156
  261.0 0.8 copy-start
  261.8 27.5 %copy-start.3 = (bf16[1024,1024]{1,0:T(8,128)(2,1)S(1)}, bf16[1024,1024]{1,0:T(8,128)(2,1)}, u32[]{:S(2)}) copy-start(bf16[1024,1024]{1,0:T(8,128)(2,1)} %get-tuple-element.89) | copy-start | bytes 6291460
  289.3 1.9 copy-start.4
  291.2 3.8 copy-start.12
  295.0 6.3 %copy-start.9 = (f32[1,1024]{1,0:T(1,128)S(1)}, f32[1,1024]{1,0:T(1,128)}, u32[]{:S(2)}) copy-start(f32[1,1024]{1,0:T(1,128)} %get-tuple-element.92) | copy-start | bytes 12292
  301.6 11.0 %copy-start.5 = (bf16[1024,512]{1,0:T(8,128)(2,1)S(1)}, bf16[1024,512]{1,0:T(8,128)(2,1)}, u32[]{:S(2)}) copy-start(bf16[1024,512]{1,0:T(8,128)(2,1)} %get-tuple-element.87) | copy-start | bytes 3145732
  301.6 11.0 %copy-start.8 = (bf16[1024,128]{1,0:T(8,128)(2,1)S(1)}, bf16[1024,128]{1,0:T(8,128)(2,1)}, u32[]{:S(2)}) copy-start(bf16[1024,128]{1,0:T(8,128)(2,1)} %get-tuple-element.88) | copy-start | bytes 786436
  459.5 12.3 %copy-start.7 = (f32[32,2816]{1,0:T(8,128)S(1)}, f32[32,2816]{1,0:T(8,128)}, u32[]{:S(2)}) copy-start(f32[32,2816]{1,0:T(8,128)} %get-tuple-element.177) | copy-start | bytes 1081348
  459.5 13.1 %copy-start.6 = (f32[88,1024]{1,0:T(8,128)S(1)}, f32[88,1024]{1,0:T(8,128)}, u32[]{:S(2)}) copy-start(f32[88,1024]{1,0:T(8,128)} %get-tuple-element.178) | copy-start | bytes 1081348

commit v4 on v3

--- a/solution.py
+++ b/solution.py
@@ -286,10 +286,16 @@
         self.partial, self.columns, self.held, self.bufs, self.out = partial, columns, held, bufs, out
         self.load, self.send, self.recv = load, send, recv
 
+    def lines(self):
+        size = self.place.sizes[LINE]
+        return [k // 2 if k % 2 == 0 else size - 1 - k // 2 for k in range(size)]
+
     def own(self, line):
         first, width = self.columns
         where = (line, slice(None), slice(None), self.place.here[CORE], slice(None), pl.ds(first, width))
-        return pltpu.make_async_copy(self.partial.at[where], self.held.at[line], self.load.at[self.part, line])
+        return pltpu.make_async_copy(
+            self.partial.at[where], self.bufs[0].at[self.lines().index(line) % 2], self.load.at[self.part, line]
+        )
 
     def block(self, stage, line, along):
         where, done = [], self.order[:stage]
@@ -329,7 +335,7 @@
         there = self.slot(stage, line, number)
         return pltpu.make_async_remote_copy(
             src_ref=source,
-            dst_ref=self.bufs[stage].at[there],
+            dst_ref=self.held.at[line] if axis == CORE else self.bufs[stage].at[there],
             send_sem=self.send.at[(self.part, stage) + sem],
             recv_sem=self.recv.at[(self.part, stage) + there + ((0,) if axis == LINE else ())],
             device_id=place.toward(axis, step),
@@ -338,8 +344,8 @@
 
     def wait(self, stage, line, number):
         there = self.slot(stage, line, number)
-        buf = self.bufs[stage].at[there]
         axis = self.order[stage]
+        buf = self.held.at[line] if axis == CORE else self.bufs[stage].at[there]
         pltpu.make_async_copy(
             buf, buf, self.recv.at[(self.part, stage) + there + ((0,) if axis == LINE else ())]
         ).wait()
@@ -354,6 +360,7 @@
         where = self.block(stage, line, along)
         if self.order[stage] == CORE:
             where = (line, slice(None), slice(None))
+            there = (self.lines().index(line) % 2,)
         total = self.held[where].astype(jnp.float32) + buf[there].astype(jnp.float32)
         self.held[where] = total.astype(self.held.dtype)
 
@@ -415,9 +422,7 @@
     def steps(self):
         place = self.place
         size, here = place.sizes[LINE], place.here[LINE]
-        lines = []
-        for k in range(size):
-            lines.append(k // 2 if k % 2 == 0 else size - 1 - k // 2)
+        lines = self.lines()
         spot = self.order.index(LINE)
 
         def begin(k):
@@ -504,6 +509,8 @@
             slots = 1 if sizes[axis] <= 2 else sizes[axis] + 1
             if axis == LINE:
                 lead = (slots,)
+            elif axis == CORE:
+                lead = (2,)
             else:
                 lead = (1 if LINE in stages[:stage] else sizes[LINE], slots)
             scratch.append(pltpu.VMEM(lead + free + (rows, width), dtype))
@@ -908,16 +915,10 @@
             enters_ref[h] = enters_ref[h] * jnp.exp(total[:, ks]) + update
 
 
-def back_kernel(
-    tokens, query, key, value, logit, within_all, d_mixed, starts, update, leaving_ref, d_gate, d_hidden,
-    gains, weights, up,
-    d_qkv_ref, d_logit_ref, d_mid_ref, tokens_grad_ref, gain_ref, state,
+def back_rows(
+    tokens, query, key, value, logit, within_all, d_mixed, starts, update, d_gate, d_hidden, gains, weights, up,
+    d_proj_ref, d_logit_ref, tokens_grad_ref, gain_ref, state,
 ):
-    @pl.when(pl.program_id(0) == 0)
-    def _():
-        state[...] = leaving_ref[...]
-        gain_ref[...] = jnp.zeros_like(gain_ref)
-
     mask = causal_mask(CHUNK)
     upper = triangle(True)
     keys = HEADS * HK
@@ -943,9 +944,9 @@
             d_query = nn(d_scores, right[:, ks]) * q_middle[:, ks] + nn(grad, start) * q_start[:, ks]
             d_end = nn(values, after) * k_end[:, ks]
             d_key = tn(d_scores, left[:, ks]) * k_middle[:, ks] + d_end
-            d_qkv_ref[rows, ks] = d_query.astype(BF16)
-            d_qkv_ref[rows, slice(keys + ks.start, keys + ks.stop)] = d_key.astype(BF16)
-            d_qkv_ref[rows, slice(2 * keys + vs.start, 2 * keys + vs.stop)] = d_value.astype(BF16)
+            d_proj_ref[rows, ks] = d_query.astype(BF16)
+            d_proj_ref[rows, slice(keys + ks.start, keys + ks.stop)] = d_key.astype(BF16)
+            d_proj_ref[rows, slice(2 * keys + vs.start, 2 * keys + vs.stop)] = d_value.astype(BF16)
             moves.append(queries[:, ks] * d_query - keys_f[:, ks] * d_key)
             extras.append(
                 jnp.sum(keys_f[:, ks] * d_end, axis=0, keepdims=True)
@@ -957,15 +958,75 @@
         d_logit_ref[rows] = d_logit.astype(BF16)
     d_mid = nn(d_logit_ref[...], up[...])
     d_mid = jnp.where(lax.broadcasted_iota(jnp.int32, d_mid.shape, 1) < RANK, d_mid, 0.0).astype(BF16)
-    d_mid_ref[...] = d_mid
     inner = 2 * keys + HEADS * HV
     outer = inner + HEADS * HV
-    d_normed = (
-        nt(d_qkv_ref[...], weights[:, :inner]) + nt(d_gate[...], weights[:, inner:outer]) + nt(d_mid, weights[:, outer:])
-    )
+    d_proj_ref[:, inner:outer] = d_gate[...]
+    d_proj_ref[:, outer:] = d_mid
+    d_normed = nt(d_proj_ref[...], weights[...])
     through, terms = norm_back(tokens[...].astype(F32), gains[0:1], d_normed)
     gain_ref[...] += jnp.sum(terms, axis=0, keepdims=True)
     tokens_grad_ref[...] = d_hidden[...] + through
+
+
+def back_kernel(*refs):
+    tiles, leaving_ref, refs = refs[:11], refs[11], refs[12:]
+    gain_ref, state = refs[-2:]
+
+    @pl.when(pl.program_id(0) == 0)
+    def _():
+        state[...] = leaving_ref[...]
+        gain_ref[...] = jnp.zeros_like(gain_ref)
+
+    back_rows(*tiles, *refs)
+
+
+def tail_kernel(sizes, steps, count, *refs):
+    tiles, (enters, logs), refs = refs[:11], refs[11:13], refs[13:]
+    kept, partials, refs = refs[:3], refs[3 : 3 + count], refs[3 + count :]
+    outs, gain_ref, sums, refs = refs[:3], refs[3], refs[4 : 4 + count], refs[4 + count :]
+    state, load, send, recv = refs[:4]
+    scratch, scan = refs[4 : 4 + 5 * len(TAIL_PARTS)], refs[4 + 5 * len(TAIL_PARTS) :]
+    place = Place(sizes)
+    step = pl.program_id(0)
+    scatters = []
+    for k, (which, columns, order) in enumerate(TAIL_PARTS):
+        held, *bufs = scratch[5 * k : 5 * k + 5]
+        scatters.append(
+            Scatter(place, k, order, partials[which], columns, held, bufs, sums[which], load, send, recv)
+        )
+    moves = [s.steps() for s in scatters]
+
+    def turn():
+        for move in moves:
+            next(move, None)
+
+    def during(hop):
+        for _ in range(TAIL_TURNS[0].count(hop)):
+            turn()
+
+    @pl.when(step == 0)
+    def _():
+        gain_ref[...] = jnp.zeros_like(gain_ref)
+        place.greet(partners_of(sizes))
+        turn()
+        scan_states(place, True, during, enters, logs, state, *scan)
+
+    for k in range(1, steps + 1):
+
+        @pl.when(step == k)
+        def _(k=k):
+            for _ in range(TAIL_TURNS[1].count(k)):
+                turn()
+
+    @pl.when(step > 0)
+    def _():
+        back_rows(*tiles, *kept, *outs, gain_ref, state)
+
+    @pl.when(step == steps)
+    def _():
+        run_all(moves)
+        for s in scatters:
+            s.drain()
 
 
 def rows_spec(width, steps, backward):
@@ -1219,29 +1280,80 @@
     )(ffn_back, hidden, cotangent, gate, mixed, query, within, gains, out_weight)
 
 
-def back(tokens, query, key, value, logit, within, d_mixed, starts, update, leaving, d_gate, d_hidden, gains, weights, up):
-    length, width = tokens.shape
+def back(tiles, leaving, gains, weights, up):
+    length, width = tiles[0].shape
     steps, keys, values = length // ROWS, HEADS * HK, HEADS * HV
     row = lambda w: rows_spec(w, steps, True)
     shape = jax.ShapeDtypeStruct
-    inner = 2 * keys + values
     return pl.pallas_call(
         back_kernel,
         grid=(steps,),
         in_specs=[row(w) for w in (width, keys, keys, values, keys, keys, values)]
-        + [chunks_spec(steps, True)] * 2 + [kept_spec(leaving.shape), row(values), row(width)]
-        + [kept_spec(a.shape) for a in (gains, weights, up)],
-        out_specs=[row(w) for w in (inner, keys, 128, width)] + [kept_out((1, width))],
+        + [chunks_spec(steps, True)] * 2 + [row(values), row(width)]
+        + [kept_spec(a.shape) for a in (leaving, gains, weights, up)],
+        out_specs=[row(w) for w in (weights.shape[1], keys, width)] + [kept_out((1, width))],
         out_shape=[
-            shape((length, inner), BF16), shape((length, keys), BF16), shape((length, 128), BF16),
+            shape((length, weights.shape[1]), BF16), shape((length, keys), BF16),
             shape((length, width), F32), shape((1, width), F32),
         ],
         scratch_shapes=[pltpu.VMEM(STATE, F32)],
         compiler_params=pltpu.CompilerParams(**PARAMS),
-    )(tokens, query, key, value, logit, within, d_mixed, starts, update, leaving, d_gate, d_hidden, gains, weights, up)
-
-
-BACK_PARTS = tuple((which, columns, order[::-1]) for which, columns, order in FRONT_PARTS)
+    )(*tiles, leaving, gains, weights, up)
+
+
+TAIL_PARTS = (
+    (0, (0, 2816), ORDERS[1][::-1]),
+    (1, (0, 2816), ORDERS[0][::-1]),
+    (2, (0, 512), ORDERS[2][::-1]),
+    (2, (512, 512), ORDERS[3][::-1]),
+    (3, (0, 512), ORDERS[2][::-1]),
+    (3, (512, 512), ORDERS[3][::-1]),
+)
+TAIL_TURNS = ((1, 2, 3), (1, 2, 3, 4))
+LAST_PARTS = (
+    (0, (0, 128), ORDERS[0][::-1]),
+    (1, (0, 1024), ORDERS[0][::-1]),
+    (1, (1024, 1024), ORDERS[1][::-1]),
+    (1, (2048, 640), ORDERS[2][::-1]),
+    (1, (2688, 512), ORDERS[3][::-1]),
+)
+
+
+def tail(tiles, enters, logs, gains, weights, up, partials, sizes, collective_id):
+    length, width = tiles[0].shape
+    steps, keys, values = length // ROWS, HEADS * HK, HEADS * HV
+    shape, at = jax.ShapeDtypeStruct, lambda i: steps - jnp.maximum(i, 1)
+    row = lambda w: pl.BlockSpec((ROWS, w), lambda i: (at(i), 0))
+    chunk = pl.BlockSpec((ROWS // CHUNK,) + STATE, lambda i: (at(i), 0, 0, 0))
+    count = len(partials)
+    devices = sizes[0] * sizes[1] * sizes[2] * sizes[3]
+    partials = [p.reshape(sizes + (p.shape[0] // devices, p.shape[1])) for p in partials]
+    lanes = max([1] + [size + 1 for size in sizes[1:] if size > 2])
+    sems = (len(TAIL_PARTS), 4, sizes[0] + 1, lanes)
+    out = pl.pallas_call(
+        functools.partial(tail_kernel, sizes, steps, count),
+        grid=(steps + 1,),
+        in_specs=[row(w) for w in (width, keys, keys, values, keys, keys, values)]
+        + [chunk] * 2 + [row(values), row(width)]
+        + [kept_spec(a.shape) for a in (enters, logs, gains, weights, up)]
+        + [pl.BlockSpec(memory_space=pl.ANY)] * count,
+        out_specs=[row(w) for w in (weights.shape[1], keys, width)] + [kept_out((1, width))]
+        + [kept_out(p.shape[4:]) for p in partials],
+        out_shape=[
+            shape((length, weights.shape[1]), BF16), shape((length, keys), BF16),
+            shape((length, width), F32), shape((1, width), F32),
+        ] + [shape(p.shape[4:], F32) for p in partials],
+        scratch_shapes=[
+            pltpu.VMEM(STATE, F32),
+            pltpu.SemaphoreType.DMA((len(TAIL_PARTS), sizes[0])),
+            pltpu.SemaphoreType.DMA(sems),
+            pltpu.SemaphoreType.DMA(sems),
+        ]
+        + scatter_scratch(sizes, TAIL_PARTS, [p.shape for p in partials], BF16)
+        + scan_scratch(sizes),
+        compiler_params=pltpu.CompilerParams(collective_id=collective_id, has_side_effects=True, **PARAMS),
+    )(*tiles, enters, logs, gains, weights, up, *partials)
+    return out[:4], out[4:]
 
 
 def beside(pieces):
@@ -1289,24 +1401,28 @@
     d_hidden, hidden_low, d_gate, d_mixed, back_update, enters, ffn_gain_grad, head_gain_grad = unmix(
         ffn_back, hidden, cotangent, gate, mixed, query, within, gains, out
     )
-    leaving = entering(enters, logs, sizes, True, 3)
-    d_qkv, d_logit, d_mid, tokens_grad, gain_grad = back(
-        tokens, query, key, value, logit, within, d_mixed, starts, back_update, leaving, d_gate, d_hidden,
-        gains, proj, up,
-    )
-    rank_grad = tn(normed, d_mid)[:, :RANK]
-    extra_grad = beside([rank_grad] + [g.reshape(-1, 1) for g in (gain_grad, head_gain_grad, ffn_gain_grad)])
-    proj_wgrad = jnp.concatenate(
-        [tn(normed, d_qkv).astype(BF16), tn(normed, d_gate).astype(BF16), extra_grad.astype(BF16)], axis=1
-    )
     out_wgrad = tn(gated, hidden_low).astype(BF16)
-    up_wgrad = tn(d_logit, mid).astype(BF16)
-    up_sum, proj_sum, out_sum, fgate_sum, fup_sum, fdown_sum = scatter_all(
-        [up_wgrad, proj_wgrad, out_wgrad, fgate_wgrad, fup_wgrad, fdown_wgrad], BACK_PARTS, sizes, 1
-    )
+    early = [fgate_wgrad, fup_wgrad, fdown_wgrad, out_wgrad]
+    tiles = (tokens, query, key, value, logit, within, d_mixed, starts, back_update, d_gate, d_hidden)
+    if rank_up.shape[1] % 16 == 0:
+        backs, early_sums = tail(tiles, enters, logs, gains, proj, up, early, sizes, 3)
+    else:
+        leaving = entering(enters, logs, sizes, True, 3)
+        backs = back(tiles, leaving, gains, proj, up)
+        early_sums = scatter_all(early, TAIL_PARTS, sizes, 4)
+    d_proj, d_logit, tokens_grad, gain_grad = backs
+    fgate_sum, fup_sum, fdown_sum, out_sum = early_sums
+    proj_wgrad = tn(normed, d_proj).astype(BF16)
+    keys_here = rank_up.shape[1]
+    gain_grads = jnp.concatenate([gain_grad, head_gain_grad, ffn_gain_grad]).reshape(3, -1, norm_gain.shape[0] // keys_here, keys_here)
+    gain_grads = gain_grads.transpose(1, 3, 0, 2).reshape(HEADS * HK, -1)
+    up_wgrad = beside([tn(d_logit, mid)[:, : RANK + 1], gain_grads]).astype(BF16)
+    up_sum, proj_sum = scatter_all([up_wgrad, proj_wgrad], LAST_PARTS, sizes, 1)
     keys, values = HEADS * HK, HEADS * HV
     last = 2 * (keys + values)
-    gain_sum, head_sum, ffn_sum = (proj_sum[:, last + RANK + k] for k in range(3))
+    gain_sum, head_sum, ffn_sum = (
+        up_sum[:, RANK + 1 : RANK + 1 + 3 * (norm_gain.shape[0] // keys_here)].reshape(keys_here, 3, -1).transpose(1, 2, 0).reshape(3, -1)
+    )
     return (
         block_output,
         tokens_grad,

time: 481 us -> 458 us (0.952)
  Pallas kernels: 417 us -> 400 us
  local copies, waits for them, and re-layouts: 36.5 us -> 28.7 us
    pallas_call x1, Pallas kernels: 146 us -> 45.5 us  [scatter_all(): pl.pallas_call(functools.partial(scatter_kernel, sizes, parts, len(partia...]
    pallas_call x2 -> x1, Pallas kernels: 51 us -> 135 us  [tail(): pl.pallas_call(functools.partial(tail_kernel, sizes, steps, count), grid=...]
    concatenate x1 -> x0, local copies, waits for them, and re-layouts: 10.9 us -> none  [local(): jnp.concatenate([tn(normed, d_qkv).astype(BF16), tn(normed, d_gate).astyp...]
    unnamed x36 -> x31, local copies, waits for them, and re-layouts: 8.51 us -> 10.7 us
    dot_general x5 -> x3, matrix products: 18.5 us -> 17.9 us  [tn(): lax.dot_general(left, right, (((0,), (0,)), ((), ())), preferred_element_...]
where the time goes in v4:
time: 458 us; the launch traced here: 449 us
  Pallas kernels  400 us (87%)
  local copies, waits for them, and re-layouts  28.7 us (6%)
  matrix products  17.9 us (4%)
    pallas_call x1, Pallas kernels, front(): pl.pallas_call(functools.partial(front_kernel, sizes, steps), grid=(2 * s...  138 us
    pallas_call x1, Pallas kernels, tail(): pl.pallas_call(functools.partial(tail_kernel, sizes, steps, count), grid=...  135 us
    pallas_call x1, Pallas kernels, feed_forward(): pl.pallas_call(ffn_kernel, grid=(inner // FTILE,), in_specs=[kept_spec(a....  64.8 us
    pallas_call x1, Pallas kernels, scatter_all(): pl.pallas_call(functools.partial(scatter_kernel, sizes, parts, len(partia...  45.5 us
    dot_general x3, matrix products, tn(): lax.dot_general(left, right, (((0,), (0,)), ((), ())), preferred_element_...  17.9 us
    pallas_call x1, Pallas kernels, unmix(): pl.pallas_call(unmix_kernel, grid=(steps,), in_specs=[row(w) for w in (wi...  17 us
    unnamed x31, local copies, waits for them, and re-layouts  10.7 us

profile of v4, /device:TPU:8, one launch (start us, length us, event | category | flops | bytes accessed | tf_op | source)
XLA Modules:
  0.0 449.5 jit_solution(16445636444674073828)
XLA Ops:
  0.6 0.8 copy.46
  1.4 0.8 copy.47
  2.2 0.8 copy.48
  2.9 0.8 copy.49
  3.7 1.7 concatenate.20.refs_2_
  5.4 0.8 copy.44
  6.1 0.7 copy.45
  7.6 138.3 %shard_map.279 = (bf16[4,2,2,2,16,128]{5,4,3,2,1,0:T(8,128)(2,1)}, bf16[4,2,2,2,32,3200]{5,4,3,2,1,0:T(8,128)(2,1)}, bf16[4,2,2,2,32,1024]{5,4,3,2,1,0:T(8,128)(...) custom-call(bf16[1024,1024]{1,0:T(8,128)(2,1)} %refs_0_.3, ...), custom_call_target="tpu_custom_call" | custom-call | tf_op jit(solution)/shard_map/pallas_call | solution.py:1215
  145.9 3.9 copy.50
  149.9 64.8 %shard_map.280 = (f32[1024,1024]{1,0:T(8,128)}, f32[1024,1024]{1,0:T(8,128)}, bf16[1024,2816]{1,0:T(8,128)(2,1)}, bf16[1024,2816]{1,0:T(8,128)(2,1)}, bf16[2816,1024]{1,0:T(8,128)(2,1)}) custom-call(bf16[1024,1024]{1,0:T(8,128)(2,1)} %get-tuple-element.60.ffn_in, bf16[1024,1024]{1,0:T(8,128)(2,1)} %bitcast.31, bf16[1024,1024]{1,0:T(8,128)(2,1)} %cotangent.3, ...), custom_call_target="tpu_custom_call" | custom-call | tf_op jit(solution)/shard_map/pallas_call | solution.py:1250
  214.7 17.0 %shard_map.281 = (f32[1024,1024]{1,0:T(8,128)}, bf16[1024,1024]{1,0:T(8,128)(2,1)}, bf16[1024,1024]{1,0:T(8,128)(2,1)}, f32[1024,1024]{1,0:T(8,128)}, bf16[8,4,2...) custom-call(f32[1024,1024]{1,0:T(8,128)} %get-tuple-element.71.ffn_back, ...), custom_call_target="tpu_custom_call" | custom-call | tf_op jit(solution)/shard_map/pallas_call | solution.py:1267
  231.7 5.3 %convolution_convert_fusion.1 = bf16[1024,1024]{1,0:T(8,128)(2,1)} fusion(bf16[1024,1024]{1,0:T(8,128)(2,1)S(1)} %copy-done.10, bf16[1024,1024]{1,0:T(8,128)(2,1)} %get-tuple-element.89), kind=kOutput, calls=%fused_computation.1 | convolution fusion | flops 2148532224 | bytes 6291456 | tf_op jit(solution)/shard_map/dot_general | solution.py:712
  237.0 134.6 %shard_map.282 = (bf16[1024,3200]{1,0:T(8,128)(2,1)}, bf16[1024,512]{1,0:T(8,128)(2,1)}, f32[1024,1024]{1,0:T(8,128)}, f32[1,1024]{1,0:T(1,128)}, f32[32,2816]{1...) custom-call(bf16[1024,1024]{1,0:T(8,128)(2,1)} %refs_0_.3, ...), custom_call_target="tpu_custom_call" | custom-call | tf_op jit(solution)/shard_map/pallas_call | solution.py:1333
  371.6 12.2 %convolution_convert_fusion = bf16[1024,3200]{1,0:T(8,128)(2,1)} fusion(bf16[1024,1024]{1,0:T(8,128)(2,1)S(1)} %copy-done.9, bf16[1024,3200]{1,0:T(8,128)(2,1)} %get-tuple-element.97), kind=kOutput, calls=%fused_computation | convolution fusion | flops 6714163200 | bytes 15204352 | tf_op jit(solution)/shard_map/dot_general | solution.py:712
  384.9 0.8 maximum_maximum_fusion.refs_0_
  385.7 45.5 %shard_map.283 = (f32[16,128]{1,0:T(8,128)}, f32[32,3200]{1,0:T(8,128)}) custom-call(bf16[4,2,2,2,16,128]{5,4,3,2,1,0:T(8,128)(2,1)} %maximum_maximum_fusion.refs_0_, bf16[4,2,2,2,32,3200]{5,4,3,2,1,0:T(8,128)(2,1)} %bitcast.32), custom_call_target="tpu_custom_call" | custom-call | tf_op jit(solution)/shard_map/pallas_call | solution.py:527
  431.2 1.7 fusion
  432.9 1.5 fusion.1
  435.8 0.8 slice.32
  439.9 1.4 slice_reduce_fusion
  441.3 4.9 %copy.62 = f32[1024,1024]{1,0:T(8,128)} copy(f32[1024,1024]{1,0:T(8,128)} %get-tuple-element.160) | data formatting | bytes 8388608
  446.8 0.7 copy.64
  447.5 0.7 copy.65
  448.3 0.7 copy.66
  (49 shorter events, 7.1 us)
Async XLA Ops:
  214.7 17.0 %copy-start.10 = (bf16[1024,1024]{1,0:T(8,128)(2,1)S(1)}, bf16[1024,1024]{1,0:T(8,128)(2,1)}, u32[]{:S(2)}) copy-start(bf16[1024,1024]{1,0:T(8,128)(2,1)} %get-tuple-element.88) | copy-start | bytes 6291460
  237.0 134.6 %copy-start.9 = (bf16[1024,1024]{1,0:T(8,128)(2,1)S(1)}, bf16[1024,1024]{1,0:T(8,128)(2,1)}, u32[]{:S(2)}) copy-start(bf16[1024,1024]{1,0:T(8,128)(2,1)} %get-tuple-element.96) | copy-start | bytes 6291460
  371.5 12.3 %copy-start = (bf16[1024,512]{1,0:T(8,128)(2,1)S(1)}, bf16[1024,512]{1,0:T(8,128)(2,1)}, u32[]{:S(2)}) copy-start(bf16[1024,512]{1,0:T(8,128)(2,1)} %get-tuple-element.91) | copy-start | bytes 3145732
  371.5 12.3 %copy-start.4 = (bf16[1024,128]{1,0:T(8,128)(2,1)S(1)}, bf16[1024,128]{1,0:T(8,128)(2,1)}, u32[]{:S(2)}) copy-start(bf16[1024,128]{1,0:T(8,128)(2,1)} %get-tuple-element.92) | copy-start | bytes 786436
  371.5 12.8 %copy-start.8 = (f32[1,1024]{1,0:T(1,128)S(1)}, f32[1,1024]{1,0:T(1,128)}, u32[]{:S(2)}) copy-start(f32[1,1024]{1,0:T(1,128)} %get-tuple-element.93) | copy-start | bytes 12292
  371.6 12.8 %copy-start.7 = (f32[1,1024]{1,0:T(1,128)S(1)}, f32[1,1024]{1,0:T(1,128)}, u32[]{:S(2)}) copy-start(f32[1,1024]{1,0:T(1,128)} %get-tuple-element.94) | copy-start | bytes 12292
  371.6 12.8 %copy-start.6 = (f32[1,1024]{1,0:T(1,128)S(1)}, f32[1,1024]{1,0:T(1,128)}, u32[]{:S(2)}) copy-start(f32[1,1024]{1,0:T(1,128)} %get-tuple-element.95) | copy-start | bytes 12292
  441.3 4.9 %copy-start.5 = (f32[32,1024]{1,0:T(8,128)S(1)}, f32[32,1024]{1,0:T(8,128)}, u32[]{:S(2)}) copy-start(f32[32,1024]{1,0:T(8,128)} %get-tuple-element.170) | copy-start | bytes 393220
  441.3 5.6 %copy-start.3 = (f32[32,2816]{1,0:T(8,128)S(1)}, f32[32,2816]{1,0:T(8,128)}, u32[]{:S(2)}) copy-start(f32[32,2816]{1,0:T(8,128)} %get-tuple-element.172) | copy-start | bytes 1081348
  441.3 6.3 %copy-start.2 = (f32[32,2816]{1,0:T(8,128)S(1)}, f32[32,2816]{1,0:T(8,128)}, u32[]{:S(2)}) copy-start(f32[32,2816]{1,0:T(8,128)} %get-tuple-element.173) | copy-start | bytes 1081348
  441.3 7.0 %copy-start.1 = (f32[88,1024]{1,0:T(8,128)S(1)}, f32[88,1024]{1,0:T(8,128)}, u32[]{:S(2)}) copy-start(f32[88,1024]{1,0:T(8,128)} %get-tuple-element.174) | copy-start | bytes 1081348

commit v5 on v4

--- a/solution.py
+++ b/solution.py
@@ -280,6 +280,9 @@
     return [o.reshape((-1,) + o.shape[5:]) for o in out]
 
 
+PACE = 1
+
+
 class Scatter:
     def __init__(self, place, part, order, partial, columns, held, bufs, out, load, send, recv):
         self.place, self.part, self.order = place, part, (CORE,) + order
@@ -294,7 +297,7 @@
         first, width = self.columns
         where = (line, slice(None), slice(None), self.place.here[CORE], slice(None), pl.ds(first, width))
         return pltpu.make_async_copy(
-            self.partial.at[where], self.bufs[0].at[self.lines().index(line) % 2], self.load.at[self.part, line]
+            self.partial.at[where], self.bufs[0].at[self.lines().index(line) % (2 * PACE)], self.load.at[self.part, line]
         )
 
     def block(self, stage, line, along):
@@ -360,7 +363,7 @@
         where = self.block(stage, line, along)
         if self.order[stage] == CORE:
             where = (line, slice(None), slice(None))
-            there = (self.lines().index(line) % 2,)
+            there = (self.lines().index(line) % (2 * PACE),)
         total = self.held[where].astype(jnp.float32) + buf[there].astype(jnp.float32)
         self.held[where] = total.astype(self.held.dtype)
 
@@ -425,28 +428,33 @@
         lines = self.lines()
         spot = self.order.index(LINE)
 
-        def begin(k):
-            self.own(lines[k]).start()
-            self.launch(0, lines[k])
-
-        begin(0)
+        groups = [lines[k : k + PACE] for k in range(0, size, PACE)]
+
+        def begin(group):
+            for line in group:
+                self.own(line).start()
+                self.launch(0, line)
+
+        begin(groups[0])
         yield
-        for turn in range(2 * size + spot - 2):
-            if turn + 1 < size:
-                begin(turn + 1)
-            for k in range(size):
+        for turn in range(len(groups) + spot + size - 2):
+            if turn + 1 < len(groups):
+                begin(groups[turn + 1])
+            for k, group in enumerate(groups):
                 hop = turn - k - spot
                 if 0 <= hop < size - 1:
-                    self.line_hop(lines[k], hop)
+                    for line in group:
+                        self.line_hop(line, hop)
             for stage in range(spot - 1, -1, -1):
                 k = turn - stage
-                if not 0 <= k < size:
+                if not 0 <= k < len(groups):
                     continue
-                if stage == 0:
-                    self.own(lines[k]).wait()
-                self.whole(stage, lines[k])
-                if stage + 1 < spot:
-                    self.launch(stage + 1, lines[k])
+                for line in groups[k]:
+                    if stage == 0:
+                        self.own(line).wait()
+                    self.whole(stage, line)
+                    if stage + 1 < spot:
+                        self.launch(stage + 1, line)
             yield
         if spot == 3:
             self.begin_out()
@@ -510,7 +518,7 @@
             if axis == LINE:
                 lead = (slots,)
             elif axis == CORE:
-                lead = (2,)
+                lead = (2 * PACE,)
             else:
                 lead = (1 if LINE in stages[:stage] else sizes[LINE], slots)
             scratch.append(pltpu.VMEM(lead + free + (rows, width), dtype))
@@ -765,8 +773,9 @@
 def project_rows(tokens, gain, weight, up, outs, final_ref, logs_ref):
     normed_ref, query_ref, key_ref, value_ref, gate_ref, mid_ref, logit_ref, within_ref, update_ref = outs
     inputs = tokens[...].astype(F32)
-    normed = (inputs * inverse_rms(inputs) * gain).astype(BF16)
-    normed_ref[...] = normed
+    normed = inputs * inverse_rms(inputs) * gain
+    normed_ref[...] = (normed.T if normed_ref.shape[0] != tokens.shape[0] else normed).astype(BF16)
+    normed = normed.astype(BF16)
     keys = HEADS * HK
     values = HEADS * HV
     mid = with_one(nn(normed, weight(2 * keys + 2 * values, 128)))
@@ -829,7 +838,9 @@
             gated_ref[rows, vs] = gated.astype(BF16)
     hidden = tokens[...].astype(F32) + nn(gated_ref[...], out_weight)
     hidden_ref[...] = hidden
-    ffn_ref[...] = (hidden * inverse_rms(hidden) * ffn_gain).astype(BF16)
+    ffn_in = hidden * inverse_rms(hidden) * ffn_gain
+    ffn_ref[...] = ffn_in.astype(BF16)
+    return ffn_in
 
 
 def mix_kernel(tokens, query, key, value, gate, within_all, update, entering_ref, gains, out_weight, *refs):
@@ -1110,7 +1121,7 @@
 def front_kernel(sizes, steps, *refs):
     tokens, shards, refs = refs[0], refs[1:7], refs[7:]
     buffers, refs = refs[:6], refs[6:]
-    outs, mixed_outs, (logs_out, gains_out), refs = refs[:8], refs[8:13], refs[13:15], refs[15:]
+    outs, mixed_outs, (logs_out, gains_out, ffn_t_ref), refs = refs[:8], refs[8:13], refs[13:16], refs[16:]
     up_all, proj_all, out_all, query, key, value, gate, within, update, state, final, logs, gains, refs = *refs[:13], refs[13:]
     send, recv, own, flush = refs[:4]
     scan = refs[4:]
@@ -1187,10 +1198,11 @@
         at = step - steps
         rows = pl.ds(pl.multiple_of(at * ROWS, ROWS), ROWS)
         chunks = pl.ds(at * (ROWS // CHUNK), ROWS // CHUNK)
-        mix_rows(
+        ffn_in = mix_rows(
             tokens, query.at[rows], key.at[rows], value.at[rows], gate.at[rows], within.at[rows], update.at[chunks], state,
             gains[1:2], out_all[...].reshape(-1, out_all.shape[-1]), gains[2:3], mixed_outs,
         )
+        ffn_t_ref[...] = ffn_in.T.astype(BF16)
 
     @pl.when(step == 2 * steps - 1)
     def _():
@@ -1210,20 +1222,22 @@
     lanes = lanes_of(sizes)
     parts = len(FRONT_PARTS)
     one = lambda w, t: ((length, w), t)
-    results = [one(width, BF16), one(keys, BF16), one(keys, BF16), one(values, BF16), one(values, BF16), one(128, BF16), one(keys, F32), one(keys, F32)]
+    turned = lambda first: pl.BlockSpec((width, ROWS), lambda i: (0, jnp.minimum(i, steps - 1) if first else jnp.maximum(i - steps, 0)))
+    results = [one(keys, BF16), one(keys, BF16), one(values, BF16), one(values, BF16), one(128, BF16), one(keys, F32), one(keys, F32)]
     mixes = [one(values, F32), one(values, BF16), one(width, F32), one(width, BF16)]
     out = pl.pallas_call(
         functools.partial(front_kernel, sizes, steps),
         grid=(2 * steps,),
         in_specs=[pl.BlockSpec((ROWS, width), lambda i: (lax.rem(i, steps), 0))] + [kept_spec(s.shape) for s in shards],
         out_specs=[pl.BlockSpec(memory_space=pl.ANY)] * len(shards)
-        + [first(s[1]) for s, _ in results]
+        + [turned(True)] + [first(s[1]) for s, _ in results]
         + [second(s[1]) for s, _ in mixes]
         + [pl.BlockSpec((ROWS // CHUNK,) + STATE, lambda i: (jnp.maximum(i - steps, 0), 0, 0, 0))]
-        + [kept_out((HEADS, 8, HK)), kept_out((8, width))],
+        + [kept_out((HEADS, 8, HK)), kept_out((8, width)), turned(False)],
         out_shape=[shape(sizes + s.shape, s.dtype) for s in shards]
+        + [shape((width, length), BF16)]
         + [shape(s, t) for s, t in results + mixes]
-        + [shape(chunks, BF16), shape((HEADS, 8, HK), F32), shape((8, width), F32)],
+        + [shape(chunks, BF16), shape((HEADS, 8, HK), F32), shape((8, width), F32), shape((width, length), BF16)],
         scratch_shapes=[pltpu.VMEM(sizes + s.shape, s.dtype) for s in shards[:3]]
         + [pltpu.VMEM((length, w), t) for w, t in ((keys, BF16), (keys, BF16), (values, BF16), (values, BF16), (keys, F32))]
         + [pltpu.VMEM(chunks, BF16), pltpu.VMEM(STATE, F32), pltpu.VMEM(STATE, F32), pltpu.VMEM((HEADS, 8, HK), F32), pltpu.VMEM((8, width), F32)]
@@ -1240,10 +1254,10 @@
     return weights, out[len(shards) :]
 
 
-def feed_forward(ffn_in, cotangent, hidden, gate_weight, up_weight, down_weight):
+def feed_forward(ffn_in, ffn_t, cotangent, hidden, gate_weight, up_weight, down_weight):
     length, width = ffn_in.shape
     inner = gate_weight.shape[1]
-    whole = [ffn_in, ffn_in.T, cotangent, hidden]
+    whole = [ffn_in, ffn_t, cotangent, hidden]
     wide = pl.BlockSpec((width, FTILE), lambda i: (0, i))
     tall = pl.BlockSpec((FTILE, width), lambda i: (i, 0))
     shape = jax.ShapeDtypeStruct
@@ -1309,7 +1323,7 @@
     (3, (0, 512), ORDERS[2][::-1]),
     (3, (512, 512), ORDERS[3][::-1]),
 )
-TAIL_TURNS = ((1, 2, 3), (1, 2, 3, 4))
+TAIL_TURNS = ((2, 4), (1, 2, 3, 4))
 LAST_PARTS = (
     (0, (0, 128), ORDERS[0][::-1]),
     (1, (0, 1024), ORDERS[0][::-1]),
@@ -1356,6 +1370,56 @@
     return out[:4], out[4:]
 
 
+def last_kernel(sizes, *refs):
+    normed_t, d_proj, small, small_out, proj_out, load, send, recv = refs[:8]
+    scratch = refs[8 : 8 + 5 * len(LAST_PARTS)]
+    partials = [small] + list(refs[8 + 5 * len(LAST_PARTS) :])
+    place = Place(sizes)
+    place.greet()
+    moves, scatters = [], []
+    for k, (which, (first, width), order) in enumerate(LAST_PARTS):
+        for move in moves:
+            next(move, None)
+        out = small_out
+        if which:
+            out = proj_out.at[:, pl.ds(first, width)]
+            for at in range(0, width, 512):
+                tile = min(512, width - at)
+                grad = nn(normed_t[...], d_proj[:, first + at : first + at + tile]).astype(BF16)
+                partials[k][..., pl.ds(at, tile)] = grad.reshape(partials[k].shape[:-1] + (tile,))
+        held, *bufs = scratch[5 * k : 5 * k + 5]
+        scatters.append(Scatter(place, k, order, partials[k], (0, width), held, bufs, out, load, send, recv))
+        moves.append(scatters[-1].steps())
+        next(moves[-1])
+    run_all(moves)
+    for s in scatters:
+        s.drain()
+
+
+def project_grads(normed_t, d_proj, small, sizes, collective_id):
+    devices = sizes[0] * sizes[1] * sizes[2] * sizes[3]
+    small = small.reshape(sizes + (small.shape[0] // devices, small.shape[1]))
+    rows = d_proj.shape[1], normed_t.shape[0] // devices
+    shapes = [small.shape, sizes + (rows[1], rows[0])]
+    lanes = max([1] + [size + 1 for size in sizes[1:] if size > 2])
+    sems = (len(LAST_PARTS), 4, sizes[0] + 1, lanes)
+    vmem = pl.BlockSpec(memory_space=pltpu.VMEM)
+    return pl.pallas_call(
+        functools.partial(last_kernel, sizes),
+        out_shape=[jax.ShapeDtypeStruct(s[4:], F32) for s in shapes],
+        in_specs=[vmem, vmem, pl.BlockSpec(memory_space=pl.ANY)],
+        out_specs=[vmem] * 2,
+        scratch_shapes=[
+            pltpu.SemaphoreType.DMA((len(LAST_PARTS), sizes[0])),
+            pltpu.SemaphoreType.DMA(sems),
+            pltpu.SemaphoreType.DMA(sems),
+        ]
+        + scatter_scratch(sizes, LAST_PARTS, shapes, BF16)
+        + [pltpu.VMEM(shapes[1][:-1] + (width,), BF16) for which, (_, width), _ in LAST_PARTS if which],
+        compiler_params=pltpu.CompilerParams(collective_id=collective_id, has_side_effects=True, **PARAMS),
+    )(normed_t, d_proj, small)
+
+
 def beside(pieces):
     rows, used = pieces[0].shape[0], sum(p.shape[1] for p in pieces)
     return jnp.concatenate(pieces + [jnp.zeros((rows, 128 - used), pieces[0].dtype)], axis=1)
@@ -1386,7 +1450,7 @@
     if rank_up.shape[1] % 16 == 0:
         weights, kept = front(tokens, shards, sizes, 0)
         up, proj, out, full_fgate, full_fup, full_fdown = weights
-        normed, query, key, value, gate, mid, logit, within, mixed, gated, hidden, ffn_in, starts, logs, gains = kept
+        normed_t, query, key, value, gate, mid, logit, within, mixed, gated, hidden, ffn_in, starts, logs, gains, ffn_t = kept
     else:
         up, proj, out, full_fgate, full_fup, full_fdown = gather_all(shards, FRONT_PARTS, sizes, 0)
         gains = jnp.pad(proj[:, -128 + RANK : -128 + RANK + 3].astype(F32).T, ((0, 5), (0, 0)))
@@ -1395,8 +1459,9 @@
         mixed, gated, hidden, ffn_in, starts = mix(
             tokens, query, key, value, gate, within, update, incoming, gains, out
         )
+        normed_t, ffn_t = normed.T, ffn_in.T
     block_output, ffn_back, fgate_wgrad, fup_wgrad, fdown_wgrad = feed_forward(
-        ffn_in, cotangent, hidden, full_fgate, full_fup, full_fdown
+        ffn_in, ffn_t, cotangent, hidden, full_fgate, full_fup, full_fdown
     )
     d_hidden, hidden_low, d_gate, d_mixed, back_update, enters, ffn_gain_grad, head_gain_grad = unmix(
         ffn_back, hidden, cotangent, gate, mixed, query, within, gains, out
@@ -1412,12 +1477,14 @@
         early_sums = scatter_all(early, TAIL_PARTS, sizes, 4)
     d_proj, d_logit, tokens_grad, gain_grad = backs
     fgate_sum, fup_sum, fdown_sum, out_sum = early_sums
-    proj_wgrad = tn(normed, d_proj).astype(BF16)
     keys_here = rank_up.shape[1]
     gain_grads = jnp.concatenate([gain_grad, head_gain_grad, ffn_gain_grad]).reshape(3, -1, norm_gain.shape[0] // keys_here, keys_here)
     gain_grads = gain_grads.transpose(1, 3, 0, 2).reshape(HEADS * HK, -1)
     up_wgrad = beside([tn(d_logit, mid)[:, : RANK + 1], gain_grads]).astype(BF16)
-    up_sum, proj_sum = scatter_all([up_wgrad, proj_wgrad], LAST_PARTS, sizes, 1)
+    if keys_here % 16 == 0:
+        up_sum, proj_sum = project_grads(normed_t, d_proj, up_wgrad, sizes, 1)
+    else:
+        up_sum, proj_sum = scatter_all([up_wgrad, nn(normed_t, d_proj).astype(BF16)], LAST_PARTS, sizes, 1)
     keys, values = HEADS * HK, HEADS * HV
     last = 2 * (keys + values)
     gain_sum, head_sum, ffn_sum = (

time: 458 us -> 448 us (0.978)
  matrix products: 17.9 us -> 6.87 us
  Pallas kernels: 400 us -> 405 us
    dot_general x3 -> x2, matrix products: 17.9 us -> 6.87 us  [tn(): lax.dot_general(left, right, (((0,), (0,)), ((), ())), preferred_element_...]
    pallas_call x1, Pallas kernels: 45.5 us -> 53.5 us  [project_grads(): pl.pallas_call(functools.partial(last_kernel, sizes), out_shape=[jax.Shap...]
    unnamed x31 -> x25, local copies, waits for them, and re-layouts: 10.7 us -> 10.6 us
where the time goes in v5:
time: 448 us; the launch traced here: 440 us
  Pallas kernels  405 us (90%)
  local copies, waits for them, and re-layouts  24.7 us (6%)
  matrix products  6.87 us (2%)
    pallas_call x1, Pallas kernels, front(): pl.pallas_call(functools.partial(front_kernel, sizes, steps), grid=(2 * s...  139 us
    pallas_call x1, Pallas kernels, tail(): pl.pallas_call(functools.partial(tail_kernel, sizes, steps, count), grid=...  131 us
    pallas_call x1, Pallas kernels, feed_forward(): pl.pallas_call(ffn_kernel, grid=(inner // FTILE,), in_specs=[kept_spec(a....  64.8 us
    pallas_call x1, Pallas kernels, project_grads(): pl.pallas_call(functools.partial(last_kernel, sizes), out_shape=[jax.Shap...  53.5 us
    pallas_call x1, Pallas kernels, unmix(): pl.pallas_call(unmix_kernel, grid=(steps,), in_specs=[row(w) for w in (wi...  17 us
    unnamed x25, local copies, waits for them, and re-layouts  10.6 us

profile of v5, /device:TPU:8, one launch (start us, length us, event | category | flops | bytes accessed | tf_op | source)
XLA Modules:
  0.0 439.9 jit_solution(8430397233688288534)
XLA Ops:
  0.6 0.8 copy.45
  1.4 0.8 copy.46
  2.2 0.8 copy.47
  2.9 0.8 copy.48
  3.7 1.7 concatenate.20.refs_2_
  5.4 0.8 copy.43
  6.1 0.7 copy.44
  7.6 138.9 %shard_map.279 = (bf16[4,2,2,2,16,128]{5,4,3,2,1,0:T(8,128)(2,1)}, bf16[4,2,2,2,32,3200]{5,4,3,2,1,0:T(8,128)(2,1)}, bf16[4,2,2,2,32,1024]{5,4,3,2,1,0:T(8,128)(...) custom-call(bf16[1024,1024]{1,0:T(8,128)(2,1)} %refs_0_.3, ...), custom_call_target="tpu_custom_call" | custom-call | tf_op jit(solution)/shard_map/pallas_call | solution.py:1228
  146.5 64.8 %shard_map.280 = (f32[1024,1024]{1,0:T(8,128)}, f32[1024,1024]{1,0:T(8,128)}, bf16[1024,2816]{1,0:T(8,128)(2,1)}, bf16[1024,2816]{1,0:T(8,128)(2,1)}, bf16[2816,1024]{1,0:T(8,128)(2,1)}) custom-call(bf16[1024,1024]{1,0:T(8,128)(2,1)} %get-tuple-element.61.ffn_in, bf16[1024,1024]{1,0:T(8,128)(2,1)} %get-tuple-element.62.ffn_in_t, ...), custom_call_target="tpu_custom_call" | custom-call | tf_op jit(solution)/shard_map/pallas_call | solution.py:1264
  211.4 17.0 %shard_map.281 = (f32[1024,1024]{1,0:T(8,128)}, bf16[1024,1024]{1,0:T(8,128)(2,1)}, bf16[1024,1024]{1,0:T(8,128)(2,1)}, f32[1024,1024]{1,0:T(8,128)}, bf16[8,4,2...) custom-call(f32[1024,1024]{1,0:T(8,128)} %get-tuple-element.73.ffn_back, ...), custom_call_target="tpu_custom_call" | custom-call | tf_op jit(solution)/shard_map/pallas_call | solution.py:1281
  228.3 5.3 %convolution_convert_fusion = bf16[1024,1024]{1,0:T(8,128)(2,1)} fusion(bf16[1024,1024]{1,0:T(8,128)(2,1)S(1)} %copy-done.7, bf16[1024,1024]{1,0:T(8,128)(2,1)} %get-tuple-element.91), kind=kOutput, calls=%fused_computation | convolution fusion | flops 2148532224 | bytes 6291456 | tf_op jit(solution)/shard_map/dot_general | solution.py:720
  233.6 130.8 %shard_map.282 = (bf16[1024,3200]{1,0:T(8,128)(2,1)}, bf16[1024,512]{1,0:T(8,128)(2,1)}, f32[1024,1024]{1,0:T(8,128)}, f32[1,1024]{1,0:T(1,128)}, f32[32,2816]{1...) custom-call(bf16[1024,1024]{1,0:T(8,128)(2,1)} %refs_0_.3, ...), custom_call_target="tpu_custom_call" | custom-call | tf_op jit(solution)/shard_map/pallas_call | solution.py:1347
  364.4 1.6 fusion.3
  367.4 0.8 maximum_maximum_fusion.refs_2_
  368.2 53.5 %shard_map.283 = (f32[16,128]{1,0:T(8,128)}, f32[32,3200]{1,0:T(8,128)}) custom-call(bf16[1024,1024]{1,0:T(8,128)(2,1)} %get-tuple-element.93.refs_0_, bf16[1024,3200]{1,0:T(8,128)(2,1)} %get-tuple-element.94.refs_1_, bf16[4,2,2,2,16,128]{5,4,3,2,1,0:T(8,128)(2,1)} %maximum_maximum_fusion.refs_2_), custom_call_target="tpu_custom_call" | custom-call | tf_op jit(solution)/shard_map/pallas_call | solution.py:1407
  421.7 1.7 fusion
  423.3 1.5 fusion.1
  424.9 0.7 slice.37
  426.3 0.8 slice.32
  430.3 1.4 slice_reduce_fusion
  431.7 4.9 %copy.60 = f32[1024,1024]{1,0:T(8,128)} copy(f32[1024,1024]{1,0:T(8,128)} %get-tuple-element.162) | data formatting | bytes 8388608
  437.2 0.7 copy.62
  438.0 0.7 copy.63
  438.7 0.7 copy.64
  (41 shorter events, 6.7 us)
Async XLA Ops:
  211.4 17.0 %copy-start.7 = (bf16[1024,1024]{1,0:T(8,128)(2,1)S(1)}, bf16[1024,1024]{1,0:T(8,128)(2,1)}, u32[]{:S(2)}) copy-start(bf16[1024,1024]{1,0:T(8,128)(2,1)} %get-tuple-element.90) | copy-start | bytes 6291460
  233.6 130.8 %copy-start.3 = (bf16[1024,128]{1,0:T(8,128)(2,1)S(1)}, bf16[1024,128]{1,0:T(8,128)(2,1)}, u32[]{:S(2)}) copy-start(bf16[1024,128]{1,0:T(8,128)(2,1)} %get-tuple-element.96) | copy-start | bytes 786436
  233.6 133.2 %copy-start.6 = (f32[1,1024]{1,0:T(1,128)S(1)}, f32[1,1024]{1,0:T(1,128)}, u32[]{:S(2)}) copy-start(f32[1,1024]{1,0:T(1,128)} %get-tuple-element.98) | copy-start | bytes 12292
  233.6 133.2 %copy-start.5 = (f32[1,1024]{1,0:T(1,128)S(1)}, f32[1,1024]{1,0:T(1,128)}, u32[]{:S(2)}) copy-start(f32[1,1024]{1,0:T(1,128)} %get-tuple-element.99) | copy-start | bytes 12292
  431.7 4.9 %copy-start.4 = (f32[32,1024]{1,0:T(8,128)S(1)}, f32[32,1024]{1,0:T(8,128)}, u32[]{:S(2)}) copy-start(f32[32,1024]{1,0:T(8,128)} %get-tuple-element.172) | copy-start | bytes 393220
  431.7 5.6 %copy-start.2 = (f32[32,2816]{1,0:T(8,128)S(1)}, f32[32,2816]{1,0:T(8,128)}, u32[]{:S(2)}) copy-start(f32[32,2816]{1,0:T(8,128)} %get-tuple-element.174) | copy-start | bytes 1081348
  431.7 6.3 %copy-start.1 = (f32[32,2816]{1,0:T(8,128)S(1)}, f32[32,2816]{1,0:T(8,128)}, u32[]{:S(2)}) copy-start(f32[32,2816]{1,0:T(8,128)} %get-tuple-element.175) | copy-start | bytes 1081348
  431.7 7.0 %copy-start = (f32[88,1024]{1,0:T(8,128)S(1)}, f32[88,1024]{1,0:T(8,128)}, u32[]{:S(2)}) copy-start(f32[88,1024]{1,0:T(8,128)} %get-tuple-element.176) | copy-start | bytes 1081348

commit v6 on v5

--- a/solution.py
+++ b/solution.py
@@ -1316,12 +1316,11 @@
 
 
 TAIL_PARTS = (
-    (0, (0, 2816), ORDERS[1][::-1]),
-    (1, (0, 2816), ORDERS[0][::-1]),
-    (2, (0, 512), ORDERS[2][::-1]),
-    (2, (512, 512), ORDERS[3][::-1]),
-    (3, (0, 512), ORDERS[2][::-1]),
-    (3, (512, 512), ORDERS[3][::-1]),
+    (2, (0, 512), (0, 2, 1)),
+    (3, (0, 1024), (0, 1, 2)),
+    (0, (0, 2816), (1, 2, 0)),
+    (1, (0, 2816), (2, 1, 0)),
+    (2, (512, 512), (1, 2, 0)),
 )
 TAIL_TURNS = ((2, 4), (1, 2, 3, 4))
 LAST_PARTS = (

time: 448 us -> 443 us (0.989)
  Pallas kernels: 405 us -> 400 us
    pallas_call x1, Pallas kernels: 131 us -> 124 us  [tail(): pl.pallas_call(functools.partial(tail_kernel, sizes, steps, count), grid=...]
where the time goes in v6:
time: 443 us; the launch traced here: 435 us
  Pallas kernels  400 us (90%)
  local copies, waits for them, and re-layouts  24.7 us (6%)
  matrix products  6.86 us (2%)
    pallas_call x1, Pallas kernels, front(): pl.pallas_call(functools.partial(front_kernel, sizes, steps), grid=(2 * s...  139 us
    pallas_call x1, Pallas kernels, tail(): pl.pallas_call(functools.partial(tail_kernel, sizes, steps, count), grid=...  124 us
    pallas_call x1, Pallas kernels, feed_forward(): pl.pallas_call(ffn_kernel, grid=(inner // FTILE,), in_specs=[kept_spec(a....  64.8 us
    pallas_call x1, Pallas kernels, project_grads(): pl.pallas_call(functools.partial(last_kernel, sizes), out_shape=[jax.Shap...  55.4 us
    pallas_call x1, Pallas kernels, unmix(): pl.pallas_call(unmix_kernel, grid=(steps,), in_specs=[row(w) for w in (wi...  17 us
    unnamed x25, local copies, waits for them, and re-layouts  10.6 us

profile of v6, /device:TPU:8, one launch (start us, length us, event | category | flops | bytes accessed | tf_op | source)
XLA Modules:
  0.0 435.1 jit_solution(5401956639684441062)
XLA Ops:
  0.6 0.8 copy.45
  1.4 0.8 copy.46
  2.2 0.8 copy.47
  2.9 0.8 copy.48
  3.7 1.7 concatenate.20.refs_2_
  5.4 0.8 copy.43
  6.1 0.7 copy.44
  7.6 138.9 %shard_map.279 = (bf16[4,2,2,2,16,128]{5,4,3,2,1,0:T(8,128)(2,1)}, bf16[4,2,2,2,32,3200]{5,4,3,2,1,0:T(8,128)(2,1)}, bf16[4,2,2,2,32,1024]{5,4,3,2,1,0:T(8,128)(...) custom-call(bf16[1024,1024]{1,0:T(8,128)(2,1)} %refs_0_.3, ...), custom_call_target="tpu_custom_call" | custom-call | tf_op jit(solution)/shard_map/pallas_call | solution.py:1228
  146.5 64.8 %shard_map.280 = (f32[1024,1024]{1,0:T(8,128)}, f32[1024,1024]{1,0:T(8,128)}, bf16[1024,2816]{1,0:T(8,128)(2,1)}, bf16[1024,2816]{1,0:T(8,128)(2,1)}, bf16[2816,1024]{1,0:T(8,128)(2,1)}) custom-call(bf16[1024,1024]{1,0:T(8,128)(2,1)} %get-tuple-element.61.ffn_in, bf16[1024,1024]{1,0:T(8,128)(2,1)} %get-tuple-element.62.ffn_in_t, ...), custom_call_target="tpu_custom_call" | custom-call | tf_op jit(solution)/shard_map/pallas_call | solution.py:1264
  211.4 17.0 %shard_map.281 = (f32[1024,1024]{1,0:T(8,128)}, bf16[1024,1024]{1,0:T(8,128)(2,1)}, bf16[1024,1024]{1,0:T(8,128)(2,1)}, f32[1024,1024]{1,0:T(8,128)}, bf16[8,4,2...) custom-call(f32[1024,1024]{1,0:T(8,128)} %get-tuple-element.73.ffn_back, ...), custom_call_target="tpu_custom_call" | custom-call | tf_op jit(solution)/shard_map/pallas_call | solution.py:1281
  228.3 5.3 %convolution_convert_fusion = bf16[1024,1024]{1,0:T(8,128)(2,1)} fusion(bf16[1024,1024]{1,0:T(8,128)(2,1)S(1)} %copy-done.7, bf16[1024,1024]{1,0:T(8,128)(2,1)} %get-tuple-element.91), kind=kOutput, calls=%fused_computation | convolution fusion | flops 2148532224 | bytes 6291456 | tf_op jit(solution)/shard_map/dot_general | solution.py:720
  233.6 124.0 %shard_map.282 = (bf16[1024,3200]{1,0:T(8,128)(2,1)}, bf16[1024,512]{1,0:T(8,128)(2,1)}, f32[1024,1024]{1,0:T(8,128)}, f32[1,1024]{1,0:T(1,128)}, f32[32,2816]{1...) custom-call(bf16[1024,1024]{1,0:T(8,128)(2,1)} %refs_0_.3, ...), custom_call_target="tpu_custom_call" | custom-call | tf_op jit(solution)/shard_map/pallas_call | solution.py:1346
  357.7 1.6 fusion.3
  360.7 0.8 maximum_maximum_fusion.refs_2_
  361.4 55.4 %shard_map.283 = (f32[16,128]{1,0:T(8,128)}, f32[32,3200]{1,0:T(8,128)}) custom-call(bf16[1024,1024]{1,0:T(8,128)(2,1)} %get-tuple-element.93.refs_0_, bf16[1024,3200]{1,0:T(8,128)(2,1)} %get-tuple-element.94.refs_1_, bf16[4,2,2,2,16,128]{5,4,3,2,1,0:T(8,128)(2,1)} %maximum_maximum_fusion.refs_2_), custom_call_target="tpu_custom_call" | custom-call | tf_op jit(solution)/shard_map/pallas_call | solution.py:1406
  416.9 1.7 fusion
  418.6 1.5 fusion.1
  420.1 0.7 slice.37
  421.5 0.8 slice.32
  425.5 1.4 slice_reduce_fusion
  426.9 4.9 %copy.60 = f32[1024,1024]{1,0:T(8,128)} copy(f32[1024,1024]{1,0:T(8,128)} %get-tuple-element.162) | data formatting | bytes 8388608
  432.5 0.7 copy.62
  433.2 0.7 copy.63
  433.9 0.7 copy.64
  (41 shorter events, 6.7 us)
Async XLA Ops:
  211.4 17.0 %copy-start.7 = (bf16[1024,1024]{1,0:T(8,128)(2,1)S(1)}, bf16[1024,1024]{1,0:T(8,128)(2,1)}, u32[]{:S(2)}) copy-start(bf16[1024,1024]{1,0:T(8,128)(2,1)} %get-tuple-element.90) | copy-start | bytes 6291460
  233.6 124.1 %copy-start.3 = (bf16[1024,128]{1,0:T(8,128)(2,1)S(1)}, bf16[1024,128]{1,0:T(8,128)(2,1)}, u32[]{:S(2)}) copy-start(bf16[1024,128]{1,0:T(8,128)(2,1)} %get-tuple-element.96) | copy-start | bytes 786436
  233.6 126.5 %copy-start.6 = (f32[1,1024]{1,0:T(1,128)S(1)}, f32[1,1024]{1,0:T(1,128)}, u32[]{:S(2)}) copy-start(f32[1,1024]{1,0:T(1,128)} %get-tuple-element.98) | copy-start | bytes 12292
  233.6 126.5 %copy-start.5 = (f32[1,1024]{1,0:T(1,128)S(1)}, f32[1,1024]{1,0:T(1,128)}, u32[]{:S(2)}) copy-start(f32[1,1024]{1,0:T(1,128)} %get-tuple-element.99) | copy-start | bytes 12292
  426.9 4.9 %copy-start.4 = (f32[32,1024]{1,0:T(8,128)S(1)}, f32[32,1024]{1,0:T(8,128)}, u32[]{:S(2)}) copy-start(f32[32,1024]{1,0:T(8,128)} %get-tuple-element.172) | copy-start | bytes 393220
  426.9 5.6 %copy-start.2 = (f32[32,2816]{1,0:T(8,128)S(1)}, f32[32,2816]{1,0:T(8,128)}, u32[]{:S(2)}) copy-start(f32[32,2816]{1,0:T(8,128)} %get-tuple-element.174) | copy-start | bytes 1081348
  426.9 6.3 %copy-start.1 = (f32[32,2816]{1,0:T(8,128)S(1)}, f32[32,2816]{1,0:T(8,128)}, u32[]{:S(2)}) copy-start(f32[32,2816]{1,0:T(8,128)} %get-tuple-element.175) | copy-start | bytes 1081348
  426.9 7.0 %copy-start = (f32[88,1024]{1,0:T(8,128)S(1)}, f32[88,1024]{1,0:T(8,128)}, u32[]{:S(2)}) copy-start(f32[88,1024]{1,0:T(8,128)} %get-tuple-element.176) | copy-start | bytes 1081348

commit v7 on v6

--- a/solution.py
+++ b/solution.py
@@ -1322,7 +1322,7 @@
     (1, (0, 2816), (2, 1, 0)),
     (2, (512, 512), (1, 2, 0)),
 )
-TAIL_TURNS = ((2, 4), (1, 2, 3, 4))
+TAIL_TURNS = ((3, 5), (1, 2, 3, 4))
 LAST_PARTS = (
     (0, (0, 128), ORDERS[0][::-1]),
     (1, (0, 1024), ORDERS[0][::-1]),

time: 443 us -> 443 us (level)
  no operation moved by 1% of the time
where the time goes in v7:
time: 443 us; the launch traced here: 435 us
  Pallas kernels  400 us (90%)
  local copies, waits for them, and re-layouts  24.7 us (6%)
  matrix products  6.87 us (2%)
    pallas_call x1, Pallas kernels, front(): pl.pallas_call(functools.partial(front_kernel, sizes, steps), grid=(2 * s...  139 us
    pallas_call x1, Pallas kernels, tail(): pl.pallas_call(functools.partial(tail_kernel, sizes, steps, count), grid=...  124 us
    pallas_call x1, Pallas kernels, feed_forward(): pl.pallas_call(ffn_kernel, grid=(inner // FTILE,), in_specs=[kept_spec(a....  64.8 us
    pallas_call x1, Pallas kernels, project_grads(): pl.pallas_call(functools.partial(last_kernel, sizes), out_shape=[jax.Shap...  55.3 us
    pallas_call x1, Pallas kernels, unmix(): pl.pallas_call(unmix_kernel, grid=(steps,), in_specs=[row(w) for w in (wi...  17 us
    unnamed x25, local copies, waits for them, and re-layouts  10.6 us

profile of v7, /device:TPU:8, one launch (start us, length us, event | category | flops | bytes accessed | tf_op | source)
XLA Modules:
  0.0 434.6 jit_solution(3818935032432768693)
XLA Ops:
  0.6 0.8 copy.45
  1.4 0.8 copy.46
  2.2 0.8 copy.47
  2.9 0.8 copy.48
  3.7 1.7 concatenate.20.refs_2_
  5.4 0.8 copy.43
  6.1 0.7 copy.44
  7.6 138.9 %shard_map.279 = (bf16[4,2,2,2,16,128]{5,4,3,2,1,0:T(8,128)(2,1)}, bf16[4,2,2,2,32,3200]{5,4,3,2,1,0:T(8,128)(2,1)}, bf16[4,2,2,2,32,1024]{5,4,3,2,1,0:T(8,128)(...) custom-call(bf16[1024,1024]{1,0:T(8,128)(2,1)} %refs_0_.3, ...), custom_call_target="tpu_custom_call" | custom-call | tf_op jit(solution)/shard_map/pallas_call | solution.py:1228
  146.5 64.8 %shard_map.280 = (f32[1024,1024]{1,0:T(8,128)}, f32[1024,1024]{1,0:T(8,128)}, bf16[1024,2816]{1,0:T(8,128)(2,1)}, bf16[1024,2816]{1,0:T(8,128)(2,1)}, bf16[2816,1024]{1,0:T(8,128)(2,1)}) custom-call(bf16[1024,1024]{1,0:T(8,128)(2,1)} %get-tuple-element.61.ffn_in, bf16[1024,1024]{1,0:T(8,128)(2,1)} %get-tuple-element.62.ffn_in_t, ...), custom_call_target="tpu_custom_call" | custom-call | tf_op jit(solution)/shard_map/pallas_call | solution.py:1264
  211.4 17.0 %shard_map.281 = (f32[1024,1024]{1,0:T(8,128)}, bf16[1024,1024]{1,0:T(8,128)(2,1)}, bf16[1024,1024]{1,0:T(8,128)(2,1)}, f32[1024,1024]{1,0:T(8,128)}, bf16[8,4,2...) custom-call(f32[1024,1024]{1,0:T(8,128)} %get-tuple-element.73.ffn_back, ...), custom_call_target="tpu_custom_call" | custom-call | tf_op jit(solution)/shard_map/pallas_call | solution.py:1281
  228.3 5.3 %convolution_convert_fusion = bf16[1024,1024]{1,0:T(8,128)(2,1)} fusion(bf16[1024,1024]{1,0:T(8,128)(2,1)S(1)} %copy-done.7, bf16[1024,1024]{1,0:T(8,128)(2,1)} %get-tuple-element.91), kind=kOutput, calls=%fused_computation | convolution fusion | flops 2148532224 | bytes 6291456 | tf_op jit(solution)/shard_map/dot_general | solution.py:720
  233.6 123.6 %shard_map.282 = (bf16[1024,3200]{1,0:T(8,128)(2,1)}, bf16[1024,512]{1,0:T(8,128)(2,1)}, f32[1024,1024]{1,0:T(8,128)}, f32[1,1024]{1,0:T(1,128)}, f32[32,2816]{1...) custom-call(bf16[1024,1024]{1,0:T(8,128)(2,1)} %refs_0_.3, ...), custom_call_target="tpu_custom_call" | custom-call | tf_op jit(solution)/shard_map/pallas_call | solution.py:1346
  357.3 1.6 fusion.3
  360.2 0.8 maximum_maximum_fusion.refs_2_
  361.0 55.3 %shard_map.283 = (f32[16,128]{1,0:T(8,128)}, f32[32,3200]{1,0:T(8,128)}) custom-call(bf16[1024,1024]{1,0:T(8,128)(2,1)} %get-tuple-element.93.refs_0_, bf16[1024,3200]{1,0:T(8,128)(2,1)} %get-tuple-element.94.refs_1_, bf16[4,2,2,2,16,128]{5,4,3,2,1,0:T(8,128)(2,1)} %maximum_maximum_fusion.refs_2_), custom_call_target="tpu_custom_call" | custom-call | tf_op jit(solution)/shard_map/pallas_call | solution.py:1406
  416.3 1.7 fusion
  418.0 1.5 fusion.1
  419.5 0.7 slice.37
  420.9 0.8 slice.32
  425.0 1.4 slice_reduce_fusion
  426.4 4.9 %copy.60 = f32[1024,1024]{1,0:T(8,128)} copy(f32[1024,1024]{1,0:T(8,128)} %get-tuple-element.162) | data formatting | bytes 8388608
  431.9 0.7 copy.62
  432.6 0.7 copy.63
  433.4 0.7 copy.64
  (41 shorter events, 6.7 us)
Async XLA Ops:
  211.4 17.0 %copy-start.7 = (bf16[1024,1024]{1,0:T(8,128)(2,1)S(1)}, bf16[1024,1024]{1,0:T(8,128)(2,1)}, u32[]{:S(2)}) copy-start(bf16[1024,1024]{1,0:T(8,128)(2,1)} %get-tuple-element.90) | copy-start | bytes 6291460
  233.6 123.6 %copy-start.3 = (bf16[1024,128]{1,0:T(8,128)(2,1)S(1)}, bf16[1024,128]{1,0:T(8,128)(2,1)}, u32[]{:S(2)}) copy-start(bf16[1024,128]{1,0:T(8,128)(2,1)} %get-tuple-element.96) | copy-start | bytes 786436
  233.6 126.0 %copy-start.6 = (f32[1,1024]{1,0:T(1,128)S(1)}, f32[1,1024]{1,0:T(1,128)}, u32[]{:S(2)}) copy-start(f32[1,1024]{1,0:T(1,128)} %get-tuple-element.98) | copy-start | bytes 12292
  233.6 126.0 %copy-start.5 = (f32[1,1024]{1,0:T(1,128)S(1)}, f32[1,1024]{1,0:T(1,128)}, u32[]{:S(2)}) copy-start(f32[1,1024]{1,0:T(1,128)} %get-tuple-element.99) | copy-start | bytes 12292
  426.3 4.9 %copy-start.4 = (f32[32,1024]{1,0:T(8,128)S(1)}, f32[32,1024]{1,0:T(8,128)}, u32[]{:S(2)}) copy-start(f32[32,1024]{1,0:T(8,128)} %get-tuple-element.172) | copy-start | bytes 393220
  426.3 5.6 %copy-start.2 = (f32[32,2816]{1,0:T(8,128)S(1)}, f32[32,2816]{1,0:T(8,128)}, u32[]{:S(2)}) copy-start(f32[32,2816]{1,0:T(8,128)} %get-tuple-element.174) | copy-start | bytes 1081348
  426.3 6.3 %copy-start.1 = (f32[32,2816]{1,0:T(8,128)S(1)}, f32[32,2816]{1,0:T(8,128)}, u32[]{:S(2)}) copy-start(f32[32,2816]{1,0:T(8,128)} %get-tuple-element.175) | copy-start | bytes 1081348
  426.4 7.0 %copy-start = (f32[88,1024]{1,0:T(8,128)S(1)}, f32[88,1024]{1,0:T(8,128)}, u32[]{:S(2)}) copy-start(f32[88,1024]{1,0:T(8,128)} %get-tuple-element.176) | copy-start | bytes 1081348
